TPU v7x, 32 devices: a whole 2x2x4 slice. The times are simulated.
32 devices in a mesh: band: 16 (over z, y, core), mp: 2 (over x).
Axes of the slice: x: 2, y: 2, z: 4, core: 2. Of those that a mesh axis runs over, the one named last changes fastest.
Arguments:
- grid_latent: bfloat16 [16384, 1024], P(('band', 'mp')), may hold values from -6 to 6
- grid_gain: float32 [1024], replicated, may hold values from 0.1 to 1.9
- hidden_in: bfloat16 [4096, 1024], P('band'), may hold values from -6 to 6
- hid_gain: float32 [1024], replicated, may hold values from 0.1 to 1.9
- enc_wq: bfloat16 [1024, 1024], P(None, 'mp'), may hold values from -8 to 8
- enc_wk: bfloat16 [1024, 1024], P(None, 'mp'), may hold values from -0.1875 to 0.1875
- enc_wv: bfloat16 [1024, 1024], P(None, 'mp'), may hold values from -0.1875 to 0.1875
- enc_wo: bfloat16 [1024, 1024], P('mp'), may hold values from -0.1875 to 0.1875
- enc_edges: int32 [4096, 32], P('band'), may hold values from 0 to 16383, as said below
- enc_counts: int32 [4096], P('band'), may hold values from 1 to 32
- proc_gain: float32 [1024], replicated, may hold values from 0.1 to 1.9
- proc_wq: bfloat16 [1024, 1024], P(None, 'mp'), may hold values from -8 to 8
- proc_wk: bfloat16 [1024, 1024], P(None, 'mp'), may hold values from -0.25 to 0.25
- proc_wv: bfloat16 [1024, 1024], P(None, 'mp'), may hold values from -0.1875 to 0.1875
- proc_wo: bfloat16 [1024, 1024], P('mp'), may hold values from -0.1875 to 0.1875
Outputs:
- mixed: bfloat16 [4096, 1024], P('band')
Inputs may be any that keep to these rules, and one draw needn't show every extreme that they name: `enc_edges`: node n lies in band b = n // 256; each of its edges references a grid point from b * 1024 - 128 to (b + 1) * 1024 + 127. Slots at or beyond the node's count hold valid grid points as well.
All inputs are finite; a program needn't handle non-finite values.
Results may differ from a plain program's by a relative error of at most 0.02.
Values may be sent and summed in bfloat16 or wider, within the bound.
No kernel may reach another device: no remote copies, remote signals or barrier semaphores. Data moves between devices by JAX's collectives and lax.ppermute only.
A program may use at most 128 MiB of HBM per device.

v0:
```python
import jax
import jax.numpy as jnp
from jax import lax
from jax.sharding import PartitionSpec as P

D = 1024
HEADS = 16
WIN = 128


EPSILON = 1e-05


def with_halo(shard, sides, width):
    for axis, dim in sides:
        peers, length = (lax.axis_size(axis), shard.shape[dim])
        up = [(i, (i + 1) % peers) for i in range(peers - 1)]
        down = [(j, i) for i, j in up]
        last = lax.slice_in_dim(shard, length - width, length, axis=dim)
        initial = lax.slice_in_dim(shard, 0, width, axis=dim)
        before = lax.ppermute(last, axis, up)
        after = lax.ppermute(initial, axis, down)
        shard = jnp.concatenate([before, shard, after], axis=dim)
    return shard


def layer_norm(values, gain):
    values = values.astype(jnp.float32)
    center = values - jnp.mean(values, axis=-1, keepdims=True)
    spread = jnp.mean(center * center, axis=-1, keepdims=True)
    return center * lax.rsqrt(spread + EPSILON) * gain


def softmax_rows(scores):
    top = jnp.max(scores, axis=-1, keepdims=True)
    expd = jnp.exp(scores - top)
    return (expd / jnp.sum(expd, axis=-1, keepdims=True)).astype(jnp.bfloat16)


def edge_attention(query, keys, values, valid):
    scale = query.shape[-1] ** (-0.5)
    scores = jnp.einsum("nhe,nshe->nhs", query, keys, preferred_element_type=jnp.float32) * scale
    scores = jnp.where(valid[:, None, :], scores, -jnp.inf)
    weights = softmax_rows(scores)
    out = jnp.einsum("nhs,nshe->nhe", weights, values, preferred_element_type=jnp.float32)
    return out.astype(jnp.bfloat16)


def window_attention(query, keys, values, valid):
    scale = query.shape[-1] ** (-0.5)
    scores = jnp.einsum("nhe,mhe->nhm", query, keys, preferred_element_type=jnp.float32) * scale
    scores = jnp.where(valid[:, None, :], scores, -jnp.inf)
    weights = softmax_rows(scores)
    out = jnp.einsum("nhm,mhe->nhe", weights, values, preferred_element_type=jnp.float32)
    return out.astype(jnp.bfloat16)


def project(rows, weight):
    return jnp.dot(rows, weight, preferred_element_type=jnp.float32).astype(jnp.bfloat16)


def mix_heads(heads, w_out):
    return lax.psum(
        jnp.dot(heads, w_out, preferred_element_type=jnp.float32).astype(jnp.bfloat16), "mp"
    ).astype(jnp.float32)


def shards(
    grid_latent,
    grid_gain,
    hidden_in,
    hid_gain,
    enc_wq,
    enc_wk,
    enc_wv,
    enc_wo,
    enc_edges,
    enc_counts,
    proc_gain,
    proc_wq,
    proc_wk,
    proc_wv,
    proc_wo,
):
    band_index = lax.axis_index("band")
    band_count = lax.axis_size("band")
    columns = enc_wk.shape[1]
    head_dim = D // HEADS
    local_heads = columns // head_dim
    node_rows = hidden_in.shape[0]
    slots = enc_edges.shape[1]
    grid_norm = layer_norm(grid_latent, grid_gain).astype(jnp.bfloat16)
    pair_weight = jnp.stack([enc_wk, enc_wv])
    grid_pair = jnp.einsum(
        "rd,sdc->src",
        lax.all_gather(grid_norm, "mp", axis=0, tiled=True),
        pair_weight,
        preferred_element_type=jnp.float32,
    ).astype(jnp.bfloat16)
    grid_band = grid_pair.shape[1]
    rim_rows = grid_band // 8
    grid_wide = with_halo(grid_pair, (("band", 1),), rim_rows)
    node_norm = layer_norm(hidden_in, hid_gain).astype(jnp.bfloat16)
    enc_query = project(node_norm, enc_wq).reshape(node_rows, local_heads, head_dim)
    first_row = band_index * grid_band - rim_rows
    local_edges = (enc_edges - first_row).reshape(-1)
    near = jnp.take(grid_wide, local_edges, axis=1).reshape(
        2, node_rows, slots, local_heads, head_dim
    )
    valid = jnp.arange(slots, dtype=jnp.int32)[None, :] < enc_counts[:, None]
    enc_heads = edge_attention(enc_query, near[0], near[1], valid).reshape(node_rows, columns)
    latent = hidden_in.astype(jnp.float32) + mix_heads(enc_heads, enc_wo)
    proc_norm = layer_norm(latent, proc_gain).astype(jnp.bfloat16)
    proc_query = project(proc_norm, proc_wq).reshape(node_rows, local_heads, head_dim)
    own_pair = jnp.stack([project(proc_norm, proc_wk), project(proc_norm, proc_wv)])
    pair_wide = with_halo(own_pair, (("band", 1),), WIN)
    keys_wide = pair_wide[0]
    values_wide = pair_wide[1]
    span = node_rows + 2 * WIN
    keys_wide = keys_wide.reshape(span, local_heads, head_dim)
    values_wide = values_wide.reshape(span, local_heads, head_dim)
    start = band_index * node_rows
    own = start + jnp.arange(node_rows, dtype=jnp.int32)
    other = start - WIN + jnp.arange(span, dtype=jnp.int32)
    total = band_count * node_rows
    window_valid = (
        (jnp.abs(own[:, None] - other[None, :]) <= WIN)
        & (other >= 0)[None, :]
        & (other < total)[None, :]
    )
    proc_heads = window_attention(proc_query, keys_wide, values_wide, window_valid).reshape(
        node_rows, columns
    )
    return (latent + mix_heads(proc_heads, proc_wo)).astype(jnp.bfloat16)


def solution(mesh):
    return jax.shard_map(
        shards,
        mesh=mesh,
        in_specs=(
            P(("band", "mp"), None),
            P(),
            P("band", None),
            P(),
            P(None, "mp"),
            P(None, "mp"),
            P(None, "mp"),
            P("mp", None),
            P("band", None),
            P("band"),
            P(),
            P(None, "mp"),
            P(None, "mp"),
            P(None, "mp"),
            P("mp", None),
        ),
        out_specs=P("band", None),
        check_vma=False,
    )
```

profile of v0, /device:TPU:0, one launch (start us, length us, event | category | flops | bytes accessed | tf_op | source)
XLA Modules:
  0.0 448.7 jit_solution(13786889315813020844)
XLA Ops:
  6.5 0.0 all-gather.2.cloned.1.call-start
  6.6 1.6 convert_reduce_fusion
  8.2 1.6 fusion.7
  9.8 0.0 copy-start.13
  9.8 2.6 fusion.9
  12.4 0.0 all-gather.2.cloned.1.call-update
  12.5 0.0 all-reduce.3.cloned.1.call-start
  12.5 0.1 copy.33
  12.6 0.1 reshape.180
  12.8 0.1 convert_reduce_fusion.1
  12.9 0.3 fusion.33
  13.2 0.1 reshape.181
  13.4 1.3 copy.34
  14.7 2.4 copy.35
  17.1 2.4 convolution_convert_fusion.5
  19.5 28.9 %all-gather.2.cloned.1.call-done = bf16[1024,1024]{1,0:T(8,128)(2,1)} async-done(((bf16[512,1024]{1,0:T(8,128)(2,1)}), bf16[1024,1024]{1,0:T(8,128)(2,1)}) %all-gather.2.cloned.1.call-update) | async-done | bytes 2097168 | tf_op jit(solution)/shard_map/all_gather | solution.py:96
  48.4 4.3 convert_bitcast_fusion
  52.7 1.3 copy-done.3
  54.0 0.9 fusion.61
  54.9 1.7 collective-permute-start
  56.7 1.3 collective-permute-start.1
  58.0 1.1 copy.32
  59.1 0.3 copy.57
  59.4 2.1 collective-permute-done.1
  61.6 3.3 pad_maximum_fusion
  64.9 7.4 %copy.37 = bf16[2,1280,512]{2,0,1:T(2,128)(2,1)} copy(bf16[2,1280,512]{1,2,0:T(8,128)(2,1)} %pad_maximum_fusion) | data formatting | bytes 5242880 | tf_op jit(solution)/shard_map/concatenate | solution.py:23
  72.3 85.8 %gather_fusion = bf16[8192,2,512]{2,1,0:T(2,128)(2,1)} fusion(bf16[2,1280,512]{2,0,1:T(2,128)(2,1)} %copy.37, s32[8192]{0:T(1024)S(1)} %broadcast_clamp_fusion), kind=kCustom, calls=%fused_computation | custom fusion | bytes 33587200 | tf_op jit(solution)/shard_map/jit(_take)/gather | solution.py:107
  158.1 31.7 %fusion.3 = bf16[2,8192,512]{2,0,1:T(2,128)(2,1)} fusion(bf16[8192,2,512]{2,1,0:T(2,128)(2,1)} %gather_fusion, pred[8192]{0:T(1024)(128)(4,1)S(1)} %compare_and_fusion), kind=kLoop, calls=%fused_computation.9 | loop fusion | flops 8388608 | bytes 33562624 | tf_op jit(solution)/shard_map/jit(_take)/select_n | solution.py:107
  189.8 84.6 %slice_reduce_fusion = (bf16[8192,512]{1,0:T(8,128)(2,1)}, bf16[8192,512]{1,0:T(8,128)(2,1)}) fusion(bf16[2,8192,512]{2,0,1:T(2,128)(2,1)} %fusion.3), kind=kLoop, calls=%fused_computation.7 | loop fusion | bytes 33554432 | tf_op jit(solution)/shard_map/slice | solution.py:111
  274.5 21.2 %squeeze.6 = bf16[256,32,8,64]{3,2,1,0:T(8,128)(2,1)} reshape(bf16[8192,512]{1,0:T(8,128)(2,1)} %get-tuple-element.6) | data formatting | bytes 16777216 | tf_op jit(solution)/shard_map/squeeze | solution.py:111
  295.7 14.7 %multiply_reduce_fusion.1 = f32[256,8,32]{1,2,0:T(8,128)} fusion(f32[256,8,64]{2,1,0:T(8,128)S(1)} %copy.57, bf16[256,32,8,64]{3,2,1,0:T(8,128)(2,1)} %squeeze.6), kind=kLoop, calls=%fused_computation.5 | loop fusion | flops 12517376 | bytes 9175040
  310.3 3.7 copy.48
  314.0 0.1 fusion.32
  314.1 4.5 %copy.58 = f32[256,8,32]{1,2,0:T(8,128)} copy(f32[256,8,32]{0,2,1:T(8,128)S(1)} %fusion.32) | data formatting | bytes 524288
  318.7 21.2 %squeeze.7 = bf16[256,32,8,64]{3,2,1,0:T(8,128)(2,1)} reshape(bf16[8192,512]{1,0:T(8,128)(2,1)} %get-tuple-element.5) | data formatting | bytes 16777216 | tf_op jit(solution)/shard_map/squeeze | solution.py:111
  339.9 11.6 %multiply_reduce_fusion = bf16[256,8,64]{2,1,0:T(8,128)(2,1)S(1)} fusion(f32[256,8,32]{1,2,0:T(8,128)} %copy.58, bf16[256,32,8,64]{3,2,1,0:T(8,128)(2,1)} %squeeze.7), kind=kLoop, calls=%fused_computation.4 | loop fusion | flops 12451840 | bytes 8912896
  351.5 0.0 copy-start.11
  351.5 0.0 copy-start.4
  351.6 0.3 copy.55
  351.9 1.3 convolution_convert_fusion.1
  353.2 0.0 all-reduce.3.cloned.1.call-update
  353.2 0.0 all-reduce.5.cloned.1.call-start
  353.3 0.3 fusion.42
  353.6 32.8 %all-reduce.3.cloned.1.call-done = bf16[256,1024]{1,0:T(8,128)(2,1)} async-done(((bf16[256,1024]{1,0:T(8,128)(2,1)}), bf16[256,1024]{1,0:T(8,128)(2,1)}) %all-reduce.3.cloned.1.call-update) | async-done | bytes 524304 | tf_op jit(solution)/shard_map/psum | solution.py:63
  386.4 1.4 fusion.36
  387.8 1.3 multiply_reduce_fusion.2
  389.1 1.3 multiply_convert_fusion
  390.4 0.4 fusion.29
  390.9 0.4 fusion.30
  391.4 1.8 collective-permute-start.2
  393.1 1.3 collective-permute-start.3
  394.4 0.4 convolution_convert_fusion.2
  394.9 0.1 copy.40
  395.0 2.9 collective-permute-done.3
  397.9 1.0 pad_maximum_fusion.1
  399.0 0.1 fusion.62
  399.0 0.2 copy.39
  399.3 0.2 copy.38
  399.5 3.4 fusion.63
  402.9 2.8 fusion.27
  405.7 1.3 convolution_convert_fusion
  407.0 0.0 all-reduce.5.cloned.1.call-update
  407.0 33.1 %all-reduce.5.cloned.1.call-done = bf16[256,1024]{1,0:T(8,128)(2,1)} async-done(((bf16[256,1024]{1,0:T(8,128)(2,1)}), bf16[256,1024]{1,0:T(8,128)(2,1)}) %all-reduce.5.cloned.1.call-update) | async-done | bytes 524304 | tf_op jit(solution)/shard_map/psum | solution.py:63
  440.1 2.1 add_convert_fusion
  (41 shorter events, 0.2 us)
Async XLA Ops:
  6.5 345.4 %copy-start = (bf16[512,1024]{1,0:T(8,128)(2,1)S(1)}, bf16[512,1024]{1,0:T(8,128)(2,1)}, u32[]{:S(2)}) copy-start(bf16[512,1024]{1,0:T(8,128)(2,1)} %param.22) | copy-start | bytes 3145732
  6.5 6.0 %copy-start.10 = (s32[256,32]{0,1:T(8,128)S(1)}, s32[256,32]{0,1:T(8,128)}, u32[]{:S(2)}) copy-start(s32[256,32]{0,1:T(8,128)} %param.23) | copy-start | bytes 98308
  6.5 6.2 %copy-start.1 = (bf16[256,1024]{1,0:T(8,128)(2,1)S(1)}, bf16[256,1024]{1,0:T(8,128)(2,1)}, u32[]{:S(2)}) copy-start(bf16[256,1024]{1,0:T(8,128)(2,1)} %param.17) | copy-start | bytes 1572868
  6.5 6.8 %copy-start.8 = (bf16[1024,512]{1,0:T(8,128)(2,1)S(1)}, bf16[1024,512]{1,0:T(8,128)(2,1)}, u32[]{:S(2)}) copy-start(bf16[1024,512]{1,0:T(8,128)(2,1)} %param.20) | copy-start | bytes 3145732
  6.5 41.9 %all-gather.2.cloned.1.call-start = ((), (), s32[]{:S(2)}) async-start(), calls=%async_computation | async-start | bytes 3145728 | tf_op jit(solution)/shard_map/all_gather | solution.py:96
  9.8 7.2 %copy-start.13 = (f32[1024]{0:T(1024)S(1)}, f32[1024]{0:T(1024)}, u32[]{:S(2)}) copy-start(f32[1024]{0:T(1024)} %param.18) | copy-start | bytes 12292
  12.5 373.9 %all-reduce.3.cloned.1.call-start = ((), (), s32[]{:S(2)}) async-start(), calls=%async_computation.1 | async-start | bytes 1048576 | tf_op jit(solution)/shard_map/psum | solution.py:63
  14.7 33.7 %copy-start.9 = (bf16[1024,512]{0,1:T(8,128)(2,1)S(1)}, bf16[1024,512]{0,1:T(8,128)(2,1)}, u32[]{:S(2)}) copy-start(bf16[1024,512]{0,1:T(8,128)(2,1)} %copy.34) | copy-start | bytes 3145732
  48.4 9.5 %copy-start.12 = (s32[256]{0:T(256)S(1)}, s32[256]{0:T(256)}, u32[]{:S(2)}) copy-start(s32[256]{0:T(256)} %param.24) | copy-start | bytes 3076
  52.7 1.3 copy-start.3
  54.9 4.5 %collective-permute-start = (bf16[2,128,512]{1,2,0:T(8,128)(2,1)}, bf16[2,128,512]{1,2,0:T(8,128)(2,1)S(1)}, u32[]{:S(2)}, u32[]{:S(2)}) collective-permute-start(bf16[2,128,512]{1,2,0:T(8,128)(2,1)} %get-tuple-element.7), channel_id=1, source_target_pairs={{0,2},{2,4},{4,6},{6,8},{8,10},{10,12},{12,14},{14,16},{16,18},{18... | collective-permute-start | bytes 786440 | tf_op jit(solution)/shard_map/ppermute | solution.py:21
  56.7 4.9 %collective-permute-start.1 = (bf16[2,128,512]{1,2,0:T(8,128)(2,1)}, bf16[2,128,512]{1,2,0:T(8,128)(2,1)S(1)}, u32[]{:S(2)}, u32[]{:S(2)}) collective-permute-start(bf16[2,128,512]{1,2,0:T(8,128)(2,1)} %get-tuple-element.8), channel_id=1, source_target_pairs={{2,0},{4,2},{6,4},{8,6},{10,8},{12,10},{14,12},{16,14},{18,16},{20... | collective-permute-start | bytes 786440 | tf_op jit(solution)/shard_map/ppermute | solution.py:22
  351.5 37.6 %copy-start.11 = (f32[1024]{0:T(1024)S(1)}, f32[1024]{0:T(1024)}, u32[]{:S(2)}) copy-start(f32[1024]{0:T(1024)} %param.25) | copy-start | bytes 12292
  351.5 38.9 %copy-start.4 = (bf16[1024,512]{1,0:T(8,128)(2,1)S(1)}, bf16[1024,512]{1,0:T(8,128)(2,1)}, u32[]{:S(2)}) copy-start(bf16[1024,512]{1,0:T(8,128)(2,1)} %param.27) | copy-start | bytes 3145732
  353.2 86.9 %all-reduce.5.cloned.1.call-start = ((), (), s32[]{:S(2)}) async-start(), calls=%async_computation.2 | async-start | bytes 1048576 | tf_op jit(solution)/shard_map/psum | solution.py:63
  386.4 4.5 %copy-start.5 = (bf16[1024,512]{1,0:T(8,128)(2,1)S(1)}, bf16[1024,512]{1,0:T(8,128)(2,1)}, u32[]{:S(2)}) copy-start(bf16[1024,512]{1,0:T(8,128)(2,1)} %param.28) | copy-start | bytes 3145732
  386.4 8.1 %copy-start.6 = (bf16[1024,512]{1,0:T(8,128)(2,1)S(1)}, bf16[1024,512]{1,0:T(8,128)(2,1)}, u32[]{:S(2)}) copy-start(bf16[1024,512]{1,0:T(8,128)(2,1)} %param.26) | copy-start | bytes 3145732
  391.4 3.7 collective-permute-start.2
  393.1 4.8 %collective-permute-start.3 = (bf16[2,128,512]{2,1,0:T(8,128)(2,1)S(1)}, bf16[2,128,512]{2,1,0:T(8,128)(2,1)}, u32[]{:S(2)}, u32[]{:S(2)}) collective-permute-start(bf16[2,128,512]{2,1,0:T(8,128)(2,1)S(1)} %get-tuple-element.12), channel_id=1, source_target_pairs={{2,0},{4,2},{6,4},{8,6},{10,8},{12,10},{14,12},{16,14},{18,16},{20... | collective-permute-start | bytes 786440 | tf_op jit(solution)/shard_map/ppermute | solution.py:22
  402.9 2.8 copy-start.7
  402.9 37.2 %copy-start.2 = (bf16[256,1024]{1,0:T(8,128)(2,1)S(1)}, bf16[256,1024]{1,0:T(8,128)(2,1)}, u32[]{:S(2)}) copy-start(bf16[256,1024]{1,0:T(8,128)(2,1)} %all-reduce.3.cloned.1.call-done) | copy-start | bytes 1572868
Sparse Core Ops, SparseCore 0:
  12.6 35.8 all-gather.1
  353.3 33.0 all-reduce.2
  407.1 32.9 all-reduce.4
where the time goes:
time: 451 us; the launch traced here: 449 us
  local copies, waits for them, and re-layouts  237 us (53%)
  waiting for transfers between devices  99.9 us (22%)
  other arithmetic  75.3 us (17%)
  matrix products  16.7 us (4%)
  between operations  13.5 us (3%)
  starting transfers between devices  6.2 us (1%)
    gather x1, local copies, waits for them, and re-layouts, shards(): jnp.take(grid_wide, local_edges, axis=1)  85.8 us
    slice x1, local copies, waits for them, and re-layouts, shards(): near[1]  84.6 us
    psum x2, waiting for transfers between devices, mix_heads(): lax.psum(jnp.dot(heads, w_out, preferred_element_type=jnp.float32).astype...  65.9 us
    select_n x2, other arithmetic, shards(): jnp.take(grid_wide, local_edges, axis=1)  31.7 us
    all_gather x1, waiting for transfers between devices, shards(): lax.all_gather(grid_norm, 'mp', axis=0, tiled=True)  28.9 us
    unnamed x2, other arithmetic  26.3 us
    squeeze x1, local copies, waits for them, and re-layouts, shards(): near[0]  21.2 us
    squeeze x1, local copies, waits for them, and re-layouts, shards(): near[1]  21.2 us
  transfers between devices with their start and end apart: 7, of which 5 were waited for; matrix products, arithmetic and copies ran while one was open for 2% of the time, Pallas kernels for 0%

commit v1 on v0

v1 whole, which is shorter than its diff:
```python
import functools

import jax
import jax.numpy as jnp
from jax import lax
from jax.experimental import pallas as pl
from jax.experimental.pallas import tpu as pltpu
from jax.sharding import PartitionSpec as P

D = 1024
HEADS = 16
WIN = 128
HEAD_DIM = D // HEADS
LANES = 128

EPSILON = 1e-05
NEG = -1e30
VMEM_LIMIT = 48 * 1024 * 1024

f32 = jnp.float32
bf16 = jnp.bfloat16


def whole(shape):
    return pl.BlockSpec(shape, lambda: (0,) * len(shape))


def call(kernel, outs, args, scratch=(), flops=0):
    moved = sum(a.size * a.dtype.itemsize for a in args)
    moved += sum(o.size * o.dtype.itemsize for o in outs)
    return pl.pallas_call(
        kernel,
        out_shape=outs,
        in_specs=[whole(a.shape) for a in args],
        out_specs=[whole(o.shape) for o in outs],
        scratch_shapes=list(scratch),
        compiler_params=pltpu.CompilerParams(vmem_limit_bytes=VMEM_LIMIT),
        cost_estimate=pl.CostEstimate(flops=flops, bytes_accessed=moved, transcendentals=0),
    )(*args)


def shape_of(*shape, dtype):
    return jax.ShapeDtypeStruct(shape, dtype)


def layer_norm(values, gain):
    values = values.astype(f32)
    center = values - jnp.mean(values, axis=-1, keepdims=True)
    spread = jnp.mean(center * center, axis=-1, keepdims=True)
    return center * lax.rsqrt(spread + EPSILON) * gain


def dot(a, b):
    return jnp.dot(a, b, preferred_element_type=f32)


def dot_nt(a, b):
    return lax.dot_general(a, b, (((1,), (1,)), ((), ())), preferred_element_type=f32)


def norm_rows(src, gain, dst, base, block=64):
    rows = src.shape[0]
    block = min(block, rows)

    def step(i, carry):
        at = pl.ds(pl.multiple_of(i * block, block), block)
        to = pl.ds(pl.multiple_of(base + i * block, block), block)
        dst[to, :] = layer_norm(src[at, :], gain[...]).astype(bf16)
        return carry

    lax.fori_loop(0, rows // block, step, 0)


def even_lanes(rows):
    return lax.broadcasted_iota(jnp.int32, (rows, LANES), 1) < HEAD_DIM


def two_heads(pair):
    even = even_lanes(pair.shape[0])
    zero = jnp.zeros_like(pair)
    return jnp.concatenate([jnp.where(even, pair, zero), jnp.where(even, zero, pair)], axis=0)


def fold_heads(stacked):
    rows = stacked.shape[0] // 2
    return jnp.where(even_lanes(rows), stacked[:rows], stacked[rows:])


def attend(query, parts):
    both = two_heads(query)
    scores = []
    top = None
    for keys, _, bias in parts:
        part = dot_nt(both, keys)
        if bias is not None:
            part = part + jnp.concatenate([bias, bias], axis=0)
        scores.append(part)
        peak = jnp.max(part, axis=1, keepdims=True)
        top = peak if top is None else jnp.maximum(top, peak)
    out = None
    for (_, values, _), part in zip(parts, scores):
        weights = jnp.exp(part - top).astype(bf16)
        wide = jnp.concatenate([values, jnp.ones_like(values)], axis=1)
        add = dot(weights, wide)
        out = add if out is None else out + add
    top = jnp.broadcast_to(top, (top.shape[0], LANES))
    return fold_heads(out[:, :LANES]), fold_heads(out[:, LANES:]), fold_heads(top)


def merge(one, two):
    out1, sum1, top1 = one
    out2, sum2, top2 = two
    top = jnp.maximum(top1, top2)
    keep1 = jnp.exp(top1 - top)
    keep2 = jnp.exp(top2 - top)
    return out1 * keep1 + out2 * keep2, sum1 * keep1 + sum2 * keep2, top


def prep_kernel(sizes, place, hidden, gain, wq, *refs):
    logs, (query, norm) = refs[: len(sizes)], refs[len(sizes) :]
    groups, width = place.shape
    nodes = 8
    slots = width // nodes
    blocks = sum(sizes) // LANES
    row_hi = lax.broadcasted_iota(jnp.int32, (blocks * nodes, width), 0)
    row_lo = lax.broadcasted_iota(jnp.int32, (LANES, width), 0)
    node = lax.broadcasted_iota(jnp.int32, (1, width), 1) // slots

    def step(g, carry):
        at = place[pl.ds(g, 1), :]
        high = jnp.where(at < 0, -1, (at // LANES) * nodes + node)
        left = (row_hi == high).astype(f32).astype(bf16)
        right = (row_lo == at % LANES).astype(f32).astype(bf16)
        count = dot_nt(left, right)
        count = jnp.where(count > 0, jnp.log(jnp.maximum(count, 1.0)), NEG)
        rows = pl.ds(pl.multiple_of(g * nodes, nodes), nodes)
        block = 0
        for log, size in zip(logs, sizes):
            for c in range(size // LANES):
                log[rows, c * LANES : (c + 1) * LANES] = count[block * nodes : (block + 1) * nodes]
                block += 1
        return carry

    lax.fori_loop(0, groups, step, 0)
    norm_rows(hidden, gain, norm, 0)
    scaled = dot(norm[...], wq[...]).astype(bf16) * (HEAD_DIM**-0.5)
    query[...] = scaled.astype(bf16)


def grid_kernel(count, first, last, *refs):
    refs = list(refs)
    rows = [refs.pop(0) for _ in range(count)]
    logs = [refs.pop(0) for _ in range(count)]
    gain, wk, wv, query = [refs.pop(0) for _ in range(4)]
    before = None if first else [refs.pop(0) for _ in range(3)]
    if last:
        wo, share = refs.pop(0), refs.pop(0)
    else:
        after = [refs.pop(0) for _ in range(3)]
    norm, keys, values = refs[:3]
    heads = refs[3] if last else None
    base = 0
    for r in rows:
        norm_rows(r, gain, norm, base)
        base += r.shape[0]
    keys[...] = dot(norm[...], wk[...]).astype(bf16)
    values[...] = dot(norm[...], wv[...]).astype(bf16)
    for p in range(query.shape[1] // LANES):
        cols = slice(p * LANES, (p + 1) * LANES)
        parts = []
        base = 0
        for r, log in zip(rows, logs):
            at = slice(base, base + r.shape[0])
            parts.append((keys[at, cols], values[at, cols], log[...]))
            base += r.shape[0]
        state = attend(query[:, cols], parts)
        if before is not None:
            state = merge([b[:, cols] for b in before], state)
        if last:
            heads[:, cols] = (state[0] / state[1]).astype(bf16)
        else:
            for ref, value in zip(after, state):
                ref[:, cols] = value
    if last:
        share[...] = dot(heads[...], wo[...]).astype(bf16)


def grid_attention(rows, logs, gain, wk, wv, query, before=None, wo=None):
    total = sum(r.shape[0] for r in rows)
    nodes, columns = query.shape
    last = wo is not None
    args = [*rows, *logs, gain, wk, wv, query, *(before or []), *([wo] if last else [])]
    if last:
        outs = [shape_of(nodes, wo.shape[1], dtype=bf16)]
    else:
        outs = [shape_of(nodes, columns, dtype=f32)] * 3
    scratch = [
        pltpu.VMEM((total, wk.shape[0]), bf16),
        pltpu.VMEM((total, columns), bf16),
        pltpu.VMEM((total, columns), bf16),
    ]
    if last:
        scratch.append(pltpu.VMEM((nodes, columns), bf16))
    kernel = functools.partial(grid_kernel, len(rows), before is None, last)
    flops = 4 * total * wk.size + 16 * nodes * total * columns
    return call(kernel, outs, args, scratch, flops)


def node_kernel(hidden, own, other, gain, wq, wk, wv, query, low, high, norm):
    latent = hidden[...].astype(f32) + (own[...].astype(f32) + other[...].astype(f32))
    norm[...] = layer_norm(latent, gain[...]).astype(bf16)
    rows, columns = query.shape
    scaled = dot(norm[...], wq[...]).astype(bf16) * (HEAD_DIM**-0.5)
    query[...] = scaled.astype(bf16)
    for weight, at in ((wk, 0), (wv, columns)):
        value = dot(norm[...], weight[...]).astype(bf16)
        low[:, at : at + columns] = value[: rows // 2]
        high[:, at : at + columns] = value[rows // 2 :]


def window_bias(queries, keys, shift):
    i = lax.broadcasted_iota(jnp.int32, (queries, keys), 0)
    j = lax.broadcasted_iota(jnp.int32, (queries, keys), 1) + shift
    return jnp.where(jnp.abs(i - j) <= WIN, 0.0, NEG).astype(f32)


def own_kernel(query, low, high, out, total, top):
    rows, columns = query.shape
    half = low.shape[0]
    bias_low = window_bias(rows, half, 0)
    bias_high = window_bias(rows, half, half)
    for p in range(columns // LANES):
        cols = slice(p * LANES, (p + 1) * LANES)
        vals = slice(columns + p * LANES, columns + (p + 1) * LANES)
        parts = [
            (low[:, cols], low[:, vals], bias_low),
            (high[:, cols], high[:, vals], bias_high),
        ]
        for ref, value in zip((out, total, top), attend(query[:, cols], parts)):
            ref[:, cols] = value


def halo_kernel(ends, query, before, after, out, total, top, wo, share, heads):
    rows, columns = query.shape
    bias_before = window_bias(WIN, WIN, -WIN) + jnp.where(ends[0] == 0, NEG, 0.0)
    bias_after = window_bias(WIN, WIN, WIN) + jnp.where(ends[1] == 0, NEG, 0.0)
    for p in range(columns // LANES):
        cols = slice(p * LANES, (p + 1) * LANES)
        vals = slice(columns + p * LANES, columns + (p + 1) * LANES)
        state = [ref[:, cols] for ref in (out, total, top)]
        side = attend(query[:WIN, cols], [(before[:, cols], before[:, vals], bias_before)])
        first = merge([s[:WIN] for s in state], side)
        state = [jnp.concatenate([f, s[WIN:]], axis=0) for f, s in zip(first, state)]
        side = attend(query[rows - WIN :, cols], [(after[:, cols], after[:, vals], bias_after)])
        final = merge([s[rows - WIN :] for s in state], side)
        state = [jnp.concatenate([s[: rows - WIN], f], axis=0) for f, s in zip(final, state)]
        heads[:, cols] = (state[0] / state[1]).astype(bf16)
    share[...] = dot(heads[...], wo[...]).astype(bf16)


def mixed_kernel(hidden, own, other, own_share, other_share, mixed):
    latent = hidden[...].astype(f32) + (own[...].astype(f32) + other[...].astype(f32))
    mixed[...] = (latent + (own_share[...].astype(f32) + other_share[...].astype(f32))).astype(bf16)


def shards(
    grid_latent,
    grid_gain,
    hidden_in,
    hid_gain,
    enc_wq,
    enc_wk,
    enc_wv,
    enc_wo,
    enc_edges,
    enc_counts,
    proc_gain,
    proc_wq,
    proc_wk,
    proc_wv,
    proc_wo,
):
    band, bands = lax.axis_index("band"), lax.axis_size("band")
    me, peers = lax.axis_index("mp"), lax.axis_size("mp")
    rows = grid_latent.shape[0]
    grid_band = rows * peers
    rim = grid_band // 8
    nodes, slots = enc_edges.shape
    columns = enc_wk.shape[1]
    up = [(i, i + 1) for i in range(bands - 1)]
    down = [(i + 1, i) for i in range(bands - 1)]
    grid_gain, hid_gain, proc_gain = [g.reshape(1, -1) for g in (grid_gain, hid_gain, proc_gain)]

    def shifted(value, by):
        return lax.ppermute(value, "mp", [((i + by) % peers, i) for i in range(peers)])

    at = enc_edges - band * grid_band
    owner, inner = at // rows, at % rows
    ahead = (owner - me) % peers
    if peers == 2:
        cut = min(rows - rim, max(LANES, (rows - rim) // 3 * 2 // LANES * LANES))
        mine = jnp.where(me == 0, 0, rows - rim)
        edge = shifted(lax.dynamic_slice_in_dim(grid_latent, mine, rim, 0), 1)
        rest = jnp.where(me == 0, rim, 0)
        middle = shifted(lax.dynamic_slice_in_dim(grid_latent, rest, cut, 0), 1)
        final = shifted(lax.dynamic_slice_in_dim(grid_latent, rest + cut, rows - rim - cut, 0), 1)
        after_band = jnp.where(me == 0, grid_latent[:rim], edge)
        before_band = jnp.where(me == 0, edge, grid_latent[rows - rim :])
        theirs = jnp.where(owner == 0, 0, rows - rim)
        inner = jnp.where(ahead == 0, inner, (inner - theirs) % rows)
        pieces = [grid_latent, edge, middle, final]
    else:
        pieces = [grid_latent] + [shifted(grid_latent, d) for d in range(1, peers)]
        stack = jnp.stack(pieces)
        after_band = lax.dynamic_index_in_dim(stack, (-me) % peers, 0, False)[:rim]
        before_band = lax.dynamic_index_in_dim(stack, (peers - 1 - me) % peers, 0, False)[rows - rim :]
    lower = lax.ppermute(before_band, "band", up)
    upper = lax.ppermute(after_band, "band", down)
    pieces += [lower, upper]
    sizes = [p.shape[0] for p in pieces]
    place = jnp.where(at < 0, grid_band + rim + at, ahead * rows + inner)
    place = jnp.where(at >= grid_band, rim + at, place)
    live = jnp.arange(slots, dtype=jnp.int32)[None, :] < enc_counts[:, None]
    place = jnp.where(live, place, -1).reshape(nodes // 8, 8 * slots)

    *logs, query = call(
        functools.partial(prep_kernel, sizes),
        [shape_of(nodes, s, dtype=f32) for s in sizes] + [shape_of(nodes, columns, dtype=bf16)],
        [place, hidden_in, hid_gain, enc_wq],
        [pltpu.VMEM((nodes, hidden_in.shape[1]), bf16)],
        2 * nodes * enc_wq.size,
    )
    encode = functools.partial(grid_attention, gain=grid_gain, wk=enc_wk, wv=enc_wv, query=query)
    if peers == 2:
        order = [[0], [1, 4, 5, 2], [3]]
    else:
        order = [[i] for i in range(len(pieces))]
    state = None
    for i, group in enumerate(order):
        wo = enc_wo if i == len(order) - 1 else None
        state = encode([pieces[k] for k in group], [logs[k] for k in group], before=state, wo=wo)
    (own,) = state

    def exchange(share):
        if peers == 2:
            return shifted(share, 1)
        total = lax.psum(share.astype(f32), "mp")
        return total - share.astype(f32)

    other = exchange(own)
    query, low, high = call(
        node_kernel,
        [
            shape_of(nodes, columns, dtype=bf16),
            shape_of(nodes // 2, 2 * columns, dtype=bf16),
            shape_of(nodes // 2, 2 * columns, dtype=bf16),
        ],
        [hidden_in, own, other, proc_gain, proc_wq, proc_wk, proc_wv],
        [pltpu.VMEM(hidden_in.shape, bf16)],
        6 * nodes * proc_wq.size,
    )
    before = lax.ppermute(high, "band", up)
    after = lax.ppermute(low, "band", down)
    state = call(
        own_kernel,
        [shape_of(nodes, columns, dtype=f32)] * 3,
        [query, low, high],
        (),
        16 * nodes * nodes * columns,
    )
    ends = jnp.stack([band > 0, band < bands - 1]).astype(jnp.int32)
    smem = pl.BlockSpec(memory_space=pltpu.SMEM)
    args = [ends, query, before, after, *state, proc_wo]
    (own_share,) = pl.pallas_call(
        halo_kernel,
        out_shape=[shape_of(nodes, proc_wo.shape[1], dtype=bf16)],
        in_specs=[smem] + [whole(a.shape) for a in args[1:]],
        out_specs=[whole((nodes, proc_wo.shape[1]))],
        scratch_shapes=[pltpu.VMEM((nodes, columns), bf16)],
        compiler_params=pltpu.CompilerParams(vmem_limit_bytes=VMEM_LIMIT),
    )(*args)
    other_share = exchange(own_share)
    (mixed,) = call(
        mixed_kernel,
        [shape_of(*hidden_in.shape, dtype=bf16)],
        [hidden_in, own, other, own_share, other_share],
    )
    return mixed


def solution(mesh):
    return jax.shard_map(
        shards,
        mesh=mesh,
        in_specs=(
            P(("band", "mp"), None),
            P(),
            P("band", None),
            P(),
            P(None, "mp"),
            P(None, "mp"),
            P(None, "mp"),
            P("mp", None),
            P("band", None),
            P("band"),
            P(),
            P(None, "mp"),
            P(None, "mp"),
            P(None, "mp"),
            P("mp", None),
        ),
        out_specs=P("band", None),
        check_vma=False,
    )
```

time: 451 us -> 89.8 us (0.20)
  the two profiles are of different devices: /device:TPU:0 before, /device:TPU:17 now
where the time goes in v1:
time: 89.8 us; the launch traced here: 89.4 us
  waiting for transfers between devices  33.8 us (38%)
  Pallas kernels  29.6 us (33%)
  starting transfers between devices  17.3 us (19%)
  local copies, waits for them, and re-layouts  7.2 us (8%)
  other arithmetic  1.16 us (1%)
    ppermute x5, waiting for transfers between devices, shifted(): lax.ppermute(value, 'mp', [((i + by) % peers, i) for i in range(peers)])  30.6 us
    pallas_call x7, Pallas kernels, call(): pl.pallas_call(kernel, out_shape=outs, in_specs=[whole(a.shape) for a in...  27.3 us
    ppermute x1, starting transfers between devices, shards(): upper = lax.ppermute(after_band, 'band', down)  4.72 us
    ppermute x5, starting transfers between devices, shifted(): lax.ppermute(value, 'mp', [((i + by) % peers, i) for i in range(peers)])  3.77 us
    ppermute x1, starting transfers between devices, shards(): before = lax.ppermute(high, 'band', up)  3.67 us
    ppermute x1, waiting for transfers between devices, shards(): after = lax.ppermute(low, 'band', down)  3.22 us
    ppermute x1, starting transfers between devices, shards(): lower = lax.ppermute(before_band, 'band', up)  3.05 us
    unnamed x36, local copies, waits for them, and re-layouts  2.53 us
  transfers between devices with their start and end apart: 9, of which 4 were waited for; matrix products, arithmetic and copies ran while one was open for 5% of the time, Pallas kernels for 25%

profile of v1, /device:TPU:17, one launch (start us, length us, event | category | flops | bytes accessed | tf_op | source)
XLA Modules:
  0.0 89.4 jit_solution(4622865924929595939)
XLA Ops:
  0.0 0.0 copy-start.1
  0.0 1.1 %constant_dynamic-slice_fusion.1 = bf16[128,1024]{1,0:T(8,128)(2,1)S(1)} fusion(bf16[512,1024]{1,0:T(8,128)(2,1)} %refs_0_.1, s32[]{:T(128)S(6)} %select_n.72), kind=kLoop, calls=%fused_computation.26 | loop fusion | bytes 524292 | tf_op jit(solution)/shard_map/dynamic_slice | solution.py:303
  1.1 1.3 %collective-permute-start.1 = (bf16[128,1024]{1,0:T(8,128)(2,1)S(1)}, bf16[128,1024]{1,0:T(8,128)(2,1)S(1)}, u32[]{:S(2)}, u32[]{:S(2)}) collective-permute-start(bf16[128,1024]{1,0:T(8,128)(2,1)S(1)} %constant_dynamic-slice_fusion.1), channel_id=1, source_target_pairs={{1,0},{0,1},{3,2},{2,3},{5,4},{4,5},{7,6},{6,7},{9,8},{8,9},{11,10... | collective-permute-start | bytes 786440 | tf_op jit(solution)/shard_map/ppermute | solution.py:295
  2.3 1.9 %constant_dynamic-slice_fusion = bf16[256,1024]{1,0:T(8,128)(2,1)} fusion(bf16[512,1024]{1,0:T(8,128)(2,1)} %refs_0_.1, s32[]{:T(128)S(6)} %select_n.61), kind=kLoop, calls=%fused_computation.25 | loop fusion | bytes 1048580 | tf_op jit(solution)/shard_map/dynamic_slice | solution.py:305
  4.2 0.3 collective-permute-start.4
  4.5 0.0 copy-start.16
  4.5 3.8 %collective-permute-done.1.refs_0_ = bf16[128,1024]{1,0:T(8,128)(2,1)S(1)} collective-permute-done((bf16[128,1024]{1,0:T(8,128)(2,1)S(1)}, bf16[128,1024]{1,0:T(8,128)(2,1)S(1)}, u32[]{:S(2)}, u32[]{:S(2)}) %collective-permute-start.1) | collective-permute-done | bytes 262176 | tf_op jit(solution)/shard_map/ppermute | solution.py:295
  8.3 0.0 copy-done.1
  8.3 0.0 copy-start.17
  8.3 0.0 copy-start
  8.3 1.0 %slice_select_fusion = (bf16[128,1024]{1,0:T(8,128)(2,1)}, bf16[128,1024]{1,0:T(8,128)(2,1)}, bf16[128,1024]{1,0:T(8,128)(2,1)}) fusion(bf16[128,1024]{1,0:T(8,128)(2,1)S(1)} %collective-permute-done.1.refs_0_, bf16[512,1024]{1,0:T(8,128)(2,1)S(1)} %copy-done.1, pred[]{:T(512)S(6)} %eq.16, s32[]{:T(128)S(6)} %select_n.62), kind=kLoop, calls=%fused_computation | loop fusion | flops 262144 | bytes 1835013 | tf_op jit(solution)/shard_map/jit(_where)/select_n | solution.py:307
  9.3 4.7 %collective-permute-start.3 = (bf16[128,1024]{1,0:T(8,128)(2,1)}, bf16[128,1024]{1,0:T(8,128)(2,1)}, u32[]{:S(2)}, u32[]{:S(2)}) collective-permute-start(bf16[128,1024]{1,0:T(8,128)(2,1)} %get-tuple-element.43), channel_id=1, source_target_pairs={{2,0},{4,2},{6,4},{8,6},{10,8},{12,10},{14,12},{16,14},{18,16},{20... | collective-permute-start | bytes 786440 | tf_op jit(solution)/shard_map/ppermute | solution.py:318
  14.1 3.0 %collective-permute-start.2 = (bf16[128,1024]{1,0:T(8,128)(2,1)}, bf16[128,1024]{1,0:T(8,128)(2,1)}, u32[]{:S(2)}, u32[]{:S(2)}) collective-permute-start(bf16[128,1024]{1,0:T(8,128)(2,1)} %get-tuple-element.44), channel_id=1, source_target_pairs={{0,2},{2,4},{4,6},{6,8},{8,10},{10,12},{12,14},{14,16},{16,18},{18... | collective-permute-start | bytes 786440 | tf_op jit(solution)/shard_map/ppermute | solution.py:317
  17.1 0.0 copy-done.16
  17.1 0.0 copy-done.17
  17.1 0.1 fusion.6
  17.2 0.7 copy.17
  18.0 1.0 %reshape.13.place = s32[32,256]{1,0:T(8,128)S(1)} reshape(s32[256,32]{1,0:T(8,128)} %copy.17) | data formatting | bytes 65536 | tf_op jit(solution)/shard_map/reshape | solution.py:324
  19.0 0.0 copy-done
  19.0 0.0 copy-done.12
  19.0 0.0 copy-start.7
  19.0 1.2 %copy-done.7 = bf16[1024,512]{1,0:T(8,128)(2,1)S(1)} copy-done((bf16[1024,512]{1,0:T(8,128)(2,1)S(1)}, bf16[1024,512]{1,0:T(8,128)(2,1)}, u32[]{:S(2)}) %copy-start.7) | copy-done | bytes 1048600
  20.2 6.9 %shard_map.145 = (f32[256,512]{1,0:T(8,128)S(1)}, f32[256,128]{1,0:T(8,128)S(1)}, f32[256,256]{1,0:T(8,128)S(1)}, f32[256,128]{1,0:T(8,128)S(1)}, f32[256,128]{1...) custom-call(s32[32,256]{1,0:T(8,128)S(1)} %reshape.13.place, bf16[256,1024]{1,0:T(8,128)(2,1)S(1)} %copy-done, ...), custom_call_target="tpu_custom_call" | custom-call | flops 268435456 | bytes 3182592 | tf_op jit(solution)/shard_map/pallas_call | solution.py:31
  27.2 0.0 copy-start.13
  27.2 0.0 copy-done.15
  27.2 1.3 %collective-permute-start = (bf16[128,1024]{1,0:T(8,128)(2,1)S(1)}, bf16[128,1024]{1,0:T(8,128)(2,1)S(1)}, u32[]{:S(2)}, u32[]{:S(2)}) collective-permute-start(bf16[128,1024]{1,0:T(8,128)(2,1)S(1)} %copy-done.15), channel_id=1, source_target_pairs={{1,0},{0,1},{3,2},{2,3},{5,4},{4,5},{7,6},{6,7},{9,8},{8,9},{11,10... | collective-permute-start | bytes 786440 | tf_op jit(solution)/shard_map/ppermute | solution.py:295
  28.5 0.0 copy-done.2
  28.5 0.0 copy-done.13
  28.5 1.2 %copy-done.4 = bf16[1024,512]{1,0:T(8,128)(2,1)S(1)} copy-done((bf16[1024,512]{1,0:T(8,128)(2,1)S(1)}, bf16[1024,512]{1,0:T(8,128)(2,1)}, u32[]{:S(2)}) %copy-start.4) | copy-done | bytes 1048600
  29.7 4.6 %shard_map.146 = (f32[256,512]{1,0:T(8,128)S(1)}, f32[256,512]{1,0:T(8,128)S(1)}, f32[256,512]{1,0:T(8,128)S(1)}) custom-call(bf16[512,1024]{1,0:T(8,128)(2,1)S(1)} %copy-done.1, f32[256,512]{1,0:T(8,128)S(1)} %get-tuple-element.30.refs_1_, f32[1,1024]{1,0:T(1,128)S(1)} %bitcast.6, bf16[1024,512]{1,0:T(8,128)(2,1)S(1)} %copy-done.2, ...), custom_call_target="tpu_custom_call" | custom-call | flops 2147483648 | bytes 5509120 | tf_op jit(solution)/shard_map/pallas_call | solution.py:31
  34.3 0.0 collective-permute-done.4.refs_3_
  34.3 0.0 collective-permute-done.3.refs_2_
  34.3 0.0 collective-permute-done.2.refs_1_
  34.3 0.0 copy-start.3
  34.3 0.0 copy-start.5
  34.3 0.0 copy-start.6
  34.3 8.0 %shard_map.147 = (f32[256,512]{1,0:T(8,128)S(1)}, f32[256,512]{1,0:T(8,128)S(1)}, f32[256,512]{1,0:T(8,128)S(1)}) custom-call(bf16[128,1024]{1,0:T(8,128)(2,1)S(1)} %collective-permute-done.1.refs_0_, bf16[128,1024]{1,0:T(8,128)(2,1)} %collective-permute-done.2.refs_1_, bf16[128,1024]{1,0:T(8,128)(2,1)} %collective-permute-done.3.refs_2_, ...), custom_call_target="tpu_custom_call" | custom-call | flops 2684354560 | bytes 7475200 | tf_op jit(solution)/shard_map/pallas_call | solution.py:31
  42.3 0.0 collective-permute-done.refs_0_
  42.3 0.0 copy-done.3
  42.3 0.0 copy-done.5
  42.3 0.0 copy-done.6
  42.4 0.0 copy-start.8
  42.4 0.0 copy-start.9
  42.4 0.0 copy-start.10
  42.4 0.0 copy-start.14
  42.4 2.1 %shard_map.148.own = bf16[256,1024]{1,0:T(8,128)(2,1)S(1)} custom-call(bf16[128,1024]{1,0:T(8,128)(2,1)S(1)} %collective-permute-done.refs_0_, f32[256,128]{1,0:T(8,128)S(1)} %get-tuple-element.24.refs_1_, f32[1,1024]{1,0:T(1,128)S(1)} %bitcast.8, bf16[1024,512]{1,0:T(8,128)(2,1)S(1)} %copy-done.3, bf16[1024,512]{1,0:T(8,128)(2,1)S(1)} %copy-done.5, ...), custom_call_target="tpu_custom_call" | custom-call | flops 536870912 | bytes 5902336 | tf_op jit(solution)/shard_map/pallas_call | solution.py:31
  44.5 0.7 collective-permute-start.5
  45.2 13.2 %collective-permute-done.5.other = bf16[256,1024]{1,0:T(8,128)(2,1)S(1)} collective-permute-done((bf16[256,1024]{1,0:T(8,128)(2,1)S(1)}, bf16[256,1024]{1,0:T(8,128)(2,1)S(1)}, u32[]{:S(2)}, u32[]{:S(2)}) %collective-permute-start.5) | collective-permute-done | bytes 524320 | tf_op jit(solution)/shard_map/ppermute | solution.py:295
  58.4 0.0 copy-done.8
  58.4 0.0 copy-done.9
  58.4 0.0 copy-done.10
  58.4 0.0 copy-done.14
  58.5 2.1 %shard_map.149 = (bf16[256,512]{1,0:T(8,128)(2,1)S(1)}, bf16[128,1024]{1,0:T(8,128)(2,1)}, bf16[128,1024]{1,0:T(8,128)(2,1)}) custom-call(bf16[256,1024]{1,0:T(8,128)(2,1)S(1)} %copy-done, bf16[256,1024]{1,0:T(8,128)(2,1)S(1)} %shard_map.148.own, bf16[256,1024]{1,0:T(8,128)(2,1)S(1)} %collective-permute-done.5.other, f32[1,1024]{1,0:T(1,128)S(1)} %bitcast.9, ...), custom_call_target="tpu_custom_call" | custom-call | flops 805306368 | bytes 5509120 | tf_op jit(solution)/shard_map/pallas_call | solution.py:31
  60.6 3.7 %collective-permute-start.6 = (bf16[128,1024]{1,0:T(8,128)(2,1)}, bf16[128,1024]{1,0:T(8,128)(2,1)S(1)}, u32[]{:S(2)}, u32[]{:S(2)}) collective-permute-start(bf16[128,1024]{1,0:T(8,128)(2,1)} %get-tuple-element.38.high), channel_id=1, source_target_pairs={{0,2},{2,4},{4,6},{6,8},{8,10},{10,12},{12,14},{14,16},{16,18},{18... | collective-permute-start | bytes 786440 | tf_op jit(solution)/shard_map/ppermute | solution.py:362
  64.3 2.1 %collective-permute-start.7 = (bf16[128,1024]{1,0:T(8,128)(2,1)}, bf16[128,1024]{1,0:T(8,128)(2,1)S(1)}, u32[]{:S(2)}, u32[]{:S(2)}) collective-permute-start(bf16[128,1024]{1,0:T(8,128)(2,1)} %get-tuple-element.39.low), channel_id=1, source_target_pairs={{2,0},{4,2},{6,4},{8,6},{10,8},{12,10},{14,12},{16,14},{18,16},{20... | collective-permute-start | bytes 786440 | tf_op jit(solution)/shard_map/ppermute | solution.py:363
  66.4 0.1 add_convert_fusion.ends
  66.5 2.5 %shard_map.150 = (f32[256,512]{1,0:T(8,128)S(1)}, f32[256,512]{1,0:T(8,128)S(1)}, f32[256,512]{1,0:T(8,128)S(1)}) custom-call(bf16[256,512]{1,0:T(8,128)(2,1)S(1)} %get-tuple-element.37.query, bf16[128,1024]{1,0:T(8,128)(2,1)} %get-tuple-element.39.low, bf16[128,1024]{1,0:T(8,128)(2,1)} %get-tuple-element.38.high), custom_call_target="tpu_custom_call" | custom-call | flops 536870912 | bytes 2359296 | tf_op jit(solution)/shard_map/pallas_call | solution.py:31
  68.9 0.0 collective-permute-done.6.before
  69.0 3.2 %collective-permute-done.7.after = bf16[128,1024]{1,0:T(8,128)(2,1)S(1)} collective-permute-done((bf16[128,1024]{1,0:T(8,128)(2,1)}, bf16[128,1024]{1,0:T(8,128)(2,1)S(1)}, u32[]{:S(2)}, u32[]{:S(2)}) %collective-permute-start.7) | collective-permute-done | bytes 262176 | tf_op jit(solution)/shard_map/ppermute | solution.py:363
  72.2 0.0 copy-done.11
  72.2 2.2 %shard_map.151.own_share = bf16[256,1024]{1,0:T(8,128)(2,1)S(1)} custom-call(s32[2]{0:T(128)S(1)} %add_convert_fusion.ends, bf16[256,512]{1,0:T(8,128)(2,1)S(1)} %get-tuple-element.37.query, bf16[128,1024]{1,0:T(8,128)(2,1)S(1)} %collective-permute-done.6.before, bf16[128,1024]{1,0:T(8,128)(2,1)S(1)} %collective-permute-done.7.after, ...), custom_call_target="tpu_custom_call" | custom-call | tf_op jit(solution)/shard_map/pallas_call | solution.py:374
  74.4 0.3 collective-permute-start.8
  74.7 13.5 %collective-permute-done.8.other_share = bf16[256,1024]{1,0:T(8,128)(2,1)S(1)} collective-permute-done((bf16[256,1024]{1,0:T(8,128)(2,1)S(1)}, bf16[256,1024]{1,0:T(8,128)(2,1)S(1)}, u32[]{:S(2)}, u32[]{:S(2)}) %collective-permute-start.8) | collective-permute-done | bytes 524320 | tf_op jit(solution)/shard_map/ppermute | solution.py:295
  88.3 1.1 %shard_map.152 = bf16[256,1024]{1,0:T(8,128)(2,1)} custom-call(bf16[256,1024]{1,0:T(8,128)(2,1)S(1)} %copy-done, bf16[256,1024]{1,0:T(8,128)(2,1)S(1)} %shard_map.148.own, bf16[256,1024]{1,0:T(8,128)(2,1)S(1)} %collective-permute-done.5.other, bf16[256,1024]{1,0:T(8,128)(2,1)S(1)} %shard_map.151.own_share, ...), custom_call_target="tpu_custom_call" | custom-call | bytes 3145728 | tf_op jit(solution)/shard_map/pallas_call | solution.py:31
  (5 shorter events, 0.0 us)
Async XLA Ops:
  0.0 8.3 %copy-start.1 = (bf16[512,1024]{1,0:T(8,128)(2,1)S(1)}, bf16[512,1024]{1,0:T(8,128)(2,1)}, u32[]{:S(2)}) copy-start(bf16[512,1024]{1,0:T(8,128)(2,1)} %refs_0_.1) | copy-start | bytes 3145732
  1.1 7.2 %collective-permute-start.1 = (bf16[128,1024]{1,0:T(8,128)(2,1)S(1)}, bf16[128,1024]{1,0:T(8,128)(2,1)S(1)}, u32[]{:S(2)}, u32[]{:S(2)}) collective-permute-start(bf16[128,1024]{1,0:T(8,128)(2,1)S(1)} %constant_dynamic-slice_fusion.1), channel_id=1, source_target_pairs={{1,0},{0,1},{3,2},{2,3},{5,4},{4,5},{7,6},{6,7},{9,8},{8,9},{11,10... | collective-permute-start | bytes 786440 | tf_op jit(solution)/shard_map/ppermute | solution.py:295
  4.2 30.1 %collective-permute-start.4 = (bf16[256,1024]{1,0:T(8,128)(2,1)}, bf16[256,1024]{1,0:T(8,128)(2,1)S(1)}, u32[]{:S(2)}, u32[]{:S(2)}) collective-permute-start(bf16[256,1024]{1,0:T(8,128)(2,1)} %constant_dynamic-slice_fusion), channel_id=1, source_target_pairs={{1,0},{0,1},{3,2},{2,3},{5,4},{4,5},{7,6},{6,7},{9,8},{8,9},{11,10... | collective-permute-start | bytes 1572872 | tf_op jit(solution)/shard_map/ppermute | solution.py:295
  4.5 12.7 %copy-start.16 = (s32[256,32]{0,1:T(8,128)S(1)}, s32[256,32]{0,1:T(8,128)}, u32[]{:S(2)}) copy-start(s32[256,32]{0,1:T(8,128)} %param.23) | copy-start | bytes 98308
  8.3 8.8 %copy-start.17 = (s32[256]{0:T(256)S(1)}, s32[256]{0:T(256)}, u32[]{:S(2)}) copy-start(s32[256]{0:T(256)} %param.24) | copy-start | bytes 3076
  8.3 10.7 %copy-start = (bf16[256,1024]{1,0:T(8,128)(2,1)S(1)}, bf16[256,1024]{1,0:T(8,128)(2,1)}, u32[]{:S(2)}) copy-start(bf16[256,1024]{1,0:T(8,128)(2,1)} %hidden.5) | copy-start | bytes 1572868
  8.3 10.7 %copy-start.12 = (f32[1024]{0:T(1024)S(1)}, f32[1024]{0:T(1024)}, u32[]{:S(2)}) copy-start(f32[1024]{0:T(1024)} %param.18) | copy-start | bytes 12292
  9.3 19.1 %copy-start.2 = (bf16[1024,512]{1,0:T(8,128)(2,1)S(1)}, bf16[1024,512]{1,0:T(8,128)(2,1)}, u32[]{:S(2)}) copy-start(bf16[1024,512]{1,0:T(8,128)(2,1)} %refs_3_.3) | copy-start | bytes 3145732
  9.3 25.0 %collective-permute-start.3 = (bf16[128,1024]{1,0:T(8,128)(2,1)}, bf16[128,1024]{1,0:T(8,128)(2,1)}, u32[]{:S(2)}, u32[]{:S(2)}) collective-permute-start(bf16[128,1024]{1,0:T(8,128)(2,1)} %get-tuple-element.43), channel_id=1, source_target_pairs={{2,0},{4,2},{6,4},{8,6},{10,8},{12,10},{14,12},{16,14},{18,16},{20... | collective-permute-start | bytes 786440 | tf_op jit(solution)/shard_map/ppermute | solution.py:318
  14.1 20.2 %collective-permute-start.2 = (bf16[128,1024]{1,0:T(8,128)(2,1)}, bf16[128,1024]{1,0:T(8,128)(2,1)}, u32[]{:S(2)}, u32[]{:S(2)}) collective-permute-start(bf16[128,1024]{1,0:T(8,128)(2,1)} %get-tuple-element.44), channel_id=1, source_target_pairs={{0,2},{2,4},{4,6},{6,8},{8,10},{10,12},{12,14},{14,16},{16,18},{18... | collective-permute-start | bytes 786440 | tf_op jit(solution)/shard_map/ppermute | solution.py:317
  19.0 1.2 %copy-start.7 = (bf16[1024,512]{1,0:T(8,128)(2,1)S(1)}, bf16[1024,512]{1,0:T(8,128)(2,1)}, u32[]{:S(2)}) copy-start(bf16[1024,512]{1,0:T(8,128)(2,1)} %wq.2) | copy-start | bytes 3145732
  20.2 7.0 %copy-start.15 = (bf16[128,1024]{1,0:T(8,128)(2,1)S(1)}, bf16[128,1024]{1,0:T(8,128)(2,1)}, u32[]{:S(2)}) copy-start(bf16[128,1024]{1,0:T(8,128)(2,1)} %get-tuple-element.45) | copy-start | bytes 786436
  27.2 1.3 %copy-start.13 = (f32[1024]{0:T(1024)S(1)}, f32[1024]{0:T(1024)}, u32[]{:S(2)}) copy-start(f32[1024]{0:T(1024)} %param.16) | copy-start | bytes 12292
  27.2 15.1 %collective-permute-start = (bf16[128,1024]{1,0:T(8,128)(2,1)S(1)}, bf16[128,1024]{1,0:T(8,128)(2,1)S(1)}, u32[]{:S(2)}, u32[]{:S(2)}) collective-permute-start(bf16[128,1024]{1,0:T(8,128)(2,1)S(1)} %copy-done.15), channel_id=1, source_target_pairs={{1,0},{0,1},{3,2},{2,3},{5,4},{4,5},{7,6},{6,7},{9,8},{8,9},{11,10... | collective-permute-start | bytes 786440 | tf_op jit(solution)/shard_map/ppermute | solution.py:295
  28.5 1.2 %copy-start.4 = (bf16[1024,512]{1,0:T(8,128)(2,1)S(1)}, bf16[1024,512]{1,0:T(8,128)(2,1)}, u32[]{:S(2)}) copy-start(bf16[1024,512]{1,0:T(8,128)(2,1)} %refs_4_.3) | copy-start | bytes 3145732
  34.3 8.0 %copy-start.3 = (bf16[1024,512]{1,0:T(8,128)(2,1)S(1)}, bf16[1024,512]{1,0:T(8,128)(2,1)}, u32[]{:S(2)}) copy-start(bf16[1024,512]{1,0:T(8,128)(2,1)} %refs_3_.3) | copy-start | bytes 3145732
  34.3 8.0 %copy-start.5 = (bf16[1024,512]{1,0:T(8,128)(2,1)S(1)}, bf16[1024,512]{1,0:T(8,128)(2,1)}, u32[]{:S(2)}) copy-start(bf16[1024,512]{1,0:T(8,128)(2,1)} %refs_4_.3) | copy-start | bytes 3145732
  34.3 8.0 %copy-start.6 = (bf16[512,1024]{1,0:T(8,128)(2,1)S(1)}, bf16[512,1024]{1,0:T(8,128)(2,1)}, u32[]{:S(2)}) copy-start(bf16[512,1024]{1,0:T(8,128)(2,1)} %refs_9_.3) | copy-start | bytes 3145732
  42.4 16.1 %copy-start.8 = (bf16[1024,512]{1,0:T(8,128)(2,1)S(1)}, bf16[1024,512]{1,0:T(8,128)(2,1)}, u32[]{:S(2)}) copy-start(bf16[1024,512]{1,0:T(8,128)(2,1)} %wq.3) | copy-start | bytes 3145732
  42.4 16.1 %copy-start.9 = (bf16[1024,512]{1,0:T(8,128)(2,1)S(1)}, bf16[1024,512]{1,0:T(8,128)(2,1)}, u32[]{:S(2)}) copy-start(bf16[1024,512]{1,0:T(8,128)(2,1)} %wk.1) | copy-start | bytes 3145732
  42.4 16.1 %copy-start.10 = (bf16[1024,512]{1,0:T(8,128)(2,1)S(1)}, bf16[1024,512]{1,0:T(8,128)(2,1)}, u32[]{:S(2)}) copy-start(bf16[1024,512]{1,0:T(8,128)(2,1)} %wv.1) | copy-start | bytes 3145732
  42.4 16.1 %copy-start.14 = (f32[1024]{0:T(1024)S(1)}, f32[1024]{0:T(1024)}, u32[]{:S(2)}) copy-start(f32[1024]{0:T(1024)} %param.25) | copy-start | bytes 12292
  44.5 13.9 %collective-permute-start.5 = (bf16[256,1024]{1,0:T(8,128)(2,1)S(1)}, bf16[256,1024]{1,0:T(8,128)(2,1)S(1)}, u32[]{:S(2)}, u32[]{:S(2)}) collective-permute-start(bf16[256,1024]{1,0:T(8,128)(2,1)S(1)} %shard_map.148.own), channel_id=1, source_target_pairs={{1,0},{0,1},{3,2},{2,3},{5,4},{4,5},{7,6},{6,7},{9,8},{8,9},{11,10... | collective-permute-start | bytes 1572872 | tf_op jit(solution)/shard_map/ppermute | solution.py:295
  60.6 11.6 %copy-start.11 = (bf16[512,1024]{1,0:T(8,128)(2,1)S(1)}, bf16[512,1024]{1,0:T(8,128)(2,1)}, u32[]{:S(2)}) copy-start(bf16[512,1024]{1,0:T(8,128)(2,1)} %wo.1) | copy-start | bytes 3145732
  60.6 8.4 %collective-permute-start.6 = (bf16[128,1024]{1,0:T(8,128)(2,1)}, bf16[128,1024]{1,0:T(8,128)(2,1)S(1)}, u32[]{:S(2)}, u32[]{:S(2)}) collective-permute-start(bf16[128,1024]{1,0:T(8,128)(2,1)} %get-tuple-element.38.high), channel_id=1, source_target_pairs={{0,2},{2,4},{4,6},{6,8},{8,10},{10,12},{12,14},{14,16},{16,18},{18... | collective-permute-start | bytes 786440 | tf_op jit(solution)/shard_map/ppermute | solution.py:362
  64.3 7.9 %collective-permute-start.7 = (bf16[128,1024]{1,0:T(8,128)(2,1)}, bf16[128,1024]{1,0:T(8,128)(2,1)S(1)}, u32[]{:S(2)}, u32[]{:S(2)}) collective-permute-start(bf16[128,1024]{1,0:T(8,128)(2,1)} %get-tuple-element.39.low), channel_id=1, source_target_pairs={{2,0},{4,2},{6,4},{8,6},{10,8},{12,10},{14,12},{16,14},{18,16},{20... | collective-permute-start | bytes 786440 | tf_op jit(solution)/shard_map/ppermute | solution.py:363
  74.4 13.8 %collective-permute-start.8 = (bf16[256,1024]{1,0:T(8,128)(2,1)S(1)}, bf16[256,1024]{1,0:T(8,128)(2,1)S(1)}, u32[]{:S(2)}, u32[]{:S(2)}) collective-permute-start(bf16[256,1024]{1,0:T(8,128)(2,1)S(1)} %shard_map.151.own_share), channel_id=1, source_target_pairs={{1,0},{0,1},{3,2},{2,3},{5,4},{4,5},{7,6},{6,7},{9,8},{8,9},{11,10... | collective-permute-start | bytes 1572872 | tf_op jit(solution)/shard_map/ppermute | solution.py:295

commit v2 on v1

v2 whole, which is shorter than its diff:
```python
import functools

import jax
import jax.numpy as jnp
from jax import lax
from jax.experimental import pallas as pl
from jax.experimental.pallas import tpu as pltpu
from jax.sharding import PartitionSpec as P

D = 1024
HEADS = 16
WIN = 128
HEAD_DIM = D // HEADS
LANES = 128

EPSILON = 1e-05
NEG = -1e30
VMEM_LIMIT = 48 * 1024 * 1024

f32 = jnp.float32
bf16 = jnp.bfloat16


def whole(shape):
    return pl.BlockSpec(shape, lambda: (0,) * len(shape))


def call(kernel, outs, args, scratch=(), flops=0):
    moved = sum(a.size * a.dtype.itemsize for a in args)
    moved += sum(o.size * o.dtype.itemsize for o in outs)
    return pl.pallas_call(
        kernel,
        out_shape=outs,
        in_specs=[whole(a.shape) for a in args],
        out_specs=[whole(o.shape) for o in outs],
        scratch_shapes=list(scratch),
        compiler_params=pltpu.CompilerParams(vmem_limit_bytes=VMEM_LIMIT),
        cost_estimate=pl.CostEstimate(flops=flops, bytes_accessed=moved, transcendentals=0),
    )(*args)


def shape_of(*shape, dtype):
    return jax.ShapeDtypeStruct(shape, dtype)


def layer_norm(values, gain):
    values = values.astype(f32)
    center = values - jnp.mean(values, axis=-1, keepdims=True)
    spread = jnp.mean(center * center, axis=-1, keepdims=True)
    return center * lax.rsqrt(spread + EPSILON) * gain


def dot(a, b):
    return jnp.dot(a, b, preferred_element_type=f32)


def dot_nt(a, b):
    return lax.dot_general(a, b, (((1,), (1,)), ((), ())), preferred_element_type=f32)


def norm_rows(src, gain, dst, base, block=64):
    rows = src.shape[0]
    block = min(block, rows)

    def step(i, carry):
        at = pl.ds(pl.multiple_of(i * block, block), block)
        to = pl.ds(pl.multiple_of(base + i * block, block), block)
        dst[to, :] = layer_norm(src[at, :], gain[...]).astype(bf16)
        return carry

    lax.fori_loop(0, rows // block, step, 0, unroll=2 if rows // block % 2 == 0 else 1)


def even_lanes(rows):
    return lax.broadcasted_iota(jnp.int32, (rows, LANES), 1) < HEAD_DIM


def two_heads(pair):
    even = even_lanes(pair.shape[0])
    zero = jnp.zeros_like(pair)
    return jnp.concatenate([jnp.where(even, pair, zero), jnp.where(even, zero, pair)], axis=0)


def fold_heads(stacked):
    rows = stacked.shape[0] // 2
    return jnp.where(even_lanes(rows), stacked[:rows], stacked[rows:])


def attend(query, parts):
    both = two_heads(query)
    scores = []
    top = None
    for keys, _, bias in parts:
        part = dot_nt(both, keys)
        if bias is not None:
            part = part + jnp.concatenate([bias, bias], axis=0)
        scores.append(part)
        peak = jnp.max(part, axis=1, keepdims=True)
        top = peak if top is None else jnp.maximum(top, peak)
    out = None
    for (_, values, _), part in zip(parts, scores):
        weights = jnp.exp(part - top).astype(bf16)
        wide = jnp.concatenate([values, jnp.ones_like(values)], axis=1)
        add = dot(weights, wide)
        out = add if out is None else out + add
    top = jnp.broadcast_to(top, (top.shape[0], LANES))
    return fold_heads(out[:, :LANES]), fold_heads(out[:, LANES:]), fold_heads(top)


def merge(one, two):
    out1, sum1, top1 = one
    out2, sum2, top2 = two
    top = jnp.maximum(top1, top2)
    keep1 = jnp.exp(top1 - top)
    keep2 = jnp.exp(top2 - top)
    return out1 * keep1 + out2 * keep2, sum1 * keep1 + sum2 * keep2, top


def pick_kernel(cuts, whole_refs, outs, sems):
    copies = [
        pltpu.make_async_copy(
            whole_refs[k].at[pl.ds(pl.multiple_of(start(), 16), out.shape[0])], out, sems.at[i]
        )
        for i, ((k, start), out) in enumerate(zip(cuts, outs))
    ]
    for copy in copies:
        copy.start()
    for copy in copies:
        copy.wait()


def pick(arrays, cuts):
    def kernel(*refs):
        n = len(arrays)
        pick_kernel([(k, start) for k, start, _ in cuts], refs[:n], refs[n:-1], refs[-1])

    outs = [shape_of(count, arrays[k].shape[1], dtype=arrays[k].dtype) for k, _, count in cuts]
    moved = 2 * sum(o.size * o.dtype.itemsize for o in outs)
    return pl.pallas_call(
        kernel,
        out_shape=outs,
        in_specs=[pl.BlockSpec(memory_space=pltpu.HBM)] * len(arrays),
        out_specs=[whole(o.shape) for o in outs],
        scratch_shapes=[pltpu.SemaphoreType.DMA((len(cuts),))],
        compiler_params=pltpu.CompilerParams(vmem_limit_bytes=VMEM_LIMIT),
        cost_estimate=pl.CostEstimate(flops=0, bytes_accessed=moved, transcendentals=0),
    )(*arrays)


def place_of(edges, rows, rim, peers):
    band, me = lax.axis_index("band"), lax.axis_index("mp")
    grid_band = rows * peers
    at = edges - band * grid_band
    owner, inner = at // rows, at % rows
    ahead = lax.rem(owner - me + peers, peers)
    if peers == 2:
        turn = jnp.where(owner == 0, 0, rim)
        inner = jnp.where(ahead == 0, inner, (inner + turn) % rows)
        lower = grid_band + (1 - me) * rim
        upper = grid_band + me * rim
    else:
        lower = grid_band
        upper = grid_band + rim
    place = jnp.where(at < 0, lower + rim + at, ahead * rows + inner)
    return jnp.where(at >= grid_band, upper + at - grid_band, place)


def prep_kernel(sizes, rows, rim, peers, edges, counts, hidden, gain, wq, *refs):
    logs, (query, norm, turned, line) = refs[: len(sizes)], refs[len(sizes) :]
    slots, nodes = edges.shape
    share = 8
    width = share * slots
    blocks = sum(sizes) // LANES
    place = place_of(edges[...], rows, rim, peers)
    live = lax.broadcasted_iota(jnp.int32, (slots, nodes), 0) < counts[...]
    node = lax.broadcasted_iota(jnp.int32, (slots, nodes), 1) % share
    high = jnp.where(live, (place // LANES) * share + node, -1)
    turned[...] = (high * LANES + place % LANES).T
    line[...] = jnp.concatenate(
        [turned[pl.ds(i, nodes // share, stride=share), :] for i in range(share)], axis=1
    )
    row_hi = lax.broadcasted_iota(jnp.int32, (blocks * share, width), 0)
    row_lo = lax.broadcasted_iota(jnp.int32, (LANES, width), 0)

    def step(g, carry):
        code = line[pl.ds(g, 1), :]
        left = (row_hi == (code >> 7)).astype(f32).astype(bf16)
        right = (row_lo == (code & (LANES - 1))).astype(f32).astype(bf16)
        count = dot_nt(left, right)
        count = jnp.where(count > 0, jnp.log(jnp.maximum(count, 1.0)), NEG)
        to = pl.ds(pl.multiple_of(g * share, share), share)
        block = 0
        for log, size in zip(logs, sizes):
            for c in range(size // LANES):
                log[to, c * LANES : (c + 1) * LANES] = count[block * share : (block + 1) * share]
                block += 1
        return carry

    lax.fori_loop(0, nodes // share, step, 0, unroll=4)
    norm_rows(hidden, gain, norm, 0)
    scaled = dot(norm[...], wq[...]).astype(bf16) * (HEAD_DIM**-0.5)
    query[...] = scaled.astype(bf16)


def encode_heads(query, log, keys, values, before, at, heads):
    for p in range(query.shape[1] // LANES):
        cols = slice(p * LANES, (p + 1) * LANES)
        state = attend(query[at, cols], [(keys[:, cols], values[:, cols], log[at, :])])
        if before is not None:
            state = merge([b[at, cols] for b in before], state)
        heads[:, cols] = (state[0] / state[1]).astype(bf16)


def grid_kernel(count, first, last, *refs):
    refs = list(refs)
    rows = [refs.pop(0) for _ in range(count)]
    log, gain, wk, wv, query = [refs.pop(0) for _ in range(5)]
    before = None if first else [refs.pop(0) for _ in range(3)]
    if last:
        wo, share, keys, values, norm, heads = refs
    else:
        *after, norm, keys, values = refs
    base = 0
    for r in rows:
        norm_rows(r, gain, norm, base)
        base += r.shape[0]
    keys[...] = dot(norm[...], wk[...]).astype(bf16)
    values[...] = dot(norm[...], wv[...]).astype(bf16)
    if last:
        encode_heads(query, log, keys, values, before, slice(0, heads.shape[0]), heads)
        share[...] = dot(heads[...], wo[...]).astype(bf16)
        return
    for p in range(query.shape[1] // LANES):
        cols = slice(p * LANES, (p + 1) * LANES)
        state = attend(query[:, cols], [(keys[:, cols], values[:, cols], log[...])])
        if before is not None:
            state = merge([b[:, cols] for b in before], state)
        for ref, value in zip(after, state):
            ref[:, cols] = value


def grid_attention(rows, log, gain, wk, wv, query, before=None, wo=None):
    total = sum(r.shape[0] for r in rows)
    nodes, columns = query.shape
    args = [*rows, log, gain, wk, wv, query, *(before or []), *([] if wo is None else [wo])]
    pair = (total, columns)
    norm = pltpu.VMEM((total, wk.shape[0]), bf16)
    if wo is None:
        outs = [shape_of(nodes, columns, dtype=f32)] * 3
        scratch = [norm, pltpu.VMEM(pair, bf16), pltpu.VMEM(pair, bf16)]
    else:
        outs = [shape_of(nodes // 2, wo.shape[1], dtype=bf16)] + [shape_of(*pair, dtype=bf16)] * 2
        scratch = [norm, pltpu.VMEM((nodes // 2, columns), bf16)]
    kernel = functools.partial(grid_kernel, len(rows), before is None, wo is not None)
    flops = 4 * total * wk.size + 16 * nodes * total * columns
    return call(kernel, outs, args, scratch, flops)


def rest_kernel(log, query, keys, values, out, total, top, wo, share, heads):
    half = heads.shape[0]
    encode_heads(query, log, keys, values, (out, total, top), slice(half, 2 * half), heads)
    share[...] = dot(heads[...], wo[...]).astype(bf16)


def latent_of(at, hidden, own, other):
    total = own[...].astype(f32) + other[...].astype(f32)
    return hidden[at : at + own.shape[0], :].astype(f32) + total


def node_kernel(at, hidden, own, other, gain, wq, wk, wv, query, pair, norm):
    norm[...] = layer_norm(latent_of(at, hidden, own, other), gain[...]).astype(bf16)
    columns = query.shape[1]
    scaled = dot(norm[...], wq[...]).astype(bf16) * (HEAD_DIM**-0.5)
    query[...] = scaled.astype(bf16)
    for weight, col in ((wk, 0), (wv, columns)):
        pair[:, col : col + columns] = dot(norm[...], weight[...]).astype(bf16)


def window_bias(queries, keys, shift):
    i = lax.broadcasted_iota(jnp.int32, (queries, keys), 0)
    j = lax.broadcasted_iota(jnp.int32, (queries, keys), 1) + shift
    return jnp.where(jnp.abs(i - j) <= WIN, 0.0, NEG).astype(f32)


def window_kernel(side, query, low, high, halo, wo, share, heads):
    band, bands = lax.axis_index("band"), lax.axis_size("band")
    rows, columns = query.shape
    end = jnp.where(band == (0 if side < 0 else bands - 1), NEG, 0.0)
    start = 0 if side < 0 else rows
    reach = -WIN if side < 0 else low.shape[0] + high.shape[0]
    places = [(low, 0), (high, low.shape[0]), (halo, reach)]
    biases = [window_bias(rows, ref.shape[0], shift - start) for ref, shift in places]
    biases[2] = biases[2] + end
    for p in range(columns // LANES):
        cols = slice(p * LANES, (p + 1) * LANES)
        vals = slice(columns + p * LANES, columns + (p + 1) * LANES)
        parts = [(ref[:, cols], ref[:, vals], b) for (ref, _), b in zip(places, biases)]
        out, total, _ = attend(query[:, cols], parts)
        heads[:, cols] = (out / total).astype(bf16)
    share[...] = dot(heads[...], wo[...]).astype(bf16)


def mixed_kernel(hidden, *refs):
    own, other, own_share, other_share = [refs[2 * i : 2 * i + 2] for i in range(4)]
    mixed = refs[-1]
    half = own[0].shape[0]
    for i in range(2):
        latent = latent_of(i * half, hidden, own[i], other[i])
        total = own_share[i][...].astype(f32) + other_share[i][...].astype(f32)
        mixed[i * half : (i + 1) * half, :] = (latent + total).astype(bf16)


def after(value, *others):
    return lax.optimization_barrier((value, *others))[0]


def shards(
    grid_latent,
    grid_gain,
    hidden_in,
    hid_gain,
    enc_wq,
    enc_wk,
    enc_wv,
    enc_wo,
    enc_edges,
    enc_counts,
    proc_gain,
    proc_wq,
    proc_wk,
    proc_wv,
    proc_wo,
):
    bands, peers = lax.axis_size("band"), lax.axis_size("mp")
    rows = grid_latent.shape[0]
    grid_band = rows * peers
    rim = grid_band // 8
    nodes, slots = enc_edges.shape
    columns = enc_wk.shape[1]
    up = [(i, i + 1) for i in range(bands - 1)]
    down = [(i + 1, i) for i in range(bands - 1)]
    grid_gain, hid_gain, proc_gain = [g.reshape(1, -1) for g in (grid_gain, hid_gain, proc_gain)]

    def shifted(value, by):
        return lax.ppermute(value, "mp", [((i + by) % peers, i) for i in range(peers)])

    if peers == 2:
        me = lambda: lax.axis_index("mp")
        cut = min(rows - rim, max(LANES, (rows - rim) // 3 * 2 // LANES * LANES))
        (ends,) = pick([grid_latent], [(0, lambda: me() * (rows - rim), rim)])
        edge = shifted(ends, 1)
        outward = [(2 * a, 2 * b) for a, b in down] + [(2 * a + 1, 2 * b + 1) for a, b in up]
        inward = [(2 * a, 2 * b) for a, b in up] + [(2 * a + 1, 2 * b + 1) for a, b in down]
        near_rim = lax.ppermute(ends, ("band", "mp"), outward)
        middle, final = pick(
            [grid_latent],
            [
                (0, lambda: (1 - me()) * rim, cut),
                (0, lambda: (1 - me()) * rim + cut, rows - rim - cut),
            ],
        )
        middle = shifted(middle, 1)
        final = shifted(final, 1)
        far_rim = lax.ppermute(edge, ("band", "mp"), inward)
        groups = [[grid_latent], [edge, middle], [final], [near_rim, far_rim]]
    else:
        me = lax.axis_index("mp")
        pieces = [grid_latent] + [shifted(grid_latent, d) for d in range(1, peers)]
        stack = jnp.stack(pieces)
        after_band = lax.dynamic_index_in_dim(stack, (-me) % peers, 0, False)[:rim]
        before_band = lax.dynamic_index_in_dim(stack, (peers - 1 - me) % peers, 0, False)[rows - rim :]
        lower = lax.ppermute(before_band, "band", up)
        upper = lax.ppermute(after_band, "band", down)
        groups = [[p] for p in pieces] + [[lower, upper]]
    sizes = [sum(p.shape[0] for p in g) for g in groups]

    *logs, query = call(
        functools.partial(prep_kernel, sizes, rows, rim, peers),
        [shape_of(nodes, s, dtype=f32) for s in sizes] + [shape_of(nodes, columns, dtype=bf16)],
        [enc_edges.T, enc_counts.reshape(1, -1), hidden_in, hid_gain, enc_wq],
        [
            pltpu.VMEM((nodes, hidden_in.shape[1]), bf16),
            pltpu.VMEM((nodes, slots), jnp.int32),
            pltpu.VMEM((nodes // 8, 8 * slots), jnp.int32),
        ],
        2 * nodes * enc_wq.size,
    )
    encode = functools.partial(grid_attention, gain=grid_gain, wk=enc_wk, wv=enc_wv, query=query)
    order = [0, 3, 1, 2] if peers == 2 else range(len(groups))
    state = None
    for i, k in enumerate(order):
        if i < len(groups) - 1:
            state = encode(groups[k], logs[k], before=state)
    half = nodes // 2
    share, keys, values = encode(groups[k], logs[k], before=state, wo=enc_wo)
    own = [share]
    own += call(
        rest_kernel,
        [shape_of(half, enc_wo.shape[1], dtype=bf16)],
        [logs[k], query, keys, values, *state, enc_wo],
        [pltpu.VMEM((half, columns), bf16)],
        2 * half * enc_wo.size,
    )

    def exchange(share):
        if peers == 2:
            return shifted(share, 1)
        return lax.psum(share.astype(f32), "mp") - share.astype(f32)

    other = [exchange(share) for share in own]
    queries, pairs = [], []
    for i in range(2):
        query, pair = call(
            functools.partial(node_kernel, i * half),
            [shape_of(half, columns, dtype=bf16), shape_of(half, 2 * columns, dtype=bf16)],
            [hidden_in, own[i], other[i], proc_gain, proc_wq, proc_wk, proc_wv],
            [pltpu.VMEM((half, hidden_in.shape[1]), bf16)],
            6 * half * proc_wq.size,
        )
        queries.append(query)
        pairs.append(pair)
    behind = lax.ppermute(pairs[0], "band", down)
    before = lax.ppermute(pairs[1], "band", up)
    shares = [None, None]
    for i, side, halo in ((1, 1, behind), (0, -1, before)):
        (shares[i],) = call(
            functools.partial(window_kernel, side),
            [shape_of(half, proc_wo.shape[1], dtype=bf16)],
            [queries[i], *pairs, halo, proc_wo],
            [pltpu.VMEM((half, columns), bf16)],
            2 * half * proc_wo.size,
        )
    other_shares = [None, None]
    for i in (1, 0):
        other_shares[i] = exchange(shares[i])
    return call(
        mixed_kernel,
        [shape_of(*hidden_in.shape, dtype=bf16)],
        [hidden_in, *own, *other, *shares, *other_shares],
    )[0]


def solution(mesh):
    return jax.shard_map(
        shards,
        mesh=mesh,
        in_specs=(
            P(("band", "mp"), None),
            P(),
            P("band", None),
            P(),
            P(None, "mp"),
            P(None, "mp"),
            P(None, "mp"),
            P("mp", None),
            P("band", None),
            P("band"),
            P(),
            P(None, "mp"),
            P(None, "mp"),
            P(None, "mp"),
            P("mp", None),
        ),
        out_specs=P("band", None),
        check_vma=False,
    )
```

time: 89.8 us -> 68.1 us (0.76)
  the two profiles are of different devices: /device:TPU:17 before, /device:TPU:0 now
where the time goes in v2:
time: 68.1 us; the launch traced here: 67.7 us
  waiting for transfers between devices  25.1 us (37%)
  Pallas kernels  23.5 us (35%)
  starting transfers between devices  15.7 us (23%)
  local copies, waits for them, and re-layouts  3.16 us (5%)
    ppermute x7, waiting for transfers between devices, shifted(): lax.ppermute(value, 'mp', [((i + by) % peers, i) for i in range(peers)])  25 us
    pallas_call x11, Pallas kernels, call(): pl.pallas_call(kernel, out_shape=outs, in_specs=[whole(a.shape) for a in...  23.4 us
    ppermute x7, starting transfers between devices, shifted(): lax.ppermute(value, 'mp', [((i + by) % peers, i) for i in range(peers)])  9.5 us
    unnamed x34, local copies, waits for them, and re-layouts  3.16 us
    ppermute x1, starting transfers between devices, shards(): before = lax.ppermute(pairs[1], 'band', up)  1.91 us
    ppermute x1, starting transfers between devices, shards(): behind = lax.ppermute(pairs[0], 'band', down)  1.6 us
    ppermute x1, starting transfers between devices, shards(): near_rim = lax.ppermute(ends, ('band', 'mp'), outward)  1.41 us
  transfers between devices with their start and end apart: 11, of which 5 were waited for; matrix products, arithmetic and copies ran while one was open for 0% of the time, Pallas kernels for 31%

profile of v2, /device:TPU:0, one launch (start us, length us, event | category | flops | bytes accessed | tf_op | source)
XLA Modules:
  0.0 67.7 jit_solution(18384811481653719236)
XLA Ops:
  0.0 0.0 copy-start.4
  0.0 1.2 %copy-done.4 = bf16[512,1024]{1,0:T(8,128)(2,1)S(1)} copy-done((bf16[512,1024]{1,0:T(8,128)(2,1)S(1)}, bf16[512,1024]{1,0:T(8,128)(2,1)}, u32[]{:S(2)}) %copy-start.4) | copy-done | bytes 1048600
  1.2 0.0 copy-start.12
  1.2 0.0 copy-start.15
  1.2 0.0 copy-start.16
  1.2 0.0 copy-start.9
  1.3 0.0 copy-start
  1.3 3.0 %collective-permute-start.1 = (bf16[128,1024]{1,0:T(8,128)(2,1)S(1)}, bf16[128,1024]{1,0:T(8,128)(2,1)S(1)}, u32[]{:S(2)}, u32[]{:S(2)}) collective-permute-start(bf16[128,1024]{1,0:T(8,128)(2,1)S(1)} %shard_map.147), channel_id=1, source_target_pairs={{1,0},{0,1},{3,2},{2,3},{5,4},{4,5},{7,6},{6,7},{9,8},{8,9},{11,10... | collective-permute-start | bytes 786440 | tf_op jit(solution)/shard_map/ppermute | solution.py:345
  4.3 0.1 shard_map.145
  4.4 0.0 copy-start.5
  4.4 0.1 collective-permute-start.2
  4.5 1.4 %collective-permute-start.3 = (bf16[128,1024]{1,0:T(8,128)(2,1)S(1)}, bf16[128,1024]{1,0:T(8,128)(2,1)S(1)}, u32[]{:S(2)}, u32[]{:S(2)}) collective-permute-start(bf16[128,1024]{1,0:T(8,128)(2,1)S(1)} %shard_map.147), channel_id=1, source_target_pairs={{2,0},{4,2},{6,4},{8,6},{10,8},{12,10},{14,12},{16,14},{18,16},{20... | collective-permute-start | bytes 786440 | tf_op jit(solution)/shard_map/ppermute | solution.py:354
  5.9 5.5 %collective-permute-done.1.refs_0_ = bf16[128,1024]{1,0:T(8,128)(2,1)S(1)} collective-permute-done((bf16[128,1024]{1,0:T(8,128)(2,1)S(1)}, bf16[128,1024]{1,0:T(8,128)(2,1)S(1)}, u32[]{:S(2)}, u32[]{:S(2)}) %collective-permute-start.1) | collective-permute-done | bytes 262176 | tf_op jit(solution)/shard_map/ppermute | solution.py:345
  11.4 1.3 %collective-permute-start.4 = (bf16[128,1024]{1,0:T(8,128)(2,1)S(1)}, bf16[128,1024]{1,0:T(8,128)(2,1)S(1)}, u32[]{:S(2)}, u32[]{:S(2)}) collective-permute-start(bf16[128,1024]{1,0:T(8,128)(2,1)S(1)} %collective-permute-done.1.refs_0_), channel_id=1, source_target_pairs={{0,2},{2,4},{4,6},{6,8},{8,10},{10,12},{12,14},{14,16},{16,18},{18... | collective-permute-start | bytes 786440 | tf_op jit(solution)/shard_map/ppermute | solution.py:364
  12.7 2.1 %collective-permute-start = (bf16[128,1024]{1,0:T(8,128)(2,1)S(1)}, bf16[128,1024]{1,0:T(8,128)(2,1)S(1)}, u32[]{:S(2)}, u32[]{:S(2)}) collective-permute-start(bf16[128,1024]{1,0:T(8,128)(2,1)S(1)} %get-tuple-element.28), channel_id=1, source_target_pairs={{1,0},{0,1},{3,2},{2,3},{5,4},{4,5},{7,6},{6,7},{9,8},{8,9},{11,10... | collective-permute-start | bytes 786440 | tf_op jit(solution)/shard_map/ppermute | solution.py:345
  14.8 0.0 copy-done.12
  14.8 0.0 copy-done.15
  14.9 0.0 copy-done.16
  14.9 0.0 copy-done
  14.9 0.0 copy-start.11
  14.9 1.2 %copy-done.11 = bf16[1024,512]{1,0:T(8,128)(2,1)S(1)} copy-done((bf16[1024,512]{1,0:T(8,128)(2,1)S(1)}, bf16[1024,512]{1,0:T(8,128)(2,1)}, u32[]{:S(2)}) %copy-start.11) | copy-done | bytes 1048600
  16.1 3.0 %shard_map.146 = (f32[256,512]{1,0:T(8,128)S(1)}, f32[256,384]{1,0:T(8,128)S(1)}, f32[256,128]{1,0:T(8,128)S(1)}, f32[256,256]{1,0:T(8,128)S(1)}, bf16[256,512]{1,0:T(8,128)(2,1)S(1)}) custom-call(s32[32,256]{1,0:T(8,128)S(1)} %bitcast.5, s32[1,256]{1,0:T(1,128)S(1)} %bitcast.13, bf16[256,1024]{1,0:T(8,128)(2,1)S(1)} %copy-done, f32[1,1024]{1,0:T(1,128)S(1)} %bitcast.12, ...), custom_call_target="tpu_custom_call" | custom-call | flops 268435456 | bytes 3183616 | tf_op jit(solution)/shard_map/pallas_call | solution.py:31
  19.1 0.0 copy-start.14
  19.2 0.0 copy-done.9
  19.2 0.0 copy-done.8
  19.2 0.0 copy-done.5
  19.2 0.6 copy-done.14
  19.8 3.9 %shard_map.148 = (f32[256,512]{1,0:T(8,128)S(1)}, f32[256,512]{1,0:T(8,128)S(1)}, f32[256,512]{1,0:T(8,128)S(1)}) custom-call(bf16[512,1024]{1,0:T(8,128)(2,1)S(1)} %copy-done.5, f32[256,512]{1,0:T(8,128)S(1)} %get-tuple-element.34.refs_1_, f32[1,1024]{1,0:T(1,128)S(1)} %bitcast.8, bf16[1024,512]{1,0:T(8,128)(2,1)S(1)} %copy-done.8, ...), custom_call_target="tpu_custom_call" | custom-call | flops 2147483648 | bytes 5509120 | tf_op jit(solution)/shard_map/pallas_call | solution.py:31
  23.7 0.0 collective-permute-done.3.refs_0_
  23.8 0.0 collective-permute-done.4.refs_1_
  23.8 3.2 %shard_map.149 = (f32[256,512]{1,0:T(8,128)S(1)}, f32[256,512]{1,0:T(8,128)S(1)}, f32[256,512]{1,0:T(8,128)S(1)}) custom-call(bf16[128,1024]{1,0:T(8,128)(2,1)S(1)} %collective-permute-done.3.refs_0_, bf16[128,1024]{1,0:T(8,128)(2,1)S(1)} %collective-permute-done.4.refs_1_, f32[256,256]{1,0:T(8,128)S(1)} %get-tuple-element.33.refs_2_, ...), custom_call_target="tpu_custom_call" | custom-call | flops 1073741824 | bytes 6295552 | tf_op jit(solution)/shard_map/pallas_call | solution.py:31
  27.0 0.0 collective-permute-done.2.refs_1_
  27.0 0.0 copy-start.6
  27.0 0.0 copy-start.10
  27.0 4.7 %shard_map.150 = (f32[256,512]{1,0:T(8,128)S(1)}, f32[256,512]{1,0:T(8,128)S(1)}, f32[256,512]{1,0:T(8,128)S(1)}) custom-call(bf16[128,1024]{1,0:T(8,128)(2,1)S(1)} %collective-permute-done.1.refs_0_, bf16[256,1024]{1,0:T(8,128)(2,1)S(1)} %collective-permute-done.2.refs_1_, f32[256,384]{1,0:T(8,128)S(1)} %get-tuple-element.32.refs_2_, ...), custom_call_target="tpu_custom_call" | custom-call | flops 1610612736 | bytes 6688768 | tf_op jit(solution)/shard_map/pallas_call | solution.py:31
  31.7 0.0 collective-permute-done.refs_0_
  31.8 0.0 copy-done.6
  31.8 0.0 copy-done.10
  31.8 1.5 %shard_map.151 = (bf16[128,1024]{1,0:T(8,128)(2,1)S(1)}, bf16[128,512]{1,0:T(8,128)(2,1)S(1)}, bf16[128,512]{1,0:T(8,128)(2,1)S(1)}) custom-call(bf16[128,1024]{1,0:T(8,128)(2,1)S(1)} %collective-permute-done.refs_0_, f32[256,128]{1,0:T(8,128)S(1)} %get-tuple-element.29.refs_1_.log, f32[1,1024]{1,0:T(1,128)S(1)} %bitcast.11, ...), custom_call_target="tpu_custom_call" | custom-call | flops 536870912 | bytes 5902336 | tf_op jit(solution)/shard_map/pallas_call | solution.py:31
  33.3 0.1 collective-permute-start.5
  33.4 0.0 copy-start.13
  33.4 1.1 %shard_map.152.own.refs_1_ = bf16[128,1024]{1,0:T(8,128)(2,1)S(1)} custom-call(f32[256,128]{1,0:T(8,128)S(1)} %get-tuple-element.29.refs_1_.log, bf16[256,512]{1,0:T(8,128)(2,1)S(1)} %get-tuple-element.30.refs_5_.refs_6_.query, bf16[128,512]{1,0:T(8,128)(2,1)S(1)} %get-tuple-element.45.keys, bf16[128,512]{1,0:T(8,128)(2,1)S(1)} %get-tuple-element.46.values, ...), custom_call_target="tpu_custom_call" | custom-call | flops 134217728 | bytes 3538944 | tf_op jit(solution)/shard_map/pallas_call | solution.py:31
  34.5 2.0 %collective-permute-start.6 = (bf16[128,1024]{1,0:T(8,128)(2,1)S(1)}, bf16[128,1024]{1,0:T(8,128)(2,1)S(1)}, u32[]{:S(2)}, u32[]{:S(2)}) collective-permute-start(bf16[128,1024]{1,0:T(8,128)(2,1)S(1)} %shard_map.152.own.refs_1_), channel_id=1, source_target_pairs={{1,0},{0,1},{3,2},{2,3},{5,4},{4,5},{7,6},{6,7},{9,8},{8,9},{11,10... | collective-permute-start | bytes 786440 | tf_op jit(solution)/shard_map/ppermute | solution.py:345
  36.5 6.0 %collective-permute-done.5.other.refs_2_ = bf16[128,1024]{1,0:T(8,128)(2,1)S(1)} collective-permute-done((bf16[128,1024]{1,0:T(8,128)(2,1)S(1)}, bf16[128,1024]{1,0:T(8,128)(2,1)S(1)}, u32[]{:S(2)}, u32[]{:S(2)}) %collective-permute-start.5) | collective-permute-done | bytes 262176 | tf_op jit(solution)/shard_map/ppermute | solution.py:345
  42.5 0.0 copy-done.1
  42.5 0.0 copy-done.2
  42.5 0.0 copy-done.3
  42.5 0.0 copy-done.13
  42.6 0.8 %shard_map.153 = (bf16[128,512]{1,0:T(8,128)(2,1)S(1)}, bf16[128,1024]{1,0:T(8,128)(2,1)S(1)}) custom-call(bf16[256,1024]{1,0:T(8,128)(2,1)S(1)} %copy-done, bf16[128,1024]{1,0:T(8,128)(2,1)S(1)} %get-tuple-element.44.own.refs_0_, bf16[128,1024]{1,0:T(8,128)(2,1)S(1)} %collective-permute-done.5.other.refs_2_, f32[1,1024]{1,0:T(1,128)S(1)} %bitcast.6, ...), custom_call_target="tpu_custom_call" | custom-call | flops 402653184 | bytes 4591616 | tf_op jit(solution)/shard_map/pallas_call | solution.py:31
  43.4 0.0 copy-start.7
  43.4 1.6 %collective-permute-start.8 = (bf16[128,1024]{1,0:T(8,128)(2,1)S(1)}, bf16[128,1024]{1,0:T(8,128)(2,1)S(1)}, u32[]{:S(2)}, u32[]{:S(2)}) collective-permute-start(bf16[128,1024]{1,0:T(8,128)(2,1)S(1)} %get-tuple-element.48.low), channel_id=1, source_target_pairs={{2,0},{4,2},{6,4},{8,6},{10,8},{12,10},{14,12},{16,14},{18,16},{20... | collective-permute-start | bytes 786440 | tf_op jit(solution)/shard_map/ppermute | solution.py:422
  45.0 3.0 %collective-permute-done.6.other.refs_3_ = bf16[128,1024]{1,0:T(8,128)(2,1)S(1)} collective-permute-done((bf16[128,1024]{1,0:T(8,128)(2,1)S(1)}, bf16[128,1024]{1,0:T(8,128)(2,1)S(1)}, u32[]{:S(2)}, u32[]{:S(2)}) %collective-permute-start.6) | collective-permute-done | bytes 262176 | tf_op jit(solution)/shard_map/ppermute | solution.py:345
  48.0 0.8 %shard_map.154 = (bf16[128,512]{1,0:T(8,128)(2,1)S(1)}, bf16[128,1024]{1,0:T(8,128)(2,1)S(1)}) custom-call(bf16[256,1024]{1,0:T(8,128)(2,1)S(1)} %copy-done, bf16[128,1024]{1,0:T(8,128)(2,1)S(1)} %shard_map.152.own.refs_1_, bf16[128,1024]{1,0:T(8,128)(2,1)S(1)} %collective-permute-done.6.other.refs_3_, f32[1,1024]{1,0:T(1,128)S(1)} %bitcast.7, ...), custom_call_target="tpu_custom_call" | custom-call | flops 402653184 | bytes 4591616 | tf_op jit(solution)/shard_map/pallas_call | solution.py:31
  48.8 1.9 %collective-permute-start.7 = (bf16[128,1024]{1,0:T(8,128)(2,1)S(1)}, bf16[128,1024]{1,0:T(8,128)(2,1)S(1)}, u32[]{:S(2)}, u32[]{:S(2)}) collective-permute-start(bf16[128,1024]{1,0:T(8,128)(2,1)S(1)} %get-tuple-element.49.high), channel_id=1, source_target_pairs={{0,2},{2,4},{4,6},{6,8},{8,10},{10,12},{12,14},{14,16},{16,18},{18... | collective-permute-start | bytes 786440 | tf_op jit(solution)/shard_map/ppermute | solution.py:423
  50.8 0.0 collective-permute-done.8.halo
  50.8 0.0 copy-done.7
  50.8 1.6 %shard_map.156.refs_5_ = bf16[128,1024]{1,0:T(8,128)(2,1)S(1)} custom-call(bf16[128,512]{1,0:T(8,128)(2,1)S(1)} %get-tuple-element.50.query, bf16[128,1024]{1,0:T(8,128)(2,1)S(1)} %get-tuple-element.48.low, bf16[128,1024]{1,0:T(8,128)(2,1)S(1)} %get-tuple-element.49.high, bf16[128,1024]{1,0:T(8,128)(2,1)S(1)} %collective-permute-done.8.halo, ...), custom_call_target="tpu_custom_call" | custom-call | flops 134217728 | bytes 2228224 | tf_op jit(solution)/shard_map/pallas_call | solution.py:31
  52.4 0.1 collective-permute-start.10
  52.5 0.0 collective-permute-done.7.halo
  52.5 1.6 %shard_map.155.refs_4_ = bf16[128,1024]{1,0:T(8,128)(2,1)S(1)} custom-call(bf16[128,512]{1,0:T(8,128)(2,1)S(1)} %get-tuple-element.47.query, bf16[128,1024]{1,0:T(8,128)(2,1)S(1)} %get-tuple-element.48.low, bf16[128,1024]{1,0:T(8,128)(2,1)S(1)} %get-tuple-element.49.high, bf16[128,1024]{1,0:T(8,128)(2,1)S(1)} %collective-permute-done.7.halo, ...), custom_call_target="tpu_custom_call" | custom-call | flops 134217728 | bytes 2228224 | tf_op jit(solution)/shard_map/pallas_call | solution.py:31
  54.1 2.1 %collective-permute-start.9 = (bf16[128,1024]{1,0:T(8,128)(2,1)S(1)}, bf16[128,1024]{1,0:T(8,128)(2,1)S(1)}, u32[]{:S(2)}, u32[]{:S(2)}) collective-permute-start(bf16[128,1024]{1,0:T(8,128)(2,1)S(1)} %shard_map.155.refs_4_), channel_id=1, source_target_pairs={{1,0},{0,1},{3,2},{2,3},{5,4},{4,5},{7,6},{6,7},{9,8},{8,9},{11,10... | collective-permute-start | bytes 786440 | tf_op jit(solution)/shard_map/ppermute | solution.py:345
  56.1 4.9 %collective-permute-done.10.refs_7_ = bf16[128,1024]{1,0:T(8,128)(2,1)S(1)} collective-permute-done((bf16[128,1024]{1,0:T(8,128)(2,1)S(1)}, bf16[128,1024]{1,0:T(8,128)(2,1)S(1)}, u32[]{:S(2)}, u32[]{:S(2)}) %collective-permute-start.10) | collective-permute-done | bytes 262176 | tf_op jit(solution)/shard_map/ppermute | solution.py:345
  61.0 5.6 %collective-permute-done.9.refs_6_ = bf16[128,1024]{1,0:T(8,128)(2,1)S(1)} collective-permute-done((bf16[128,1024]{1,0:T(8,128)(2,1)S(1)}, bf16[128,1024]{1,0:T(8,128)(2,1)S(1)}, u32[]{:S(2)}, u32[]{:S(2)}) %collective-permute-start.9) | collective-permute-done | bytes 262176 | tf_op jit(solution)/shard_map/ppermute | solution.py:345
  66.6 1.1 %shard_map.157 = bf16[256,1024]{1,0:T(8,128)(2,1)} custom-call(bf16[256,1024]{1,0:T(8,128)(2,1)S(1)} %copy-done, bf16[128,1024]{1,0:T(8,128)(2,1)S(1)} %get-tuple-element.44.own.refs_0_, bf16[128,1024]{1,0:T(8,128)(2,1)S(1)} %shard_map.152.own.refs_1_, bf16[128,1024]{1,0:T(8,128)(2,1)S(1)} %collective-permute-done.5.other.refs_2_, ...), custom_call_target="tpu_custom_call" | custom-call | bytes 3145728 | tf_op jit(solution)/shard_map/pallas_call | solution.py:31
  (5 shorter events, 0.0 us)
Async XLA Ops:
  0.0 1.2 %copy-start.4 = (bf16[512,1024]{1,0:T(8,128)(2,1)S(1)}, bf16[512,1024]{1,0:T(8,128)(2,1)}, u32[]{:S(2)}) copy-start(bf16[512,1024]{1,0:T(8,128)(2,1)} %refs_0_.5) | copy-start | bytes 3145732
  1.2 13.6 %copy-start.12 = (s32[256,32]{0,1:T(8,128)S(1)}, s32[256,32]{0,1:T(8,128)}, u32[]{:S(2)}) copy-start(s32[256,32]{0,1:T(8,128)} %param.23) | copy-start | bytes 98308
  1.2 13.6 %copy-start.15 = (f32[1024]{0:T(1024)S(1)}, f32[1024]{0:T(1024)}, u32[]{:S(2)}) copy-start(f32[1024]{0:T(1024)} %param.18) | copy-start | bytes 12292
  1.2 13.6 %copy-start.16 = (s32[256]{0:T(256)S(1)}, s32[256]{0:T(256)}, u32[]{:S(2)}) copy-start(s32[256]{0:T(256)} %param.24) | copy-start | bytes 3076
  1.2 17.9 %copy-start.9 = (bf16[1024,512]{1,0:T(8,128)(2,1)S(1)}, bf16[1024,512]{1,0:T(8,128)(2,1)}, u32[]{:S(2)}) copy-start(bf16[1024,512]{1,0:T(8,128)(2,1)} %refs_4_.7) | copy-start | bytes 3145732
  1.3 13.6 %copy-start = (bf16[256,1024]{1,0:T(8,128)(2,1)S(1)}, bf16[256,1024]{1,0:T(8,128)(2,1)}, u32[]{:S(2)}) copy-start(bf16[256,1024]{1,0:T(8,128)(2,1)} %hidden.7) | copy-start | bytes 1572868
  1.3 10.1 %collective-permute-start.1 = (bf16[128,1024]{1,0:T(8,128)(2,1)S(1)}, bf16[128,1024]{1,0:T(8,128)(2,1)S(1)}, u32[]{:S(2)}, u32[]{:S(2)}) collective-permute-start(bf16[128,1024]{1,0:T(8,128)(2,1)S(1)} %shard_map.147), channel_id=1, source_target_pairs={{1,0},{0,1},{3,2},{2,3},{5,4},{4,5},{7,6},{6,7},{9,8},{8,9},{11,10... | collective-permute-start | bytes 786440 | tf_op jit(solution)/shard_map/ppermute | solution.py:345
  4.3 14.9 %copy-start.8 = (bf16[1024,512]{1,0:T(8,128)(2,1)S(1)}, bf16[1024,512]{1,0:T(8,128)(2,1)}, u32[]{:S(2)}) copy-start(bf16[1024,512]{1,0:T(8,128)(2,1)} %refs_3_.3) | copy-start | bytes 3145732
  4.4 14.8 %copy-start.5 = (bf16[512,1024]{1,0:T(8,128)(2,1)S(1)}, bf16[512,1024]{1,0:T(8,128)(2,1)}, u32[]{:S(2)}) copy-start(bf16[512,1024]{1,0:T(8,128)(2,1)} %refs_0_.5) | copy-start | bytes 3145732
  4.4 22.6 %collective-permute-start.2 = (bf16[256,1024]{1,0:T(8,128)(2,1)S(1)}, bf16[256,1024]{1,0:T(8,128)(2,1)S(1)}, u32[]{:S(2)}, u32[]{:S(2)}) collective-permute-start(bf16[256,1024]{1,0:T(8,128)(2,1)S(1)} %get-tuple-element.31), channel_id=1, source_target_pairs={{1,0},{0,1},{3,2},{2,3},{5,4},{4,5},{7,6},{6,7},{9,8},{8,9},{11,10... | collective-permute-start | bytes 1572872 | tf_op jit(solution)/shard_map/ppermute | solution.py:345
  4.5 19.3 %collective-permute-start.3 = (bf16[128,1024]{1,0:T(8,128)(2,1)S(1)}, bf16[128,1024]{1,0:T(8,128)(2,1)S(1)}, u32[]{:S(2)}, u32[]{:S(2)}) collective-permute-start(bf16[128,1024]{1,0:T(8,128)(2,1)S(1)} %shard_map.147), channel_id=1, source_target_pairs={{2,0},{4,2},{6,4},{8,6},{10,8},{12,10},{14,12},{16,14},{18,16},{20... | collective-permute-start | bytes 786440 | tf_op jit(solution)/shard_map/ppermute | solution.py:354
  11.4 12.3 %collective-permute-start.4 = (bf16[128,1024]{1,0:T(8,128)(2,1)S(1)}, bf16[128,1024]{1,0:T(8,128)(2,1)S(1)}, u32[]{:S(2)}, u32[]{:S(2)}) collective-permute-start(bf16[128,1024]{1,0:T(8,128)(2,1)S(1)} %collective-permute-done.1.refs_0_), channel_id=1, source_target_pairs={{0,2},{2,4},{4,6},{6,8},{8,10},{10,12},{12,14},{14,16},{16,18},{18... | collective-permute-start | bytes 786440 | tf_op jit(solution)/shard_map/ppermute | solution.py:364
  12.7 19.0 %collective-permute-start = (bf16[128,1024]{1,0:T(8,128)(2,1)S(1)}, bf16[128,1024]{1,0:T(8,128)(2,1)S(1)}, u32[]{:S(2)}, u32[]{:S(2)}) collective-permute-start(bf16[128,1024]{1,0:T(8,128)(2,1)S(1)} %get-tuple-element.28), channel_id=1, source_target_pairs={{1,0},{0,1},{3,2},{2,3},{5,4},{4,5},{7,6},{6,7},{9,8},{8,9},{11,10... | collective-permute-start | bytes 786440 | tf_op jit(solution)/shard_map/ppermute | solution.py:345
  14.9 1.2 %copy-start.11 = (bf16[1024,512]{1,0:T(8,128)(2,1)S(1)}, bf16[1024,512]{1,0:T(8,128)(2,1)}, u32[]{:S(2)}) copy-start(bf16[1024,512]{1,0:T(8,128)(2,1)} %wq.3) | copy-start | bytes 3145732
  19.1 0.7 %copy-start.14 = (f32[1024]{0:T(1024)S(1)}, f32[1024]{0:T(1024)}, u32[]{:S(2)}) copy-start(f32[1024]{0:T(1024)} %param.16) | copy-start | bytes 12292
  27.0 4.8 %copy-start.6 = (bf16[512,1024]{1,0:T(8,128)(2,1)S(1)}, bf16[512,1024]{1,0:T(8,128)(2,1)}, u32[]{:S(2)}) copy-start(bf16[512,1024]{1,0:T(8,128)(2,1)} %wo.3) | copy-start | bytes 3145732
  27.0 4.8 %copy-start.10 = (bf16[1024,512]{1,0:T(8,128)(2,1)S(1)}, bf16[1024,512]{1,0:T(8,128)(2,1)}, u32[]{:S(2)}) copy-start(bf16[1024,512]{1,0:T(8,128)(2,1)} %refs_4_.7) | copy-start | bytes 3145732
  33.3 9.2 %collective-permute-start.5 = (bf16[128,1024]{1,0:T(8,128)(2,1)S(1)}, bf16[128,1024]{1,0:T(8,128)(2,1)S(1)}, u32[]{:S(2)}, u32[]{:S(2)}) collective-permute-start(bf16[128,1024]{1,0:T(8,128)(2,1)S(1)} %get-tuple-element.44.own.refs_0_), channel_id=1, source_target_pairs={{1,0},{0,1},{3,2},{2,3},{5,4},{4,5},{7,6},{6,7},{9,8},{8,9},{11,10... | collective-permute-start | bytes 786440 | tf_op jit(solution)/shard_map/ppermute | solution.py:345
  33.4 9.1 %copy-start.1 = (bf16[1024,512]{1,0:T(8,128)(2,1)S(1)}, bf16[1024,512]{1,0:T(8,128)(2,1)}, u32[]{:S(2)}) copy-start(bf16[1024,512]{1,0:T(8,128)(2,1)} %wq.5) | copy-start | bytes 3145732
  33.4 9.1 %copy-start.2 = (bf16[1024,512]{1,0:T(8,128)(2,1)S(1)}, bf16[1024,512]{1,0:T(8,128)(2,1)}, u32[]{:S(2)}) copy-start(bf16[1024,512]{1,0:T(8,128)(2,1)} %wk.3) | copy-start | bytes 3145732
  33.4 9.1 %copy-start.3 = (bf16[1024,512]{1,0:T(8,128)(2,1)S(1)}, bf16[1024,512]{1,0:T(8,128)(2,1)}, u32[]{:S(2)}) copy-start(bf16[1024,512]{1,0:T(8,128)(2,1)} %wv.3) | copy-start | bytes 3145732
  33.4 9.1 %copy-start.13 = (f32[1024]{0:T(1024)S(1)}, f32[1024]{0:T(1024)}, u32[]{:S(2)}) copy-start(f32[1024]{0:T(1024)} %param.25) | copy-start | bytes 12292
  34.5 13.5 %collective-permute-start.6 = (bf16[128,1024]{1,0:T(8,128)(2,1)S(1)}, bf16[128,1024]{1,0:T(8,128)(2,1)S(1)}, u32[]{:S(2)}, u32[]{:S(2)}) collective-permute-start(bf16[128,1024]{1,0:T(8,128)(2,1)S(1)} %shard_map.152.own.refs_1_), channel_id=1, source_target_pairs={{1,0},{0,1},{3,2},{2,3},{5,4},{4,5},{7,6},{6,7},{9,8},{8,9},{11,10... | collective-permute-start | bytes 786440 | tf_op jit(solution)/shard_map/ppermute | solution.py:345
  43.4 7.4 %copy-start.7 = (bf16[512,1024]{1,0:T(8,128)(2,1)S(1)}, bf16[512,1024]{1,0:T(8,128)(2,1)}, u32[]{:S(2)}) copy-start(bf16[512,1024]{1,0:T(8,128)(2,1)} %wo.5) | copy-start | bytes 3145732
  43.4 7.4 %collective-permute-start.8 = (bf16[128,1024]{1,0:T(8,128)(2,1)S(1)}, bf16[128,1024]{1,0:T(8,128)(2,1)S(1)}, u32[]{:S(2)}, u32[]{:S(2)}) collective-permute-start(bf16[128,1024]{1,0:T(8,128)(2,1)S(1)} %get-tuple-element.48.low), channel_id=1, source_target_pairs={{2,0},{4,2},{6,4},{8,6},{10,8},{12,10},{14,12},{16,14},{18,16},{20... | collective-permute-start | bytes 786440 | tf_op jit(solution)/shard_map/ppermute | solution.py:422
  48.8 3.6 %collective-permute-start.7 = (bf16[128,1024]{1,0:T(8,128)(2,1)S(1)}, bf16[128,1024]{1,0:T(8,128)(2,1)S(1)}, u32[]{:S(2)}, u32[]{:S(2)}) collective-permute-start(bf16[128,1024]{1,0:T(8,128)(2,1)S(1)} %get-tuple-element.49.high), channel_id=1, source_target_pairs={{0,2},{2,4},{4,6},{6,8},{8,10},{10,12},{12,14},{14,16},{16,18},{18... | collective-permute-start | bytes 786440 | tf_op jit(solution)/shard_map/ppermute | solution.py:423
  52.4 8.6 %collective-permute-start.10 = (bf16[128,1024]{1,0:T(8,128)(2,1)S(1)}, bf16[128,1024]{1,0:T(8,128)(2,1)S(1)}, u32[]{:S(2)}, u32[]{:S(2)}) collective-permute-start(bf16[128,1024]{1,0:T(8,128)(2,1)S(1)} %shard_map.156.refs_5_), channel_id=1, source_target_pairs={{1,0},{0,1},{3,2},{2,3},{5,4},{4,5},{7,6},{6,7},{9,8},{8,9},{11,10... | collective-permute-start | bytes 786440 | tf_op jit(solution)/shard_map/ppermute | solution.py:345
  54.1 12.6 %collective-permute-start.9 = (bf16[128,1024]{1,0:T(8,128)(2,1)S(1)}, bf16[128,1024]{1,0:T(8,128)(2,1)S(1)}, u32[]{:S(2)}, u32[]{:S(2)}) collective-permute-start(bf16[128,1024]{1,0:T(8,128)(2,1)S(1)} %shard_map.155.refs_4_), channel_id=1, source_target_pairs={{1,0},{0,1},{3,2},{2,3},{5,4},{4,5},{7,6},{6,7},{9,8},{8,9},{11,10... | collective-permute-start | bytes 786440 | tf_op jit(solution)/shard_map/ppermute | solution.py:345

commit v3 on v2

--- a/solution.py
+++ b/solution.py
@@ -15,7 +15,7 @@
 
 EPSILON = 1e-05
 NEG = -1e30
-VMEM_LIMIT = 48 * 1024 * 1024
+VMEM_LIMIT = 24 * 1024 * 1024
 
 f32 = jnp.float32
 bf16 = jnp.bfloat16
@@ -86,25 +86,19 @@
     return jnp.where(even_lanes(rows), stacked[:rows], stacked[rows:])
 
 
-def attend(query, parts):
-    both = two_heads(query)
-    scores = []
-    top = None
-    for keys, _, bias in parts:
-        part = dot_nt(both, keys)
-        if bias is not None:
-            part = part + jnp.concatenate([bias, bias], axis=0)
-        scores.append(part)
-        peak = jnp.max(part, axis=1, keepdims=True)
-        top = peak if top is None else jnp.maximum(top, peak)
-    out = None
-    for (_, values, _), part in zip(parts, scores):
-        weights = jnp.exp(part - top).astype(bf16)
-        wide = jnp.concatenate([values, jnp.ones_like(values)], axis=1)
-        add = dot(weights, wide)
-        out = add if out is None else out + add
-    top = jnp.broadcast_to(top, (top.shape[0], LANES))
-    return fold_heads(out[:, :LANES]), fold_heads(out[:, LANES:]), fold_heads(top)
+def attend(query, keys, values, bias):
+    bias = jnp.concatenate([bias, bias], axis=0)
+    pairs = [slice(p, p + LANES) for p in range(0, query.shape[1], LANES)]
+    scores = [dot_nt(two_heads(query[:, cols]), keys[:, cols]) + bias for cols in pairs]
+    tops = [jnp.max(s, axis=1, keepdims=True) for s in scores]
+    weights = [jnp.exp(s - top).astype(bf16) for s, top in zip(scores, tops)]
+    states = []
+    for cols, part, top in zip(pairs, weights, tops):
+        wide = jnp.concatenate([values[:, cols], jnp.ones_like(values[:, cols])], axis=1)
+        out = dot(part, wide)
+        top = jnp.broadcast_to(top, (top.shape[0], LANES))
+        states.append((fold_heads(out[:, :LANES]), fold_heads(out[:, LANES:]), fold_heads(top)))
+    return states
 
 
 def merge(one, two):
@@ -203,9 +197,8 @@
 
 
 def encode_heads(query, log, keys, values, before, at, heads):
-    for p in range(query.shape[1] // LANES):
+    for p, state in enumerate(attend(query[at, :], keys, values, log[at, :])):
         cols = slice(p * LANES, (p + 1) * LANES)
-        state = attend(query[at, cols], [(keys[:, cols], values[:, cols], log[at, :])])
         if before is not None:
             state = merge([b[at, cols] for b in before], state)
         heads[:, cols] = (state[0] / state[1]).astype(bf16)
@@ -230,9 +223,8 @@
         encode_heads(query, log, keys, values, before, slice(0, heads.shape[0]), heads)
         share[...] = dot(heads[...], wo[...]).astype(bf16)
         return
-    for p in range(query.shape[1] // LANES):
+    for p, state in enumerate(attend(query, keys, values, log[...])):
         cols = slice(p * LANES, (p + 1) * LANES)
-        state = attend(query[:, cols], [(keys[:, cols], values[:, cols], log[...])])
         if before is not None:
             state = merge([b[:, cols] for b in before], state)
         for ref, value in zip(after, state):
@@ -291,23 +283,40 @@
     places = [(low, 0), (high, low.shape[0]), (halo, reach)]
     biases = [window_bias(rows, ref.shape[0], shift - start) for ref, shift in places]
     biases[2] = biases[2] + end
-    for p in range(columns // LANES):
-        cols = slice(p * LANES, (p + 1) * LANES)
-        vals = slice(columns + p * LANES, columns + (p + 1) * LANES)
-        parts = [(ref[:, cols], ref[:, vals], b) for (ref, _), b in zip(places, biases)]
-        out, total, _ = attend(query[:, cols], parts)
-        heads[:, cols] = (out / total).astype(bf16)
+    keys, values = [
+        jnp.concatenate([ref[:, at : at + columns] for ref, _ in places], axis=0) for at in (0, columns)
+    ]
+    for p, (out, total, _) in enumerate(attend(query, keys, values, jnp.concatenate(biases, axis=1))):
+        heads[:, p * LANES : (p + 1) * LANES] = (out / total).astype(bf16)
     share[...] = dot(heads[...], wo[...]).astype(bf16)
 
 
-def mixed_kernel(hidden, *refs):
-    own, other, own_share, other_share = [refs[2 * i : 2 * i + 2] for i in range(4)]
-    mixed = refs[-1]
-    half = own[0].shape[0]
-    for i in range(2):
-        latent = latent_of(i * half, hidden, own[i], other[i])
-        total = own_share[i][...].astype(f32) + other_share[i][...].astype(f32)
-        mixed[i * half : (i + 1) * half, :] = (latent + total).astype(bf16)
+def mixed_kernel(at, hidden, own, other, own_share, other_share, *refs):
+    result, half, sem = refs[-3:]
+    total = own_share[...].astype(f32) + other_share[...].astype(f32)
+    half[...] = (latent_of(at, hidden, own, other) + total).astype(bf16)
+    copy = pltpu.make_async_copy(half, result.at[pl.ds(at, own.shape[0]), :], sem)
+    copy.start()
+    copy.wait()
+
+
+def mix_half(at, hidden, own, other, own_share, other_share, mixed):
+    args = [hidden, own, other, own_share, other_share]
+    specs = [whole(a.shape) for a in args]
+    aliases = {}
+    if not isinstance(mixed, jax.ShapeDtypeStruct):
+        args.append(mixed)
+        specs.append(pl.BlockSpec(memory_space=pltpu.HBM))
+        aliases = {len(args) - 1: 0}
+    return pl.pallas_call(
+        functools.partial(mixed_kernel, at),
+        out_shape=shape_of(*mixed.shape, dtype=mixed.dtype),
+        in_specs=specs,
+        out_specs=pl.BlockSpec(memory_space=pltpu.HBM),
+        scratch_shapes=[pltpu.VMEM(own.shape, mixed.dtype), pltpu.SemaphoreType.DMA],
+        input_output_aliases=aliases,
+        compiler_params=pltpu.CompilerParams(vmem_limit_bytes=VMEM_LIMIT),
+    )(*args)
 
 
 def after(value, *others):
@@ -349,6 +358,7 @@
         cut = min(rows - rim, max(LANES, (rows - rim) // 3 * 2 // LANES * LANES))
         (ends,) = pick([grid_latent], [(0, lambda: me() * (rows - rim), rim)])
         edge = shifted(ends, 1)
+        up, down = up + [(bands - 1, 0)], down + [(0, bands - 1)]
         outward = [(2 * a, 2 * b) for a, b in down] + [(2 * a + 1, 2 * b + 1) for a, b in up]
         inward = [(2 * a, 2 * b) for a, b in up] + [(2 * a + 1, 2 * b + 1) for a, b in down]
         near_rim = lax.ppermute(ends, ("band", "mp"), outward)
@@ -361,8 +371,7 @@
         )
         middle = shifted(middle, 1)
         final = shifted(final, 1)
-        far_rim = lax.ppermute(edge, ("band", "mp"), inward)
-        groups = [[grid_latent], [edge, middle], [final], [near_rim, far_rim]]
+        groups = [[grid_latent], [edge, middle], [final], [near_rim, near_rim]]
     else:
         me = lax.axis_index("mp")
         pieces = [grid_latent] + [shifted(grid_latent, d) for d in range(1, peers)]
@@ -385,6 +394,9 @@
         ],
         2 * nodes * enc_wq.size,
     )
+    if peers == 2:
+        far_rim = lax.ppermute(after(edge, query), ("band", "mp"), inward)
+        groups[3] = [near_rim, far_rim]
     encode = functools.partial(grid_attention, gain=grid_gain, wk=enc_wk, wv=enc_wv, query=query)
     order = [0, 3, 1, 2] if peers == 2 else range(len(groups))
     state = None
@@ -433,11 +445,10 @@
     other_shares = [None, None]
     for i in (1, 0):
         other_shares[i] = exchange(shares[i])
-    return call(
-        mixed_kernel,
-        [shape_of(*hidden_in.shape, dtype=bf16)],
-        [hidden_in, *own, *other, *shares, *other_shares],
-    )[0]
+    mixed = shape_of(*hidden_in.shape, dtype=bf16)
+    for i in (1, 0):
+        mixed = mix_half(i * half, hidden_in, own[i], other[i], shares[i], other_shares[i], mixed)
+    return mixed
 
 
 def solution(mesh):

time: 68.1 us -> 60.3 us (0.89)
  Pallas kernels: 23.5 us -> 19.9 us
  waiting for transfers between devices: 25.1 us -> 22 us
    ppermute x7, waiting for transfers between devices: 25 us -> 14 us  [shifted(): lax.ppermute(value, 'mp', [((i + by) % peers, i) for i in range(peers)])]
    ppermute x1, waiting for transfers between devices: 0.01 us -> 5.46 us  [shards(): before = lax.ppermute(pairs[1], 'band', up)]
    pallas_call x11 -> x10, Pallas kernels: 23.4 us -> 18 us  [call(): pl.pallas_call(kernel, out_shape=outs, in_specs=[whole(a.shape) for a in...]
    ppermute x1, starting transfers between devices: 1.41 us -> 3.94 us  [shards(): near_rim = lax.ppermute(ends, ('band', 'mp'), outward)]
    ppermute x1, waiting for transfers between devices: 0.01 us -> 2.09 us  [shards(): far_rim = lax.ppermute(after(edge, query), ('band', 'mp'), inward)]
    ppermute x1, starting transfers between devices: 1.91 us -> 0.06 us  [shards(): before = lax.ppermute(pairs[1], 'band', up)]
    pallas_call x0 -> x2, Pallas kernels: none -> 1.81 us  [mix_half(): pl.pallas_call(functools.partial(mixed_kernel, at), out_shape=shape_of(*m...]
    ppermute x7, starting transfers between devices: 9.5 us -> 11 us  [shifted(): lax.ppermute(value, 'mp', [((i + by) % peers, i) for i in range(peers)])]
  transfers between devices with their start and end apart: 11 -> 11, of which waited for: 5 -> 7; matrix products, arithmetic and copies ran while one was open for 0% -> 0% of each run, Pallas kernels for 31% -> 29%
where the time goes in v3:
time: 60.3 us; the launch traced here: 60.1 us
  waiting for transfers between devices  22 us (36%)
  Pallas kernels  19.9 us (33%)
  starting transfers between devices  15.5 us (26%)
  local copies, waits for them, and re-layouts  2.51 us (4%)
    pallas_call x10, Pallas kernels, call(): pl.pallas_call(kernel, out_shape=outs, in_specs=[whole(a.shape) for a in...  18 us
    ppermute x7, waiting for transfers between devices, shifted(): lax.ppermute(value, 'mp', [((i + by) % peers, i) for i in range(peers)])  14 us
    ppermute x7, starting transfers between devices, shifted(): lax.ppermute(value, 'mp', [((i + by) % peers, i) for i in range(peers)])  11 us
    ppermute x1, waiting for transfers between devices, shards(): before = lax.ppermute(pairs[1], 'band', up)  5.46 us
    ppermute x1, starting transfers between devices, shards(): near_rim = lax.ppermute(ends, ('band', 'mp'), outward)  3.94 us
    unnamed x32, local copies, waits for them, and re-layouts  2.51 us
    ppermute x1, waiting for transfers between devices, shards(): far_rim = lax.ppermute(after(edge, query), ('band', 'mp'), inward)  2.09 us
    pallas_call x2, Pallas kernels, mix_half(): pl.pallas_call(functools.partial(mixed_kernel, at), out_shape=shape_of(*m...  1.81 us
  transfers between devices with their start and end apart: 11, of which 7 were waited for; matrix products, arithmetic and copies ran while one was open for 0% of the time, Pallas kernels for 29%

profile of v3, /device:TPU:0, one launch (start us, length us, event | category | flops | bytes accessed | tf_op | source)
XLA Modules:
  0.0 60.1 jit_solution(479584327348919287)
XLA Ops:
  0.0 0.0 copy-start.4
  0.0 1.2 %copy-done.4 = bf16[512,1024]{1,0:T(8,128)(2,1)S(1)} copy-done((bf16[512,1024]{1,0:T(8,128)(2,1)S(1)}, bf16[512,1024]{1,0:T(8,128)(2,1)}, u32[]{:S(2)}) %copy-start.4) | copy-done | bytes 1048600
  1.2 0.0 copy-start.11
  1.2 0.0 copy-start.14
  1.2 0.0 copy-start.15
  1.2 0.0 copy-start.9
  1.3 0.0 copy-start
  1.3 3.0 %collective-permute-start.1 = (bf16[128,1024]{1,0:T(8,128)(2,1)S(1)}, bf16[128,1024]{1,0:T(8,128)(2,1)S(1)}, u32[]{:S(2)}, u32[]{:S(2)}) collective-permute-start(bf16[128,1024]{1,0:T(8,128)(2,1)S(1)} %shard_map.147), channel_id=1, source_target_pairs={{1,0},{0,1},{3,2},{2,3},{5,4},{4,5},{7,6},{6,7},{9,8},{8,9},{11,10... | collective-permute-start | bytes 786440 | tf_op jit(solution)/shard_map/ppermute | solution.py:354
  4.3 0.0 copy-start.8
  4.3 0.1 shard_map.145
  4.4 0.0 copy-start.5
  4.4 0.1 collective-permute-start.2
  4.5 3.9 %collective-permute-start.3 = (bf16[128,1024]{1,0:T(8,128)(2,1)S(1)}, bf16[128,1024]{1,0:T(8,128)(2,1)S(1)}, u32[]{:S(2)}, u32[]{:S(2)}) collective-permute-start(bf16[128,1024]{1,0:T(8,128)(2,1)S(1)} %shard_map.147), channel_id=1, source_target_pairs={{2,0},{4,2},{6,4},{8,6},{10,8},{12,10},{14,12},{16,14},{18,16},{20... | collective-permute-start | bytes 786440 | tf_op jit(solution)/shard_map/ppermute | solution.py:364
  8.4 0.0 copy-done.11
  8.4 0.0 copy-done.14
  8.4 0.0 copy-done.15
  8.4 0.0 copy-done
  8.4 0.0 copy-start.10
  8.5 1.2 %copy-done.10 = bf16[1024,512]{1,0:T(8,128)(2,1)S(1)} copy-done((bf16[1024,512]{1,0:T(8,128)(2,1)S(1)}, bf16[1024,512]{1,0:T(8,128)(2,1)}, u32[]{:S(2)}) %copy-start.10) | copy-done | bytes 1048600
  9.7 3.0 %shard_map.146 = (f32[256,512]{1,0:T(8,128)S(1)}, f32[256,384]{1,0:T(8,128)S(1)}, f32[256,128]{1,0:T(8,128)S(1)}, f32[256,256]{1,0:T(8,128)S(1)}, bf16[256,512]{1,0:T(8,128)(2,1)S(1)}) custom-call(s32[32,256]{1,0:T(8,128)S(1)} %bitcast.5, s32[1,256]{1,0:T(1,128)S(1)} %bitcast.13, bf16[256,1024]{1,0:T(8,128)(2,1)S(1)} %copy-done, f32[1,1024]{1,0:T(1,128)S(1)} %bitcast.12, ...), custom_call_target="tpu_custom_call" | custom-call | flops 268435456 | bytes 3183616 | tf_op jit(solution)/shard_map/pallas_call | solution.py:31
  12.7 0.0 copy-start.13
  12.7 0.0 collective-permute-done.1.refs_0_
  12.8 0.1 collective-permute-start.4
  12.8 2.7 %collective-permute-start = (bf16[128,1024]{1,0:T(8,128)(2,1)S(1)}, bf16[128,1024]{1,0:T(8,128)(2,1)S(1)}, u32[]{:S(2)}, u32[]{:S(2)}) collective-permute-start(bf16[128,1024]{1,0:T(8,128)(2,1)S(1)} %get-tuple-element.29), channel_id=1, source_target_pairs={{1,0},{0,1},{3,2},{2,3},{5,4},{4,5},{7,6},{6,7},{9,8},{8,9},{11,10... | collective-permute-start | bytes 786440 | tf_op jit(solution)/shard_map/ppermute | solution.py:354
  15.5 0.0 copy-done.9
  15.5 0.0 copy-done.8
  15.5 0.0 copy-done.5
  15.5 0.0 copy-done.13
  15.5 3.7 %shard_map.148 = (f32[256,512]{1,0:T(8,128)S(1)}, f32[256,512]{1,0:T(8,128)S(1)}, f32[256,512]{1,0:T(8,128)S(1)}) custom-call(bf16[512,1024]{1,0:T(8,128)(2,1)S(1)} %copy-done.5, f32[256,512]{1,0:T(8,128)S(1)} %get-tuple-element.36.refs_1_, f32[1,1024]{1,0:T(1,128)S(1)} %bitcast.8, bf16[1024,512]{1,0:T(8,128)(2,1)S(1)} %copy-done.8, ...), custom_call_target="tpu_custom_call" | custom-call | flops 2147483648 | bytes 5509120 | tf_op jit(solution)/shard_map/pallas_call | solution.py:31
  19.2 0.0 collective-permute-done.3.refs_0_
  19.2 2.1 %collective-permute-done.4.refs_1_ = bf16[128,1024]{1,0:T(8,128)(2,1)S(1)} collective-permute-done((bf16[128,1024]{1,0:T(8,128)(2,1)S(1)}, bf16[128,1024]{1,0:T(8,128)(2,1)S(1)}, u32[]{:S(2)}, u32[]{:S(2)}) %collective-permute-start.4) | collective-permute-done | bytes 262176 | tf_op jit(solution)/shard_map/ppermute | solution.py:398
  21.3 2.0 %shard_map.149 = (f32[256,512]{1,0:T(8,128)S(1)}, f32[256,512]{1,0:T(8,128)S(1)}, f32[256,512]{1,0:T(8,128)S(1)}) custom-call(bf16[128,1024]{1,0:T(8,128)(2,1)S(1)} %collective-permute-done.3.refs_0_, bf16[128,1024]{1,0:T(8,128)(2,1)S(1)} %collective-permute-done.4.refs_1_, f32[256,256]{1,0:T(8,128)S(1)} %get-tuple-element.35.refs_2_, ...), custom_call_target="tpu_custom_call" | custom-call | flops 1073741824 | bytes 6295552 | tf_op jit(solution)/shard_map/pallas_call | solution.py:31
  23.3 0.0 collective-permute-done.2.refs_1_
  23.3 0.0 copy-start.6
  23.3 3.4 %shard_map.150 = (f32[256,512]{1,0:T(8,128)S(1)}, f32[256,512]{1,0:T(8,128)S(1)}, f32[256,512]{1,0:T(8,128)S(1)}) custom-call(bf16[128,1024]{1,0:T(8,128)(2,1)S(1)} %collective-permute-done.1.refs_0_, bf16[256,1024]{1,0:T(8,128)(2,1)S(1)} %collective-permute-done.2.refs_1_, f32[256,384]{1,0:T(8,128)S(1)} %get-tuple-element.33.refs_2_, ...), custom_call_target="tpu_custom_call" | custom-call | flops 1610612736 | bytes 6688768 | tf_op jit(solution)/shard_map/pallas_call | solution.py:31
  26.7 0.7 %collective-permute-done.refs_0_ = bf16[128,1024]{1,0:T(8,128)(2,1)S(1)} collective-permute-done((bf16[128,1024]{1,0:T(8,128)(2,1)S(1)}, bf16[128,1024]{1,0:T(8,128)(2,1)S(1)}, u32[]{:S(2)}, u32[]{:S(2)}) %collective-permute-start) | collective-permute-done | bytes 262176 | tf_op jit(solution)/shard_map/ppermute | solution.py:354
  27.5 0.0 copy-done.6
  27.5 1.3 %shard_map.151 = (bf16[128,1024]{1,0:T(8,128)(2,1)S(1)}, bf16[128,512]{1,0:T(8,128)(2,1)S(1)}, bf16[128,512]{1,0:T(8,128)(2,1)S(1)}) custom-call(bf16[128,1024]{1,0:T(8,128)(2,1)S(1)} %collective-permute-done.refs_0_, f32[256,128]{1,0:T(8,128)S(1)} %get-tuple-element.30.refs_1_.log, f32[1,1024]{1,0:T(1,128)S(1)} %bitcast.11, ...), custom_call_target="tpu_custom_call" | custom-call | flops 536870912 | bytes 5902336 | tf_op jit(solution)/shard_map/pallas_call | solution.py:31
  28.8 1.8 %collective-permute-start.5 = (bf16[128,1024]{1,0:T(8,128)(2,1)S(1)}, bf16[128,1024]{1,0:T(8,128)(2,1)S(1)}, u32[]{:S(2)}, u32[]{:S(2)}) collective-permute-start(bf16[128,1024]{1,0:T(8,128)(2,1)S(1)} %get-tuple-element.46.own), channel_id=1, source_target_pairs={{1,0},{0,1},{3,2},{2,3},{5,4},{4,5},{7,6},{6,7},{9,8},{8,9},{11,10... | collective-permute-start | bytes 786440 | tf_op jit(solution)/shard_map/ppermute | solution.py:354
  30.6 0.0 copy-start.1
  30.6 0.9 %shard_map.153.own = bf16[128,1024]{1,0:T(8,128)(2,1)S(1)} custom-call(f32[256,128]{1,0:T(8,128)S(1)} %get-tuple-element.30.refs_1_.log, bf16[256,512]{1,0:T(8,128)(2,1)S(1)} %get-tuple-element.31.refs_5_.refs_6_.query, bf16[128,512]{1,0:T(8,128)(2,1)S(1)} %get-tuple-element.49.keys, bf16[128,512]{1,0:T(8,128)(2,1)S(1)} %get-tuple-element.50.values, ...), custom_call_target="tpu_custom_call" | custom-call | flops 134217728 | bytes 3538944 | tf_op jit(solution)/shard_map/pallas_call | solution.py:31
  31.5 0.4 collective-permute-start.6
  31.8 6.3 %collective-permute-done.5.other = bf16[128,1024]{1,0:T(8,128)(2,1)S(1)} collective-permute-done((bf16[128,1024]{1,0:T(8,128)(2,1)S(1)}, bf16[128,1024]{1,0:T(8,128)(2,1)S(1)}, u32[]{:S(2)}, u32[]{:S(2)}) %collective-permute-start.5) | collective-permute-done | bytes 262176 | tf_op jit(solution)/shard_map/ppermute | solution.py:354
  38.1 0.0 copy-done.1
  38.1 0.0 copy-done.2
  38.1 0.0 copy-done.3
  38.1 0.0 copy-done.12
  38.1 0.8 %shard_map.152 = (bf16[128,512]{1,0:T(8,128)(2,1)S(1)}, bf16[128,1024]{1,0:T(8,128)(2,1)S(1)}) custom-call(bf16[256,1024]{1,0:T(8,128)(2,1)S(1)} %copy-done, bf16[128,1024]{1,0:T(8,128)(2,1)S(1)} %get-tuple-element.46.own, bf16[128,1024]{1,0:T(8,128)(2,1)S(1)} %collective-permute-done.5.other, f32[1,1024]{1,0:T(1,128)S(1)} %bitcast.6, ...), custom_call_target="tpu_custom_call" | custom-call | flops 402653184 | bytes 4591616 | tf_op jit(solution)/shard_map/pallas_call | solution.py:31
  38.9 0.0 copy-start.7
  39.0 0.4 collective-permute-start.9
  39.4 2.6 %collective-permute-done.6.other = bf16[128,1024]{1,0:T(8,128)(2,1)S(1)} collective-permute-done((bf16[128,1024]{1,0:T(8,128)(2,1)S(1)}, bf16[128,1024]{1,0:T(8,128)(2,1)S(1)}, u32[]{:S(2)}, u32[]{:S(2)}) %collective-permute-start.6) | collective-permute-done | bytes 262176 | tf_op jit(solution)/shard_map/ppermute | solution.py:354
  42.0 0.8 %shard_map.154 = (bf16[128,512]{1,0:T(8,128)(2,1)S(1)}, bf16[128,1024]{1,0:T(8,128)(2,1)S(1)}) custom-call(bf16[256,1024]{1,0:T(8,128)(2,1)S(1)} %copy-done, bf16[128,1024]{1,0:T(8,128)(2,1)S(1)} %shard_map.153.own, bf16[128,1024]{1,0:T(8,128)(2,1)S(1)} %collective-permute-done.6.other, f32[1,1024]{1,0:T(1,128)S(1)} %bitcast.7, ...), custom_call_target="tpu_custom_call" | custom-call | flops 402653184 | bytes 4591616 | tf_op jit(solution)/shard_map/pallas_call | solution.py:31
  42.8 0.1 collective-permute-start.7
  42.9 0.4 collective-permute-done.9.halo
  43.3 0.0 copy-done.7
  43.3 1.0 %shard_map.156.own_share = bf16[128,1024]{1,0:T(8,128)(2,1)S(1)} custom-call(bf16[128,512]{1,0:T(8,128)(2,1)S(1)} %get-tuple-element.52.query, bf16[128,1024]{1,0:T(8,128)(2,1)S(1)} %get-tuple-element.48.low, bf16[128,1024]{1,0:T(8,128)(2,1)S(1)} %get-tuple-element.51.high, bf16[128,1024]{1,0:T(8,128)(2,1)S(1)} %collective-permute-done.9.halo, ...), custom_call_target="tpu_custom_call" | custom-call | flops 134217728 | bytes 2228224 | tf_op jit(solution)/shard_map/pallas_call | solution.py:31
  44.3 1.6 %collective-permute-start.10 = (bf16[128,1024]{1,0:T(8,128)(2,1)S(1)}, bf16[128,1024]{1,0:T(8,128)(2,1)S(1)}, u32[]{:S(2)}, u32[]{:S(2)}) collective-permute-start(bf16[128,1024]{1,0:T(8,128)(2,1)S(1)} %shard_map.156.own_share), channel_id=1, source_target_pairs={{1,0},{0,1},{3,2},{2,3},{5,4},{4,5},{7,6},{6,7},{9,8},{8,9},{11,10... | collective-permute-start | bytes 786440 | tf_op jit(solution)/shard_map/ppermute | solution.py:354
  45.9 5.5 %collective-permute-done.7.halo = bf16[128,1024]{1,0:T(8,128)(2,1)S(1)} collective-permute-done((bf16[128,1024]{1,0:T(8,128)(2,1)S(1)}, bf16[128,1024]{1,0:T(8,128)(2,1)S(1)}, u32[]{:S(2)}, u32[]{:S(2)}) %collective-permute-start.7) | collective-permute-done | bytes 262176 | tf_op jit(solution)/shard_map/ppermute | solution.py:435
  51.3 1.0 %shard_map.155.own_share = bf16[128,1024]{1,0:T(8,128)(2,1)S(1)} custom-call(bf16[128,512]{1,0:T(8,128)(2,1)S(1)} %get-tuple-element.47.query, bf16[128,1024]{1,0:T(8,128)(2,1)S(1)} %get-tuple-element.48.low, bf16[128,1024]{1,0:T(8,128)(2,1)S(1)} %get-tuple-element.51.high, bf16[128,1024]{1,0:T(8,128)(2,1)S(1)} %collective-permute-done.7.halo, ...), custom_call_target="tpu_custom_call" | custom-call | flops 134217728 | bytes 2228224 | tf_op jit(solution)/shard_map/pallas_call | solution.py:31
  52.4 1.5 %collective-permute-start.8 = (bf16[128,1024]{1,0:T(8,128)(2,1)S(1)}, bf16[128,1024]{1,0:T(8,128)(2,1)S(1)}, u32[]{:S(2)}, u32[]{:S(2)}) collective-permute-start(bf16[128,1024]{1,0:T(8,128)(2,1)S(1)} %shard_map.155.own_share), channel_id=1, source_target_pairs={{1,0},{0,1},{3,2},{2,3},{5,4},{4,5},{7,6},{6,7},{9,8},{8,9},{11,10... | collective-permute-start | bytes 786440 | tf_op jit(solution)/shard_map/ppermute | solution.py:354
  53.9 0.0 collective-permute-done.10.other_share
  53.9 0.9 %shard_map.157.refs_0_ = bf16[256,1024]{1,0:T(8,128)(2,1)} custom-call(bf16[256,1024]{1,0:T(8,128)(2,1)S(1)} %copy-done, bf16[128,1024]{1,0:T(8,128)(2,1)S(1)} %shard_map.153.own, bf16[128,1024]{1,0:T(8,128)(2,1)S(1)} %collective-permute-done.6.other, bf16[128,1024]{1,0:T(8,128)(2,1)S(1)} %shard_map.156.own_share, ...), custom_call_target="tpu_custom_call" | custom-call | tf_op jit(solution)/shard_map/pallas_call | solution.py:311
  54.8 4.4 %collective-permute-done.8.other_share = bf16[128,1024]{1,0:T(8,128)(2,1)S(1)} collective-permute-done((bf16[128,1024]{1,0:T(8,128)(2,1)S(1)}, bf16[128,1024]{1,0:T(8,128)(2,1)S(1)}, u32[]{:S(2)}, u32[]{:S(2)}) %collective-permute-start.8) | collective-permute-done | bytes 262176 | tf_op jit(solution)/shard_map/ppermute | solution.py:354
  59.2 0.9 %shard_map.158 = bf16[256,1024]{1,0:T(8,128)(2,1)} custom-call(bf16[256,1024]{1,0:T(8,128)(2,1)S(1)} %copy-done, bf16[128,1024]{1,0:T(8,128)(2,1)S(1)} %get-tuple-element.46.own, bf16[128,1024]{1,0:T(8,128)(2,1)S(1)} %collective-permute-done.5.other, bf16[128,1024]{1,0:T(8,128)(2,1)S(1)} %shard_map.155.own_share, ...), custom_call_target="tpu_custom_call", output_to_operand_aliasing={{}: (5, {})} | custom-call | tf_op jit(solution)/shard_map/pallas_call | solution.py:311
  (4 shorter events, 0.0 us)
Async XLA Ops:
  0.0 1.2 %copy-start.4 = (bf16[512,1024]{1,0:T(8,128)(2,1)S(1)}, bf16[512,1024]{1,0:T(8,128)(2,1)}, u32[]{:S(2)}) copy-start(bf16[512,1024]{1,0:T(8,128)(2,1)} %refs_0_.5) | copy-start | bytes 3145732
  1.2 7.2 %copy-start.11 = (s32[256,32]{0,1:T(8,128)S(1)}, s32[256,32]{0,1:T(8,128)}, u32[]{:S(2)}) copy-start(s32[256,32]{0,1:T(8,128)} %param.23) | copy-start | bytes 98308
  1.2 7.2 %copy-start.14 = (f32[1024]{0:T(1024)S(1)}, f32[1024]{0:T(1024)}, u32[]{:S(2)}) copy-start(f32[1024]{0:T(1024)} %param.18) | copy-start | bytes 12292
  1.2 7.2 %copy-start.15 = (s32[256]{0:T(256)S(1)}, s32[256]{0:T(256)}, u32[]{:S(2)}) copy-start(s32[256]{0:T(256)} %param.24) | copy-start | bytes 3076
  1.2 14.2 %copy-start.9 = (bf16[1024,512]{1,0:T(8,128)(2,1)S(1)}, bf16[1024,512]{1,0:T(8,128)(2,1)}, u32[]{:S(2)}) copy-start(bf16[1024,512]{1,0:T(8,128)(2,1)} %refs_4_.7) | copy-start | bytes 3145732
  1.3 7.2 %copy-start = (bf16[256,1024]{1,0:T(8,128)(2,1)S(1)}, bf16[256,1024]{1,0:T(8,128)(2,1)}, u32[]{:S(2)}) copy-start(bf16[256,1024]{1,0:T(8,128)(2,1)} %hidden.9) | copy-start | bytes 1572868
  1.3 11.4 %collective-permute-start.1 = (bf16[128,1024]{1,0:T(8,128)(2,1)S(1)}, bf16[128,1024]{1,0:T(8,128)(2,1)S(1)}, u32[]{:S(2)}, u32[]{:S(2)}) collective-permute-start(bf16[128,1024]{1,0:T(8,128)(2,1)S(1)} %shard_map.147), channel_id=1, source_target_pairs={{1,0},{0,1},{3,2},{2,3},{5,4},{4,5},{7,6},{6,7},{9,8},{8,9},{11,10... | collective-permute-start | bytes 786440 | tf_op jit(solution)/shard_map/ppermute | solution.py:354
  4.3 11.2 %copy-start.8 = (bf16[1024,512]{1,0:T(8,128)(2,1)S(1)}, bf16[1024,512]{1,0:T(8,128)(2,1)}, u32[]{:S(2)}) copy-start(bf16[1024,512]{1,0:T(8,128)(2,1)} %refs_3_.3) | copy-start | bytes 3145732
  4.4 11.1 %copy-start.5 = (bf16[512,1024]{1,0:T(8,128)(2,1)S(1)}, bf16[512,1024]{1,0:T(8,128)(2,1)}, u32[]{:S(2)}) copy-start(bf16[512,1024]{1,0:T(8,128)(2,1)} %refs_0_.5) | copy-start | bytes 3145732
  4.4 18.9 %collective-permute-start.2 = (bf16[256,1024]{1,0:T(8,128)(2,1)S(1)}, bf16[256,1024]{1,0:T(8,128)(2,1)S(1)}, u32[]{:S(2)}, u32[]{:S(2)}) collective-permute-start(bf16[256,1024]{1,0:T(8,128)(2,1)S(1)} %get-tuple-element.32), channel_id=1, source_target_pairs={{1,0},{0,1},{3,2},{2,3},{5,4},{4,5},{7,6},{6,7},{9,8},{8,9},{11,10... | collective-permute-start | bytes 1572872 | tf_op jit(solution)/shard_map/ppermute | solution.py:354
  4.5 14.7 %collective-permute-start.3 = (bf16[128,1024]{1,0:T(8,128)(2,1)S(1)}, bf16[128,1024]{1,0:T(8,128)(2,1)S(1)}, u32[]{:S(2)}, u32[]{:S(2)}) collective-permute-start(bf16[128,1024]{1,0:T(8,128)(2,1)S(1)} %shard_map.147), channel_id=1, source_target_pairs={{2,0},{4,2},{6,4},{8,6},{10,8},{12,10},{14,12},{16,14},{18,16},{20... | collective-permute-start | bytes 786440 | tf_op jit(solution)/shard_map/ppermute | solution.py:364
  8.4 1.2 %copy-start.10 = (bf16[1024,512]{1,0:T(8,128)(2,1)S(1)}, bf16[1024,512]{1,0:T(8,128)(2,1)}, u32[]{:S(2)}) copy-start(bf16[1024,512]{1,0:T(8,128)(2,1)} %wq.3) | copy-start | bytes 3145732
  12.7 2.8 %copy-start.13 = (f32[1024]{0:T(1024)S(1)}, f32[1024]{0:T(1024)}, u32[]{:S(2)}) copy-start(f32[1024]{0:T(1024)} %param.16) | copy-start | bytes 12292
  12.8 8.5 %collective-permute-start.4 = (bf16[128,1024]{1,0:T(8,128)(2,1)S(1)}, bf16[128,1024]{1,0:T(8,128)(2,1)S(1)}, u32[]{:S(2)}, u32[]{:S(2)}) collective-permute-start(bf16[128,1024]{1,0:T(8,128)(2,1)S(1)} %collective-permute-done.1.refs_0_), channel_id=1, source_target_pairs={{0,2},{2,4},{4,6},{6,8},{8,10},{10,12},{12,14},{14,16},{16,18},{18... | collective-permute-start | bytes 786440 | tf_op jit(solution)/shard_map/ppermute | solution.py:398
  12.8 14.6 %collective-permute-start = (bf16[128,1024]{1,0:T(8,128)(2,1)S(1)}, bf16[128,1024]{1,0:T(8,128)(2,1)S(1)}, u32[]{:S(2)}, u32[]{:S(2)}) collective-permute-start(bf16[128,1024]{1,0:T(8,128)(2,1)S(1)} %get-tuple-element.29), channel_id=1, source_target_pairs={{1,0},{0,1},{3,2},{2,3},{5,4},{4,5},{7,6},{6,7},{9,8},{8,9},{11,10... | collective-permute-start | bytes 786440 | tf_op jit(solution)/shard_map/ppermute | solution.py:354
  23.3 4.2 %copy-start.6 = (bf16[512,1024]{1,0:T(8,128)(2,1)S(1)}, bf16[512,1024]{1,0:T(8,128)(2,1)}, u32[]{:S(2)}) copy-start(bf16[512,1024]{1,0:T(8,128)(2,1)} %wo.3) | copy-start | bytes 3145732
  28.8 9.3 %collective-permute-start.5 = (bf16[128,1024]{1,0:T(8,128)(2,1)S(1)}, bf16[128,1024]{1,0:T(8,128)(2,1)S(1)}, u32[]{:S(2)}, u32[]{:S(2)}) collective-permute-start(bf16[128,1024]{1,0:T(8,128)(2,1)S(1)} %get-tuple-element.46.own), channel_id=1, source_target_pairs={{1,0},{0,1},{3,2},{2,3},{5,4},{4,5},{7,6},{6,7},{9,8},{8,9},{11,10... | collective-permute-start | bytes 786440 | tf_op jit(solution)/shard_map/ppermute | solution.py:354
  30.6 7.5 %copy-start.1 = (bf16[1024,512]{1,0:T(8,128)(2,1)S(1)}, bf16[1024,512]{1,0:T(8,128)(2,1)}, u32[]{:S(2)}) copy-start(bf16[1024,512]{1,0:T(8,128)(2,1)} %wq.5) | copy-start | bytes 3145732
  30.6 7.5 %copy-start.2 = (bf16[1024,512]{1,0:T(8,128)(2,1)S(1)}, bf16[1024,512]{1,0:T(8,128)(2,1)}, u32[]{:S(2)}) copy-start(bf16[1024,512]{1,0:T(8,128)(2,1)} %wk.3) | copy-start | bytes 3145732
  30.6 7.5 %copy-start.3 = (bf16[1024,512]{1,0:T(8,128)(2,1)S(1)}, bf16[1024,512]{1,0:T(8,128)(2,1)}, u32[]{:S(2)}) copy-start(bf16[1024,512]{1,0:T(8,128)(2,1)} %wv.3) | copy-start | bytes 3145732
  30.6 7.5 %copy-start.12 = (f32[1024]{0:T(1024)S(1)}, f32[1024]{0:T(1024)}, u32[]{:S(2)}) copy-start(f32[1024]{0:T(1024)} %param.25) | copy-start | bytes 12292
  31.5 10.5 %collective-permute-start.6 = (bf16[128,1024]{1,0:T(8,128)(2,1)S(1)}, bf16[128,1024]{1,0:T(8,128)(2,1)S(1)}, u32[]{:S(2)}, u32[]{:S(2)}) collective-permute-start(bf16[128,1024]{1,0:T(8,128)(2,1)S(1)} %shard_map.153.own), channel_id=1, source_target_pairs={{1,0},{0,1},{3,2},{2,3},{5,4},{4,5},{7,6},{6,7},{9,8},{8,9},{11,10... | collective-permute-start | bytes 786440 | tf_op jit(solution)/shard_map/ppermute | solution.py:354
  38.9 4.3 %copy-start.7 = (bf16[512,1024]{1,0:T(8,128)(2,1)S(1)}, bf16[512,1024]{1,0:T(8,128)(2,1)}, u32[]{:S(2)}) copy-start(bf16[512,1024]{1,0:T(8,128)(2,1)} %wo.5) | copy-start | bytes 3145732
  39.0 4.3 %collective-permute-start.9 = (bf16[128,1024]{1,0:T(8,128)(2,1)S(1)}, bf16[128,1024]{1,0:T(8,128)(2,1)S(1)}, u32[]{:S(2)}, u32[]{:S(2)}) collective-permute-start(bf16[128,1024]{1,0:T(8,128)(2,1)S(1)} %get-tuple-element.48.low), channel_id=1, source_target_pairs={{2,0},{4,2},{6,4},{8,6},{10,8},{12,10},{14,12},{16,14},{18,16},{20... | collective-permute-start | bytes 786440 | tf_op jit(solution)/shard_map/ppermute | solution.py:434
  42.8 8.5 %collective-permute-start.7 = (bf16[128,1024]{1,0:T(8,128)(2,1)S(1)}, bf16[128,1024]{1,0:T(8,128)(2,1)S(1)}, u32[]{:S(2)}, u32[]{:S(2)}) collective-permute-start(bf16[128,1024]{1,0:T(8,128)(2,1)S(1)} %get-tuple-element.51.high), channel_id=1, source_target_pairs={{0,2},{2,4},{4,6},{6,8},{8,10},{10,12},{12,14},{14,16},{16,18},{18... | collective-permute-start | bytes 786440 | tf_op jit(solution)/shard_map/ppermute | solution.py:435
  44.3 9.5 %collective-permute-start.10 = (bf16[128,1024]{1,0:T(8,128)(2,1)S(1)}, bf16[128,1024]{1,0:T(8,128)(2,1)S(1)}, u32[]{:S(2)}, u32[]{:S(2)}) collective-permute-start(bf16[128,1024]{1,0:T(8,128)(2,1)S(1)} %shard_map.156.own_share), channel_id=1, source_target_pairs={{1,0},{0,1},{3,2},{2,3},{5,4},{4,5},{7,6},{6,7},{9,8},{8,9},{11,10... | collective-permute-start | bytes 786440 | tf_op jit(solution)/shard_map/ppermute | solution.py:354
  52.4 6.8 %collective-permute-start.8 = (bf16[128,1024]{1,0:T(8,128)(2,1)S(1)}, bf16[128,1024]{1,0:T(8,128)(2,1)S(1)}, u32[]{:S(2)}, u32[]{:S(2)}) collective-permute-start(bf16[128,1024]{1,0:T(8,128)(2,1)S(1)} %shard_map.155.own_share), channel_id=1, source_target_pairs={{1,0},{0,1},{3,2},{2,3},{5,4},{4,5},{7,6},{6,7},{9,8},{8,9},{11,10... | collective-permute-start | bytes 786440 | tf_op jit(solution)/shard_map/ppermute | solution.py:354

commit v4 on v3

--- a/solution.py
+++ b/solution.py
@@ -15,6 +15,7 @@
 
 EPSILON = 1e-05
 NEG = -1e30
+PARTS = 2
 VMEM_LIMIT = 24 * 1024 * 1024
 
 f32 = jnp.float32
@@ -291,17 +292,27 @@
     share[...] = dot(heads[...], wo[...]).astype(bf16)
 
 
-def mixed_kernel(at, hidden, own, other, own_share, other_share, *refs):
+def base_kernel(at, hidden, own, other, share, base):
+    base[...] = latent_of(at, hidden, own, other) + share[...].astype(f32)
+
+
+def mixed_kernel(at, base, share, *refs):
     result, half, sem = refs[-3:]
-    total = own_share[...].astype(f32) + other_share[...].astype(f32)
-    half[...] = (latent_of(at, hidden, own, other) + total).astype(bf16)
-    copy = pltpu.make_async_copy(half, result.at[pl.ds(at, own.shape[0]), :], sem)
-    copy.start()
-    copy.wait()
-
-
-def mix_half(at, hidden, own, other, own_share, other_share, mixed):
-    args = [hidden, own, other, own_share, other_share]
+    rows = base.shape[0] // PARTS
+    copies = []
+    for i in range(PARTS):
+        part = pl.ds(i * rows, rows)
+        half[part, :] = (base[part, :] + share[part, :].astype(f32)).astype(bf16)
+        copies.append(
+            pltpu.make_async_copy(half.at[part], result.at[pl.ds(at + i * rows, rows), :], sem.at[i])
+        )
+        copies[-1].start()
+    for copy in copies:
+        copy.wait()
+
+
+def mix_half(at, base, share, mixed):
+    args = [base, share]
     specs = [whole(a.shape) for a in args]
     aliases = {}
     if not isinstance(mixed, jax.ShapeDtypeStruct):
@@ -313,7 +324,7 @@
         out_shape=shape_of(*mixed.shape, dtype=mixed.dtype),
         in_specs=specs,
         out_specs=pl.BlockSpec(memory_space=pltpu.HBM),
-        scratch_shapes=[pltpu.VMEM(own.shape, mixed.dtype), pltpu.SemaphoreType.DMA],
+        scratch_shapes=[pltpu.VMEM(base.shape, mixed.dtype), pltpu.SemaphoreType.DMA((2,))],
         input_output_aliases=aliases,
         compiler_params=pltpu.CompilerParams(vmem_limit_bytes=VMEM_LIMIT),
     )(*args)
@@ -356,7 +367,7 @@
     if peers == 2:
         me = lambda: lax.axis_index("mp")
         cut = min(rows - rim, max(LANES, (rows - rim) // 3 * 2 // LANES * LANES))
-        (ends,) = pick([grid_latent], [(0, lambda: me() * (rows - rim), rim)])
+        ends = lax.dynamic_slice_in_dim(grid_latent, lax.axis_index("mp") * (rows - rim), rim, 0)
         edge = shifted(ends, 1)
         up, down = up + [(bands - 1, 0)], down + [(0, bands - 1)]
         outward = [(2 * a, 2 * b) for a, b in down] + [(2 * a + 1, 2 * b + 1) for a, b in up]
@@ -447,7 +458,12 @@
         other_shares[i] = exchange(shares[i])
     mixed = shape_of(*hidden_in.shape, dtype=bf16)
     for i in (1, 0):
-        mixed = mix_half(i * half, hidden_in, own[i], other[i], shares[i], other_shares[i], mixed)
+        (base,) = call(
+            functools.partial(base_kernel, i * half),
+            [shape_of(*shares[i].shape, dtype=f32)],
+            [hidden_in, own[i], other[i], shares[i]],
+        )
+        mixed = mix_half(i * half, base, other_shares[i], mixed)
     return mixed
 
 

time: 60.3 us -> 60 us (level)
  local copies, waits for them, and re-layouts: 2.51 us -> 4.7 us
  waiting for transfers between devices: 22 us -> 20.2 us
  starting transfers between devices: 15.5 us -> 14.8 us
    unnamed x32, local copies, waits for them, and re-layouts: 2.51 us -> 3.73 us
    ppermute x1, waiting for transfers between devices: 2.09 us -> 1.04 us  [shards(): far_rim = lax.ppermute(after(edge, query), ('band', 'mp'), inward)]
    dynamic_slice x0 -> x1, local copies, waits for them, and re-layouts: none -> 0.98 us  [shards(): lax.dynamic_slice_in_dim(grid_latent, lax.axis_index('mp') * (rows - rim)...]
    ppermute x7, waiting for transfers between devices: 14 us -> 13.2 us  [shifted(): lax.ppermute(value, 'mp', [((i + by) % peers, i) for i in range(peers)])]
    pallas_call x10 -> x12, Pallas kernels: 18 us -> 18.2 us  [call(): pl.pallas_call(kernel, out_shape=outs, in_specs=[whole(a.shape) for a in...]
  transfers between devices with their start and end apart: 11 -> 11, of which waited for: 7 -> 6; matrix products, arithmetic and copies ran while one was open for 0% -> 0% of each run, Pallas kernels for 29% -> 30%
where the time goes in v4:
time: 60 us; the launch traced here: 59.8 us
  waiting for transfers between devices  20.2 us (34%)
  Pallas kernels  19.8 us (33%)
  starting transfers between devices  14.8 us (25%)
  local copies, waits for them, and re-layouts  4.7 us (8%)
    pallas_call x12, Pallas kernels, call(): pl.pallas_call(kernel, out_shape=outs, in_specs=[whole(a.shape) for a in...  18.2 us
    ppermute x7, waiting for transfers between devices, shifted(): lax.ppermute(value, 'mp', [((i + by) % peers, i) for i in range(peers)])  13.2 us
    ppermute x7, starting transfers between devices, shifted(): lax.ppermute(value, 'mp', [((i + by) % peers, i) for i in range(peers)])  10.7 us
    ppermute x1, waiting for transfers between devices, shards(): before = lax.ppermute(pairs[1], 'band', up)  5.47 us
    ppermute x1, starting transfers between devices, shards(): near_rim = lax.ppermute(ends, ('band', 'mp'), outward)  3.9 us
    unnamed x32, local copies, waits for them, and re-layouts  3.73 us
    pallas_call x2, Pallas kernels, mix_half(): pl.pallas_call(functools.partial(mixed_kernel, at), out_shape=shape_of(*m...  1.48 us
  transfers between devices with their start and end apart: 11, of which 6 were waited for; matrix products, arithmetic and copies ran while one was open for 0% of the time, Pallas kernels for 30%

profile of v4, /device:TPU:0, one launch (start us, length us, event | category | flops | bytes accessed | tf_op | source)
XLA Modules:
  0.0 59.8 jit_solution(5865320923914809792)
XLA Ops:
  0.0 0.0 copy-start.11
  0.0 0.0 copy-start.15
  0.0 1.0 %constant_dynamic-slice_fusion = bf16[128,1024]{1,0:T(8,128)(2,1)S(1)} fusion(bf16[512,1024]{1,0:T(8,128)(2,1)} %refs_0_.3, s32[]{:T(128)S(6)} %select_n.3), kind=kLoop, calls=%fused_computation | loop fusion | bytes 524292 | tf_op jit(solution)/shard_map/dynamic_slice | solution.py:370
  1.0 0.0 copy-start
  1.0 3.0 %collective-permute-start.1 = (bf16[128,1024]{1,0:T(8,128)(2,1)S(1)}, bf16[128,1024]{1,0:T(8,128)(2,1)S(1)}, u32[]{:S(2)}, u32[]{:S(2)}) collective-permute-start(bf16[128,1024]{1,0:T(8,128)(2,1)S(1)} %constant_dynamic-slice_fusion), channel_id=1, source_target_pairs={{1,0},{0,1},{3,2},{2,3},{5,4},{4,5},{7,6},{6,7},{9,8},{8,9},{11,10... | collective-permute-start | bytes 786440 | tf_op jit(solution)/shard_map/ppermute | solution.py:365
  4.0 0.0 copy-start.8
  4.0 1.2 %copy-done.8 = bf16[512,1024]{1,0:T(8,128)(2,1)S(1)} copy-done((bf16[512,1024]{1,0:T(8,128)(2,1)S(1)}, bf16[512,1024]{1,0:T(8,128)(2,1)}, u32[]{:S(2)}) %copy-start.8) | copy-done | bytes 1048600
  5.3 0.0 copy-start.7
  5.3 0.1 shard_map.145
  5.3 0.0 copy-start.6
  5.4 0.1 collective-permute-start.2
  5.5 3.9 %collective-permute-start.3 = (bf16[128,1024]{1,0:T(8,128)(2,1)S(1)}, bf16[128,1024]{1,0:T(8,128)(2,1)S(1)}, u32[]{:S(2)}, u32[]{:S(2)}) collective-permute-start(bf16[128,1024]{1,0:T(8,128)(2,1)S(1)} %constant_dynamic-slice_fusion), channel_id=1, source_target_pairs={{2,0},{4,2},{6,4},{8,6},{10,8},{12,10},{14,12},{16,14},{18,16},{20... | collective-permute-start | bytes 786440 | tf_op jit(solution)/shard_map/ppermute | solution.py:375
  9.4 0.0 copy-done.11
  9.4 0.0 copy-done.14
  9.4 0.0 copy-done.15
  9.4 0.0 copy-done
  9.4 0.0 copy-start.10
  9.4 1.2 %copy-done.10 = bf16[1024,512]{1,0:T(8,128)(2,1)S(1)} copy-done((bf16[1024,512]{1,0:T(8,128)(2,1)S(1)}, bf16[1024,512]{1,0:T(8,128)(2,1)}, u32[]{:S(2)}) %copy-start.10) | copy-done | bytes 1048600
  10.6 3.0 %shard_map.146 = (f32[256,512]{1,0:T(8,128)S(1)}, f32[256,384]{1,0:T(8,128)S(1)}, f32[256,128]{1,0:T(8,128)S(1)}, f32[256,256]{1,0:T(8,128)S(1)}, bf16[256,512]{1,0:T(8,128)(2,1)S(1)}) custom-call(s32[32,256]{1,0:T(8,128)S(1)} %bitcast.5, s32[1,256]{1,0:T(1,128)S(1)} %bitcast.13, bf16[256,1024]{1,0:T(8,128)(2,1)S(1)} %copy-done, f32[1,1024]{1,0:T(1,128)S(1)} %bitcast.12, ...), custom_call_target="tpu_custom_call" | custom-call | flops 268435456 | bytes 3183616 | tf_op jit(solution)/shard_map/pallas_call | solution.py:32
  13.7 0.0 copy-start.13
  13.7 0.0 collective-permute-done.1.refs_0_
  13.7 0.1 collective-permute-start.4
  13.8 2.5 %collective-permute-start = (bf16[128,1024]{1,0:T(8,128)(2,1)S(1)}, bf16[128,1024]{1,0:T(8,128)(2,1)S(1)}, u32[]{:S(2)}, u32[]{:S(2)}) collective-permute-start(bf16[128,1024]{1,0:T(8,128)(2,1)S(1)} %get-tuple-element.29), channel_id=1, source_target_pairs={{1,0},{0,1},{3,2},{2,3},{5,4},{4,5},{7,6},{6,7},{9,8},{8,9},{11,10... | collective-permute-start | bytes 786440 | tf_op jit(solution)/shard_map/ppermute | solution.py:365
  16.3 0.0 copy-done.7
  16.3 0.0 copy-done.6
  16.3 0.0 copy-done.13
  16.3 1.2 %copy-done.9 = bf16[512,1024]{1,0:T(8,128)(2,1)S(1)} copy-done((bf16[512,1024]{1,0:T(8,128)(2,1)S(1)}, bf16[512,1024]{1,0:T(8,128)(2,1)}, u32[]{:S(2)}) %copy-start.9) | copy-done | bytes 1048600
  17.5 3.7 %shard_map.147 = (f32[256,512]{1,0:T(8,128)S(1)}, f32[256,512]{1,0:T(8,128)S(1)}, f32[256,512]{1,0:T(8,128)S(1)}) custom-call(bf16[512,1024]{1,0:T(8,128)(2,1)S(1)} %copy-done.9, f32[256,512]{1,0:T(8,128)S(1)} %get-tuple-element.36.refs_1_, f32[1,1024]{1,0:T(1,128)S(1)} %bitcast.8, bf16[1024,512]{1,0:T(8,128)(2,1)S(1)} %copy-done.6, ...), custom_call_target="tpu_custom_call" | custom-call | flops 2147483648 | bytes 5509120 | tf_op jit(solution)/shard_map/pallas_call | solution.py:32
  21.2 0.0 collective-permute-done.3.refs_0_
  21.2 1.0 %collective-permute-done.4.refs_1_ = bf16[128,1024]{1,0:T(8,128)(2,1)S(1)} collective-permute-done((bf16[128,1024]{1,0:T(8,128)(2,1)S(1)}, bf16[128,1024]{1,0:T(8,128)(2,1)S(1)}, u32[]{:S(2)}, u32[]{:S(2)}) %collective-permute-start.4) | collective-permute-done | bytes 262176 | tf_op jit(solution)/shard_map/ppermute | solution.py:409
  22.3 2.0 %shard_map.148 = (f32[256,512]{1,0:T(8,128)S(1)}, f32[256,512]{1,0:T(8,128)S(1)}, f32[256,512]{1,0:T(8,128)S(1)}) custom-call(bf16[128,1024]{1,0:T(8,128)(2,1)S(1)} %collective-permute-done.3.refs_0_, bf16[128,1024]{1,0:T(8,128)(2,1)S(1)} %collective-permute-done.4.refs_1_, f32[256,256]{1,0:T(8,128)S(1)} %get-tuple-element.35.refs_2_, ...), custom_call_target="tpu_custom_call" | custom-call | flops 1073741824 | bytes 6295552 | tf_op jit(solution)/shard_map/pallas_call | solution.py:32
  24.2 0.0 collective-permute-done.2.refs_1_
  24.3 0.0 copy-start.4
  24.3 3.4 %shard_map.149 = (f32[256,512]{1,0:T(8,128)S(1)}, f32[256,512]{1,0:T(8,128)S(1)}, f32[256,512]{1,0:T(8,128)S(1)}) custom-call(bf16[128,1024]{1,0:T(8,128)(2,1)S(1)} %collective-permute-done.1.refs_0_, bf16[256,1024]{1,0:T(8,128)(2,1)S(1)} %collective-permute-done.2.refs_1_, f32[256,384]{1,0:T(8,128)S(1)} %get-tuple-element.33.refs_2_, ...), custom_call_target="tpu_custom_call" | custom-call | flops 1610612736 | bytes 6688768 | tf_op jit(solution)/shard_map/pallas_call | solution.py:32
  27.7 0.0 collective-permute-done.refs_0_
  27.7 0.0 copy-done.4
  27.7 1.3 %shard_map.150 = (bf16[128,1024]{1,0:T(8,128)(2,1)S(1)}, bf16[128,512]{1,0:T(8,128)(2,1)S(1)}, bf16[128,512]{1,0:T(8,128)(2,1)S(1)}) custom-call(bf16[128,1024]{1,0:T(8,128)(2,1)S(1)} %collective-permute-done.refs_0_, f32[256,128]{1,0:T(8,128)S(1)} %get-tuple-element.30.refs_1_.log, f32[1,1024]{1,0:T(1,128)S(1)} %bitcast.11, ...), custom_call_target="tpu_custom_call" | custom-call | flops 536870912 | bytes 5902336 | tf_op jit(solution)/shard_map/pallas_call | solution.py:32
  29.0 1.3 %collective-permute-start.5 = (bf16[128,1024]{1,0:T(8,128)(2,1)S(1)}, bf16[128,1024]{1,0:T(8,128)(2,1)S(1)}, u32[]{:S(2)}, u32[]{:S(2)}) collective-permute-start(bf16[128,1024]{1,0:T(8,128)(2,1)S(1)} %get-tuple-element.46.own), channel_id=1, source_target_pairs={{1,0},{0,1},{3,2},{2,3},{5,4},{4,5},{7,6},{6,7},{9,8},{8,9},{11,10... | collective-permute-start | bytes 786440 | tf_op jit(solution)/shard_map/ppermute | solution.py:365
  30.4 0.9 %shard_map.152.own = bf16[128,1024]{1,0:T(8,128)(2,1)S(1)} custom-call(f32[256,128]{1,0:T(8,128)S(1)} %get-tuple-element.30.refs_1_.log, bf16[256,512]{1,0:T(8,128)(2,1)S(1)} %get-tuple-element.31.refs_5_.refs_6_.query, bf16[128,512]{1,0:T(8,128)(2,1)S(1)} %get-tuple-element.49.keys, bf16[128,512]{1,0:T(8,128)(2,1)S(1)} %get-tuple-element.50.values, ...), custom_call_target="tpu_custom_call" | custom-call | flops 134217728 | bytes 3538944 | tf_op jit(solution)/shard_map/pallas_call | solution.py:32
  31.2 0.8 %collective-permute-start.6 = (bf16[128,1024]{1,0:T(8,128)(2,1)S(1)}, bf16[128,1024]{1,0:T(8,128)(2,1)S(1)}, u32[]{:S(2)}, u32[]{:S(2)}) collective-permute-start(bf16[128,1024]{1,0:T(8,128)(2,1)S(1)} %shard_map.152.own), channel_id=1, source_target_pairs={{1,0},{0,1},{3,2},{2,3},{5,4},{4,5},{7,6},{6,7},{9,8},{8,9},{11,10... | collective-permute-start | bytes 786440 | tf_op jit(solution)/shard_map/ppermute | solution.py:365
  32.1 6.3 %collective-permute-done.5.other = bf16[128,1024]{1,0:T(8,128)(2,1)S(1)} collective-permute-done((bf16[128,1024]{1,0:T(8,128)(2,1)S(1)}, bf16[128,1024]{1,0:T(8,128)(2,1)S(1)}, u32[]{:S(2)}, u32[]{:S(2)}) %collective-permute-start.5) | collective-permute-done | bytes 262176 | tf_op jit(solution)/shard_map/ppermute | solution.py:365
  38.3 0.0 copy-done.1
  38.3 0.0 copy-done.2
  38.3 0.0 copy-done.3
  38.3 0.0 copy-done.12
  38.4 0.8 %shard_map.151 = (bf16[128,512]{1,0:T(8,128)(2,1)S(1)}, bf16[128,1024]{1,0:T(8,128)(2,1)S(1)}) custom-call(bf16[256,1024]{1,0:T(8,128)(2,1)S(1)} %copy-done, bf16[128,1024]{1,0:T(8,128)(2,1)S(1)} %get-tuple-element.46.own, bf16[128,1024]{1,0:T(8,128)(2,1)S(1)} %collective-permute-done.5.other, f32[1,1024]{1,0:T(1,128)S(1)} %bitcast.6, ...), custom_call_target="tpu_custom_call" | custom-call | flops 402653184 | bytes 4591616 | tf_op jit(solution)/shard_map/pallas_call | solution.py:32
  39.2 0.0 copy-start.5
  39.2 0.1 collective-permute-start.9
  39.2 2.5 %collective-permute-done.6.other = bf16[128,1024]{1,0:T(8,128)(2,1)S(1)} collective-permute-done((bf16[128,1024]{1,0:T(8,128)(2,1)S(1)}, bf16[128,1024]{1,0:T(8,128)(2,1)S(1)}, u32[]{:S(2)}, u32[]{:S(2)}) %collective-permute-start.6) | collective-permute-done | bytes 262176 | tf_op jit(solution)/shard_map/ppermute | solution.py:365
  41.7 0.8 %shard_map.153 = (bf16[128,512]{1,0:T(8,128)(2,1)S(1)}, bf16[128,1024]{1,0:T(8,128)(2,1)S(1)}) custom-call(bf16[256,1024]{1,0:T(8,128)(2,1)S(1)} %copy-done, bf16[128,1024]{1,0:T(8,128)(2,1)S(1)} %shard_map.152.own, bf16[128,1024]{1,0:T(8,128)(2,1)S(1)} %collective-permute-done.6.other, f32[1,1024]{1,0:T(1,128)S(1)} %bitcast.7, ...), custom_call_target="tpu_custom_call" | custom-call | flops 402653184 | bytes 4591616 | tf_op jit(solution)/shard_map/pallas_call | solution.py:32
  42.5 0.1 collective-permute-start.7
  42.6 0.5 collective-permute-done.9.halo
  43.1 0.0 copy-done.5
  43.1 1.0 %shard_map.156.share = bf16[128,1024]{1,0:T(8,128)(2,1)S(1)} custom-call(bf16[128,512]{1,0:T(8,128)(2,1)S(1)} %get-tuple-element.52.query, bf16[128,1024]{1,0:T(8,128)(2,1)S(1)} %get-tuple-element.48.low, bf16[128,1024]{1,0:T(8,128)(2,1)S(1)} %get-tuple-element.51.high, bf16[128,1024]{1,0:T(8,128)(2,1)S(1)} %collective-permute-done.9.halo, ...), custom_call_target="tpu_custom_call" | custom-call | flops 134217728 | bytes 2228224 | tf_op jit(solution)/shard_map/pallas_call | solution.py:32
  44.2 1.4 %collective-permute-start.10 = (bf16[128,1024]{1,0:T(8,128)(2,1)S(1)}, bf16[128,1024]{1,0:T(8,128)(2,1)S(1)}, u32[]{:S(2)}, u32[]{:S(2)}) collective-permute-start(bf16[128,1024]{1,0:T(8,128)(2,1)S(1)} %shard_map.156.share), channel_id=1, source_target_pairs={{1,0},{0,1},{3,2},{2,3},{5,4},{4,5},{7,6},{6,7},{9,8},{8,9},{11,10... | collective-permute-start | bytes 786440 | tf_op jit(solution)/shard_map/ppermute | solution.py:365
  45.6 5.5 %collective-permute-done.7.halo = bf16[128,1024]{1,0:T(8,128)(2,1)S(1)} collective-permute-done((bf16[128,1024]{1,0:T(8,128)(2,1)S(1)}, bf16[128,1024]{1,0:T(8,128)(2,1)S(1)}, u32[]{:S(2)}, u32[]{:S(2)}) %collective-permute-start.7) | collective-permute-done | bytes 262176 | tf_op jit(solution)/shard_map/ppermute | solution.py:446
  51.1 1.0 %shard_map.154.share = bf16[128,1024]{1,0:T(8,128)(2,1)S(1)} custom-call(bf16[128,512]{1,0:T(8,128)(2,1)S(1)} %get-tuple-element.47.query, bf16[128,1024]{1,0:T(8,128)(2,1)S(1)} %get-tuple-element.48.low, bf16[128,1024]{1,0:T(8,128)(2,1)S(1)} %get-tuple-element.51.high, bf16[128,1024]{1,0:T(8,128)(2,1)S(1)} %collective-permute-done.7.halo, ...), custom_call_target="tpu_custom_call" | custom-call | flops 134217728 | bytes 2228224 | tf_op jit(solution)/shard_map/pallas_call | solution.py:32
  52.1 1.5 %collective-permute-start.8 = (bf16[128,1024]{1,0:T(8,128)(2,1)S(1)}, bf16[128,1024]{1,0:T(8,128)(2,1)S(1)}, u32[]{:S(2)}, u32[]{:S(2)}) collective-permute-start(bf16[128,1024]{1,0:T(8,128)(2,1)S(1)} %shard_map.154.share), channel_id=1, source_target_pairs={{1,0},{0,1},{3,2},{2,3},{5,4},{4,5},{7,6},{6,7},{9,8},{8,9},{11,10... | collective-permute-start | bytes 786440 | tf_op jit(solution)/shard_map/ppermute | solution.py:365
  53.6 0.1 shard_map.157.base
  53.7 0.1 shard_map.155.base
  53.8 0.0 collective-permute-done.10.share
  53.9 0.7 %shard_map.158.refs_0_ = bf16[256,1024]{1,0:T(8,128)(2,1)} custom-call(f32[128,1024]{1,0:T(8,128)S(1)} %shard_map.157.base, bf16[128,1024]{1,0:T(8,128)(2,1)S(1)} %collective-permute-done.10.share), custom_call_target="tpu_custom_call" | custom-call | tf_op jit(solution)/shard_map/pallas_call | solution.py:322
  54.6 4.4 %collective-permute-done.8.share = bf16[128,1024]{1,0:T(8,128)(2,1)S(1)} collective-permute-done((bf16[128,1024]{1,0:T(8,128)(2,1)S(1)}, bf16[128,1024]{1,0:T(8,128)(2,1)S(1)}, u32[]{:S(2)}, u32[]{:S(2)}) %collective-permute-start.8) | collective-permute-done | bytes 262176 | tf_op jit(solution)/shard_map/ppermute | solution.py:365
  59.0 0.7 %shard_map.159 = bf16[256,1024]{1,0:T(8,128)(2,1)} custom-call(f32[128,1024]{1,0:T(8,128)S(1)} %shard_map.155.base, bf16[128,1024]{1,0:T(8,128)(2,1)S(1)} %collective-permute-done.8.share, bf16[256,1024]{1,0:T(8,128)(2,1)} %shard_map.158.refs_0_), custom_call_target="tpu_custom_call", output_to_operand_aliasing={{}: (2, {})} | custom-call | tf_op jit(solution)/shard_map/pallas_call | solution.py:322
  (6 shorter events, 0.0 us)
Async XLA Ops:
  0.0 9.4 %copy-start.11 = (s32[256,32]{0,1:T(8,128)S(1)}, s32[256,32]{0,1:T(8,128)}, u32[]{:S(2)}) copy-start(s32[256,32]{0,1:T(8,128)} %param.23) | copy-start | bytes 98308
  0.0 9.4 %copy-start.14 = (f32[1024]{0:T(1024)S(1)}, f32[1024]{0:T(1024)}, u32[]{:S(2)}) copy-start(f32[1024]{0:T(1024)} %param.18) | copy-start | bytes 12292
  0.0 9.4 %copy-start.15 = (s32[256]{0:T(256)S(1)}, s32[256]{0:T(256)}, u32[]{:S(2)}) copy-start(s32[256]{0:T(256)} %param.24) | copy-start | bytes 3076
  1.0 8.4 %copy-start = (bf16[256,1024]{1,0:T(8,128)(2,1)S(1)}, bf16[256,1024]{1,0:T(8,128)(2,1)}, u32[]{:S(2)}) copy-start(bf16[256,1024]{1,0:T(8,128)(2,1)} %hidden.9) | copy-start | bytes 1572868
  1.0 12.7 %collective-permute-start.1 = (bf16[128,1024]{1,0:T(8,128)(2,1)S(1)}, bf16[128,1024]{1,0:T(8,128)(2,1)S(1)}, u32[]{:S(2)}, u32[]{:S(2)}) collective-permute-start(bf16[128,1024]{1,0:T(8,128)(2,1)S(1)} %constant_dynamic-slice_fusion), channel_id=1, source_target_pairs={{1,0},{0,1},{3,2},{2,3},{5,4},{4,5},{7,6},{6,7},{9,8},{8,9},{11,10... | collective-permute-start | bytes 786440 | tf_op jit(solution)/shard_map/ppermute | solution.py:365
  4.0 1.2 %copy-start.8 = (bf16[512,1024]{1,0:T(8,128)(2,1)S(1)}, bf16[512,1024]{1,0:T(8,128)(2,1)}, u32[]{:S(2)}) copy-start(bf16[512,1024]{1,0:T(8,128)(2,1)} %refs_0_.3) | copy-start | bytes 3145732
  5.3 11.0 %copy-start.7 = (bf16[1024,512]{1,0:T(8,128)(2,1)S(1)}, bf16[1024,512]{1,0:T(8,128)(2,1)}, u32[]{:S(2)}) copy-start(bf16[1024,512]{1,0:T(8,128)(2,1)} %refs_4_.7) | copy-start | bytes 3145732
  5.3 10.9 %copy-start.6 = (bf16[1024,512]{1,0:T(8,128)(2,1)S(1)}, bf16[1024,512]{1,0:T(8,128)(2,1)}, u32[]{:S(2)}) copy-start(bf16[1024,512]{1,0:T(8,128)(2,1)} %refs_3_.3) | copy-start | bytes 3145732
  5.4 18.9 %collective-permute-start.2 = (bf16[256,1024]{1,0:T(8,128)(2,1)S(1)}, bf16[256,1024]{1,0:T(8,128)(2,1)S(1)}, u32[]{:S(2)}, u32[]{:S(2)}) collective-permute-start(bf16[256,1024]{1,0:T(8,128)(2,1)S(1)} %get-tuple-element.32), channel_id=1, source_target_pairs={{1,0},{0,1},{3,2},{2,3},{5,4},{4,5},{7,6},{6,7},{9,8},{8,9},{11,10... | collective-permute-start | bytes 1572872 | tf_op jit(solution)/shard_map/ppermute | solution.py:365
  5.5 15.7 %collective-permute-start.3 = (bf16[128,1024]{1,0:T(8,128)(2,1)S(1)}, bf16[128,1024]{1,0:T(8,128)(2,1)S(1)}, u32[]{:S(2)}, u32[]{:S(2)}) collective-permute-start(bf16[128,1024]{1,0:T(8,128)(2,1)S(1)} %constant_dynamic-slice_fusion), channel_id=1, source_target_pairs={{2,0},{4,2},{6,4},{8,6},{10,8},{12,10},{14,12},{16,14},{18,16},{20... | collective-permute-start | bytes 786440 | tf_op jit(solution)/shard_map/ppermute | solution.py:375
  9.4 1.2 %copy-start.10 = (bf16[1024,512]{1,0:T(8,128)(2,1)S(1)}, bf16[1024,512]{1,0:T(8,128)(2,1)}, u32[]{:S(2)}) copy-start(bf16[1024,512]{1,0:T(8,128)(2,1)} %wq.3) | copy-start | bytes 3145732
  13.7 2.6 %copy-start.13 = (f32[1024]{0:T(1024)S(1)}, f32[1024]{0:T(1024)}, u32[]{:S(2)}) copy-start(f32[1024]{0:T(1024)} %param.16) | copy-start | bytes 12292
  13.7 8.5 %collective-permute-start.4 = (bf16[128,1024]{1,0:T(8,128)(2,1)S(1)}, bf16[128,1024]{1,0:T(8,128)(2,1)S(1)}, u32[]{:S(2)}, u32[]{:S(2)}) collective-permute-start(bf16[128,1024]{1,0:T(8,128)(2,1)S(1)} %collective-permute-done.1.refs_0_), channel_id=1, source_target_pairs={{0,2},{2,4},{4,6},{6,8},{8,10},{10,12},{12,14},{14,16},{16,18},{18... | collective-permute-start | bytes 786440 | tf_op jit(solution)/shard_map/ppermute | solution.py:409
  13.8 13.9 %collective-permute-start = (bf16[128,1024]{1,0:T(8,128)(2,1)S(1)}, bf16[128,1024]{1,0:T(8,128)(2,1)S(1)}, u32[]{:S(2)}, u32[]{:S(2)}) collective-permute-start(bf16[128,1024]{1,0:T(8,128)(2,1)S(1)} %get-tuple-element.29), channel_id=1, source_target_pairs={{1,0},{0,1},{3,2},{2,3},{5,4},{4,5},{7,6},{6,7},{9,8},{8,9},{11,10... | collective-permute-start | bytes 786440 | tf_op jit(solution)/shard_map/ppermute | solution.py:365
  16.3 1.2 %copy-start.9 = (bf16[512,1024]{1,0:T(8,128)(2,1)S(1)}, bf16[512,1024]{1,0:T(8,128)(2,1)}, u32[]{:S(2)}) copy-start(bf16[512,1024]{1,0:T(8,128)(2,1)} %refs_0_.3) | copy-start | bytes 3145732
  24.3 3.4 %copy-start.4 = (bf16[512,1024]{1,0:T(8,128)(2,1)S(1)}, bf16[512,1024]{1,0:T(8,128)(2,1)}, u32[]{:S(2)}) copy-start(bf16[512,1024]{1,0:T(8,128)(2,1)} %wo.3) | copy-start | bytes 3145732
  29.0 9.3 %collective-permute-start.5 = (bf16[128,1024]{1,0:T(8,128)(2,1)S(1)}, bf16[128,1024]{1,0:T(8,128)(2,1)S(1)}, u32[]{:S(2)}, u32[]{:S(2)}) collective-permute-start(bf16[128,1024]{1,0:T(8,128)(2,1)S(1)} %get-tuple-element.46.own), channel_id=1, source_target_pairs={{1,0},{0,1},{3,2},{2,3},{5,4},{4,5},{7,6},{6,7},{9,8},{8,9},{11,10... | collective-permute-start | bytes 786440 | tf_op jit(solution)/shard_map/ppermute | solution.py:365
  30.3 8.0 %copy-start.1 = (bf16[1024,512]{1,0:T(8,128)(2,1)S(1)}, bf16[1024,512]{1,0:T(8,128)(2,1)}, u32[]{:S(2)}) copy-start(bf16[1024,512]{1,0:T(8,128)(2,1)} %wq.5) | copy-start | bytes 3145732
  30.3 8.0 %copy-start.2 = (bf16[1024,512]{1,0:T(8,128)(2,1)S(1)}, bf16[1024,512]{1,0:T(8,128)(2,1)}, u32[]{:S(2)}) copy-start(bf16[1024,512]{1,0:T(8,128)(2,1)} %wk.3) | copy-start | bytes 3145732
  30.3 8.0 %copy-start.3 = (bf16[1024,512]{1,0:T(8,128)(2,1)S(1)}, bf16[1024,512]{1,0:T(8,128)(2,1)}, u32[]{:S(2)}) copy-start(bf16[1024,512]{1,0:T(8,128)(2,1)} %wv.3) | copy-start | bytes 3145732
  30.4 8.0 %copy-start.12 = (f32[1024]{0:T(1024)S(1)}, f32[1024]{0:T(1024)}, u32[]{:S(2)}) copy-start(f32[1024]{0:T(1024)} %param.25) | copy-start | bytes 12292
  31.2 10.5 %collective-permute-start.6 = (bf16[128,1024]{1,0:T(8,128)(2,1)S(1)}, bf16[128,1024]{1,0:T(8,128)(2,1)S(1)}, u32[]{:S(2)}, u32[]{:S(2)}) collective-permute-start(bf16[128,1024]{1,0:T(8,128)(2,1)S(1)} %shard_map.152.own), channel_id=1, source_target_pairs={{1,0},{0,1},{3,2},{2,3},{5,4},{4,5},{7,6},{6,7},{9,8},{8,9},{11,10... | collective-permute-start | bytes 786440 | tf_op jit(solution)/shard_map/ppermute | solution.py:365
  39.2 4.0 %copy-start.5 = (bf16[512,1024]{1,0:T(8,128)(2,1)S(1)}, bf16[512,1024]{1,0:T(8,128)(2,1)}, u32[]{:S(2)}) copy-start(bf16[512,1024]{1,0:T(8,128)(2,1)} %wo.5) | copy-start | bytes 3145732
  39.2 3.9 %collective-permute-start.9 = (bf16[128,1024]{1,0:T(8,128)(2,1)S(1)}, bf16[128,1024]{1,0:T(8,128)(2,1)S(1)}, u32[]{:S(2)}, u32[]{:S(2)}) collective-permute-start(bf16[128,1024]{1,0:T(8,128)(2,1)S(1)} %get-tuple-element.48.low), channel_id=1, source_target_pairs={{2,0},{4,2},{6,4},{8,6},{10,8},{12,10},{14,12},{16,14},{18,16},{20... | collective-permute-start | bytes 786440 | tf_op jit(solution)/shard_map/ppermute | solution.py:445
  42.5 8.5 %collective-permute-start.7 = (bf16[128,1024]{1,0:T(8,128)(2,1)S(1)}, bf16[128,1024]{1,0:T(8,128)(2,1)S(1)}, u32[]{:S(2)}, u32[]{:S(2)}) collective-permute-start(bf16[128,1024]{1,0:T(8,128)(2,1)S(1)} %get-tuple-element.51.high), channel_id=1, source_target_pairs={{0,2},{2,4},{4,6},{6,8},{8,10},{10,12},{12,14},{14,16},{16,18},{18... | collective-permute-start | bytes 786440 | tf_op jit(solution)/shard_map/ppermute | solution.py:446
  44.2 9.7 %collective-permute-start.10 = (bf16[128,1024]{1,0:T(8,128)(2,1)S(1)}, bf16[128,1024]{1,0:T(8,128)(2,1)S(1)}, u32[]{:S(2)}, u32[]{:S(2)}) collective-permute-start(bf16[128,1024]{1,0:T(8,128)(2,1)S(1)} %shard_map.156.share), channel_id=1, source_target_pairs={{1,0},{0,1},{3,2},{2,3},{5,4},{4,5},{7,6},{6,7},{9,8},{8,9},{11,10... | collective-permute-start | bytes 786440 | tf_op jit(solution)/shard_map/ppermute | solution.py:365
  52.1 6.9 %collective-permute-start.8 = (bf16[128,1024]{1,0:T(8,128)(2,1)S(1)}, bf16[128,1024]{1,0:T(8,128)(2,1)S(1)}, u32[]{:S(2)}, u32[]{:S(2)}) collective-permute-start(bf16[128,1024]{1,0:T(8,128)(2,1)S(1)} %shard_map.154.share), channel_id=1, source_target_pairs={{1,0},{0,1},{3,2},{2,3},{5,4},{4,5},{7,6},{6,7},{9,8},{8,9},{11,10... | collective-permute-start | bytes 786440 | tf_op jit(solution)/shard_map/ppermute | solution.py:365

commit v5 on v4

--- a/solution.py
+++ b/solution.py
@@ -442,8 +442,9 @@
         )
         queries.append(query)
         pairs.append(pair)
-    behind = lax.ppermute(pairs[0], "band", down)
-    before = lax.ppermute(pairs[1], "band", up)
+    reach = half - WIN
+    behind = lax.ppermute(pairs[0][:WIN] if reach else pairs[0], "band", down)
+    before = lax.ppermute(pairs[1][reach:] if reach else pairs[1], "band", up)
     shares = [None, None]
     for i, side, halo in ((1, 1, behind), (0, -1, before)):
         (shares[i],) = call(

time: 60 us -> 60 us (level)
  no operation moved by 1% of the time
where the time goes in v5:
time: 60 us; the launch traced here: 59.8 us
  waiting for transfers between devices  20.2 us (34%)
  Pallas kernels  19.8 us (33%)
  starting transfers between devices  14.8 us (25%)
  local copies, waits for them, and re-layouts  4.7 us (8%)
    pallas_call x12, Pallas kernels, call(): pl.pallas_call(kernel, out_shape=outs, in_specs=[whole(a.shape) for a in...  18.2 us
    ppermute x7, waiting for transfers between devices, shifted(): lax.ppermute(value, 'mp', [((i + by) % peers, i) for i in range(peers)])  13.2 us
    ppermute x7, starting transfers between devices, shifted(): lax.ppermute(value, 'mp', [((i + by) % peers, i) for i in range(peers)])  10.7 us
    ppermute x1, waiting for transfers between devices, shards(): before = lax.ppermute(pairs[1][reach:] if reach else pairs[1], 'band', up)  5.47 us
    ppermute x1, starting transfers between devices, shards(): near_rim = lax.ppermute(ends, ('band', 'mp'), outward)  3.9 us
    unnamed x32, local copies, waits for them, and re-layouts  3.73 us
    pallas_call x2, Pallas kernels, mix_half(): pl.pallas_call(functools.partial(mixed_kernel, at), out_shape=shape_of(*m...  1.48 us
  transfers between devices with their start and end apart: 11, of which 6 were waited for; matrix products, arithmetic and copies ran while one was open for 0% of the time, Pallas kernels for 30%

profile of v5, /device:TPU:0, one launch (start us, length us, event | category | flops | bytes accessed | tf_op | source)
XLA Modules:
  0.0 59.8 jit_solution(5865320923914809792)
XLA Ops:
  0.0 0.0 copy-start.11
  0.0 0.0 copy-start.15
  0.0 1.0 %constant_dynamic-slice_fusion = bf16[128,1024]{1,0:T(8,128)(2,1)S(1)} fusion(bf16[512,1024]{1,0:T(8,128)(2,1)} %refs_0_.3, s32[]{:T(128)S(6)} %select_n.3), kind=kLoop, calls=%fused_computation | loop fusion | bytes 524292 | tf_op jit(solution)/shard_map/dynamic_slice | solution.py:370
  1.0 0.0 copy-start
  1.0 3.0 %collective-permute-start.1 = (bf16[128,1024]{1,0:T(8,128)(2,1)S(1)}, bf16[128,1024]{1,0:T(8,128)(2,1)S(1)}, u32[]{:S(2)}, u32[]{:S(2)}) collective-permute-start(bf16[128,1024]{1,0:T(8,128)(2,1)S(1)} %constant_dynamic-slice_fusion), channel_id=1, source_target_pairs={{1,0},{0,1},{3,2},{2,3},{5,4},{4,5},{7,6},{6,7},{9,8},{8,9},{11,10... | collective-permute-start | bytes 786440 | tf_op jit(solution)/shard_map/ppermute | solution.py:365
  4.0 0.0 copy-start.8
  4.0 1.2 %copy-done.8 = bf16[512,1024]{1,0:T(8,128)(2,1)S(1)} copy-done((bf16[512,1024]{1,0:T(8,128)(2,1)S(1)}, bf16[512,1024]{1,0:T(8,128)(2,1)}, u32[]{:S(2)}) %copy-start.8) | copy-done | bytes 1048600
  5.3 0.0 copy-start.7
  5.3 0.1 shard_map.145
  5.3 0.0 copy-start.6
  5.4 0.1 collective-permute-start.2
  5.5 3.9 %collective-permute-start.3 = (bf16[128,1024]{1,0:T(8,128)(2,1)S(1)}, bf16[128,1024]{1,0:T(8,128)(2,1)S(1)}, u32[]{:S(2)}, u32[]{:S(2)}) collective-permute-start(bf16[128,1024]{1,0:T(8,128)(2,1)S(1)} %constant_dynamic-slice_fusion), channel_id=1, source_target_pairs={{2,0},{4,2},{6,4},{8,6},{10,8},{12,10},{14,12},{16,14},{18,16},{20... | collective-permute-start | bytes 786440 | tf_op jit(solution)/shard_map/ppermute | solution.py:375
  9.4 0.0 copy-done.11
  9.4 0.0 copy-done.14
  9.4 0.0 copy-done.15
  9.4 0.0 copy-done
  9.4 0.0 copy-start.10
  9.4 1.2 %copy-done.10 = bf16[1024,512]{1,0:T(8,128)(2,1)S(1)} copy-done((bf16[1024,512]{1,0:T(8,128)(2,1)S(1)}, bf16[1024,512]{1,0:T(8,128)(2,1)}, u32[]{:S(2)}) %copy-start.10) | copy-done | bytes 1048600
  10.6 3.0 %shard_map.146 = (f32[256,512]{1,0:T(8,128)S(1)}, f32[256,384]{1,0:T(8,128)S(1)}, f32[256,128]{1,0:T(8,128)S(1)}, f32[256,256]{1,0:T(8,128)S(1)}, bf16[256,512]{1,0:T(8,128)(2,1)S(1)}) custom-call(s32[32,256]{1,0:T(8,128)S(1)} %bitcast.5, s32[1,256]{1,0:T(1,128)S(1)} %bitcast.13, bf16[256,1024]{1,0:T(8,128)(2,1)S(1)} %copy-done, f32[1,1024]{1,0:T(1,128)S(1)} %bitcast.12, ...), custom_call_target="tpu_custom_call" | custom-call | flops 268435456 | bytes 3183616 | tf_op jit(solution)/shard_map/pallas_call | solution.py:32
  13.7 0.0 copy-start.13
  13.7 0.0 collective-permute-done.1.refs_0_
  13.7 0.1 collective-permute-start.4
  13.8 2.5 %collective-permute-start = (bf16[128,1024]{1,0:T(8,128)(2,1)S(1)}, bf16[128,1024]{1,0:T(8,128)(2,1)S(1)}, u32[]{:S(2)}, u32[]{:S(2)}) collective-permute-start(bf16[128,1024]{1,0:T(8,128)(2,1)S(1)} %get-tuple-element.29), channel_id=1, source_target_pairs={{1,0},{0,1},{3,2},{2,3},{5,4},{4,5},{7,6},{6,7},{9,8},{8,9},{11,10... | collective-permute-start | bytes 786440 | tf_op jit(solution)/shard_map/ppermute | solution.py:365
  16.3 0.0 copy-done.7
  16.3 0.0 copy-done.6
  16.3 0.0 copy-done.13
  16.3 1.2 %copy-done.9 = bf16[512,1024]{1,0:T(8,128)(2,1)S(1)} copy-done((bf16[512,1024]{1,0:T(8,128)(2,1)S(1)}, bf16[512,1024]{1,0:T(8,128)(2,1)}, u32[]{:S(2)}) %copy-start.9) | copy-done | bytes 1048600
  17.5 3.7 %shard_map.147 = (f32[256,512]{1,0:T(8,128)S(1)}, f32[256,512]{1,0:T(8,128)S(1)}, f32[256,512]{1,0:T(8,128)S(1)}) custom-call(bf16[512,1024]{1,0:T(8,128)(2,1)S(1)} %copy-done.9, f32[256,512]{1,0:T(8,128)S(1)} %get-tuple-element.36.refs_1_, f32[1,1024]{1,0:T(1,128)S(1)} %bitcast.8, bf16[1024,512]{1,0:T(8,128)(2,1)S(1)} %copy-done.6, ...), custom_call_target="tpu_custom_call" | custom-call | flops 2147483648 | bytes 5509120 | tf_op jit(solution)/shard_map/pallas_call | solution.py:32
  21.2 0.0 collective-permute-done.3.refs_0_
  21.2 1.0 %collective-permute-done.4.refs_1_ = bf16[128,1024]{1,0:T(8,128)(2,1)S(1)} collective-permute-done((bf16[128,1024]{1,0:T(8,128)(2,1)S(1)}, bf16[128,1024]{1,0:T(8,128)(2,1)S(1)}, u32[]{:S(2)}, u32[]{:S(2)}) %collective-permute-start.4) | collective-permute-done | bytes 262176 | tf_op jit(solution)/shard_map/ppermute | solution.py:409
  22.3 2.0 %shard_map.148 = (f32[256,512]{1,0:T(8,128)S(1)}, f32[256,512]{1,0:T(8,128)S(1)}, f32[256,512]{1,0:T(8,128)S(1)}) custom-call(bf16[128,1024]{1,0:T(8,128)(2,1)S(1)} %collective-permute-done.3.refs_0_, bf16[128,1024]{1,0:T(8,128)(2,1)S(1)} %collective-permute-done.4.refs_1_, f32[256,256]{1,0:T(8,128)S(1)} %get-tuple-element.35.refs_2_, ...), custom_call_target="tpu_custom_call" | custom-call | flops 1073741824 | bytes 6295552 | tf_op jit(solution)/shard_map/pallas_call | solution.py:32
  24.2 0.0 collective-permute-done.2.refs_1_
  24.3 0.0 copy-start.4
  24.3 3.4 %shard_map.149 = (f32[256,512]{1,0:T(8,128)S(1)}, f32[256,512]{1,0:T(8,128)S(1)}, f32[256,512]{1,0:T(8,128)S(1)}) custom-call(bf16[128,1024]{1,0:T(8,128)(2,1)S(1)} %collective-permute-done.1.refs_0_, bf16[256,1024]{1,0:T(8,128)(2,1)S(1)} %collective-permute-done.2.refs_1_, f32[256,384]{1,0:T(8,128)S(1)} %get-tuple-element.33.refs_2_, ...), custom_call_target="tpu_custom_call" | custom-call | flops 1610612736 | bytes 6688768 | tf_op jit(solution)/shard_map/pallas_call | solution.py:32
  27.7 0.0 collective-permute-done.refs_0_
  27.7 0.0 copy-done.4
  27.7 1.3 %shard_map.150 = (bf16[128,1024]{1,0:T(8,128)(2,1)S(1)}, bf16[128,512]{1,0:T(8,128)(2,1)S(1)}, bf16[128,512]{1,0:T(8,128)(2,1)S(1)}) custom-call(bf16[128,1024]{1,0:T(8,128)(2,1)S(1)} %collective-permute-done.refs_0_, f32[256,128]{1,0:T(8,128)S(1)} %get-tuple-element.30.refs_1_.log, f32[1,1024]{1,0:T(1,128)S(1)} %bitcast.11, ...), custom_call_target="tpu_custom_call" | custom-call | flops 536870912 | bytes 5902336 | tf_op jit(solution)/shard_map/pallas_call | solution.py:32
  29.0 1.3 %collective-permute-start.5 = (bf16[128,1024]{1,0:T(8,128)(2,1)S(1)}, bf16[128,1024]{1,0:T(8,128)(2,1)S(1)}, u32[]{:S(2)}, u32[]{:S(2)}) collective-permute-start(bf16[128,1024]{1,0:T(8,128)(2,1)S(1)} %get-tuple-element.46.own), channel_id=1, source_target_pairs={{1,0},{0,1},{3,2},{2,3},{5,4},{4,5},{7,6},{6,7},{9,8},{8,9},{11,10... | collective-permute-start | bytes 786440 | tf_op jit(solution)/shard_map/ppermute | solution.py:365
  30.4 0.9 %shard_map.152.own = bf16[128,1024]{1,0:T(8,128)(2,1)S(1)} custom-call(f32[256,128]{1,0:T(8,128)S(1)} %get-tuple-element.30.refs_1_.log, bf16[256,512]{1,0:T(8,128)(2,1)S(1)} %get-tuple-element.31.refs_5_.refs_6_.query, bf16[128,512]{1,0:T(8,128)(2,1)S(1)} %get-tuple-element.49.keys, bf16[128,512]{1,0:T(8,128)(2,1)S(1)} %get-tuple-element.50.values, ...), custom_call_target="tpu_custom_call" | custom-call | flops 134217728 | bytes 3538944 | tf_op jit(solution)/shard_map/pallas_call | solution.py:32
  31.2 0.8 %collective-permute-start.6 = (bf16[128,1024]{1,0:T(8,128)(2,1)S(1)}, bf16[128,1024]{1,0:T(8,128)(2,1)S(1)}, u32[]{:S(2)}, u32[]{:S(2)}) collective-permute-start(bf16[128,1024]{1,0:T(8,128)(2,1)S(1)} %shard_map.152.own), channel_id=1, source_target_pairs={{1,0},{0,1},{3,2},{2,3},{5,4},{4,5},{7,6},{6,7},{9,8},{8,9},{11,10... | collective-permute-start | bytes 786440 | tf_op jit(solution)/shard_map/ppermute | solution.py:365
  32.1 6.3 %collective-permute-done.5.other = bf16[128,1024]{1,0:T(8,128)(2,1)S(1)} collective-permute-done((bf16[128,1024]{1,0:T(8,128)(2,1)S(1)}, bf16[128,1024]{1,0:T(8,128)(2,1)S(1)}, u32[]{:S(2)}, u32[]{:S(2)}) %collective-permute-start.5) | collective-permute-done | bytes 262176 | tf_op jit(solution)/shard_map/ppermute | solution.py:365
  38.3 0.0 copy-done.1
  38.3 0.0 copy-done.2
  38.3 0.0 copy-done.3
  38.3 0.0 copy-done.12
  38.4 0.8 %shard_map.151 = (bf16[128,512]{1,0:T(8,128)(2,1)S(1)}, bf16[128,1024]{1,0:T(8,128)(2,1)S(1)}) custom-call(bf16[256,1024]{1,0:T(8,128)(2,1)S(1)} %copy-done, bf16[128,1024]{1,0:T(8,128)(2,1)S(1)} %get-tuple-element.46.own, bf16[128,1024]{1,0:T(8,128)(2,1)S(1)} %collective-permute-done.5.other, f32[1,1024]{1,0:T(1,128)S(1)} %bitcast.6, ...), custom_call_target="tpu_custom_call" | custom-call | flops 402653184 | bytes 4591616 | tf_op jit(solution)/shard_map/pallas_call | solution.py:32
  39.2 0.0 copy-start.5
  39.2 0.1 collective-permute-start.9
  39.2 2.5 %collective-permute-done.6.other = bf16[128,1024]{1,0:T(8,128)(2,1)S(1)} collective-permute-done((bf16[128,1024]{1,0:T(8,128)(2,1)S(1)}, bf16[128,1024]{1,0:T(8,128)(2,1)S(1)}, u32[]{:S(2)}, u32[]{:S(2)}) %collective-permute-start.6) | collective-permute-done | bytes 262176 | tf_op jit(solution)/shard_map/ppermute | solution.py:365
  41.7 0.8 %shard_map.153 = (bf16[128,512]{1,0:T(8,128)(2,1)S(1)}, bf16[128,1024]{1,0:T(8,128)(2,1)S(1)}) custom-call(bf16[256,1024]{1,0:T(8,128)(2,1)S(1)} %copy-done, bf16[128,1024]{1,0:T(8,128)(2,1)S(1)} %shard_map.152.own, bf16[128,1024]{1,0:T(8,128)(2,1)S(1)} %collective-permute-done.6.other, f32[1,1024]{1,0:T(1,128)S(1)} %bitcast.7, ...), custom_call_target="tpu_custom_call" | custom-call | flops 402653184 | bytes 4591616 | tf_op jit(solution)/shard_map/pallas_call | solution.py:32
  42.5 0.1 collective-permute-start.7
  42.6 0.5 collective-permute-done.9.halo
  43.1 0.0 copy-done.5
  43.1 1.0 %shard_map.156.share = bf16[128,1024]{1,0:T(8,128)(2,1)S(1)} custom-call(bf16[128,512]{1,0:T(8,128)(2,1)S(1)} %get-tuple-element.52.query, bf16[128,1024]{1,0:T(8,128)(2,1)S(1)} %get-tuple-element.48.low, bf16[128,1024]{1,0:T(8,128)(2,1)S(1)} %get-tuple-element.51.high, bf16[128,1024]{1,0:T(8,128)(2,1)S(1)} %collective-permute-done.9.halo, ...), custom_call_target="tpu_custom_call" | custom-call | flops 134217728 | bytes 2228224 | tf_op jit(solution)/shard_map/pallas_call | solution.py:32
  44.2 1.4 %collective-permute-start.10 = (bf16[128,1024]{1,0:T(8,128)(2,1)S(1)}, bf16[128,1024]{1,0:T(8,128)(2,1)S(1)}, u32[]{:S(2)}, u32[]{:S(2)}) collective-permute-start(bf16[128,1024]{1,0:T(8,128)(2,1)S(1)} %shard_map.156.share), channel_id=1, source_target_pairs={{1,0},{0,1},{3,2},{2,3},{5,4},{4,5},{7,6},{6,7},{9,8},{8,9},{11,10... | collective-permute-start | bytes 786440 | tf_op jit(solution)/shard_map/ppermute | solution.py:365
  45.6 5.5 %collective-permute-done.7.halo = bf16[128,1024]{1,0:T(8,128)(2,1)S(1)} collective-permute-done((bf16[128,1024]{1,0:T(8,128)(2,1)S(1)}, bf16[128,1024]{1,0:T(8,128)(2,1)S(1)}, u32[]{:S(2)}, u32[]{:S(2)}) %collective-permute-start.7) | collective-permute-done | bytes 262176 | tf_op jit(solution)/shard_map/ppermute | solution.py:447
  51.1 1.0 %shard_map.154.share = bf16[128,1024]{1,0:T(8,128)(2,1)S(1)} custom-call(bf16[128,512]{1,0:T(8,128)(2,1)S(1)} %get-tuple-element.47.query, bf16[128,1024]{1,0:T(8,128)(2,1)S(1)} %get-tuple-element.48.low, bf16[128,1024]{1,0:T(8,128)(2,1)S(1)} %get-tuple-element.51.high, bf16[128,1024]{1,0:T(8,128)(2,1)S(1)} %collective-permute-done.7.halo, ...), custom_call_target="tpu_custom_call" | custom-call | flops 134217728 | bytes 2228224 | tf_op jit(solution)/shard_map/pallas_call | solution.py:32
  52.1 1.5 %collective-permute-start.8 = (bf16[128,1024]{1,0:T(8,128)(2,1)S(1)}, bf16[128,1024]{1,0:T(8,128)(2,1)S(1)}, u32[]{:S(2)}, u32[]{:S(2)}) collective-permute-start(bf16[128,1024]{1,0:T(8,128)(2,1)S(1)} %shard_map.154.share), channel_id=1, source_target_pairs={{1,0},{0,1},{3,2},{2,3},{5,4},{4,5},{7,6},{6,7},{9,8},{8,9},{11,10... | collective-permute-start | bytes 786440 | tf_op jit(solution)/shard_map/ppermute | solution.py:365
  53.6 0.1 shard_map.157.base
  53.7 0.1 shard_map.155.base
  53.8 0.0 collective-permute-done.10.share
  53.9 0.7 %shard_map.158.refs_0_ = bf16[256,1024]{1,0:T(8,128)(2,1)} custom-call(f32[128,1024]{1,0:T(8,128)S(1)} %shard_map.157.base, bf16[128,1024]{1,0:T(8,128)(2,1)S(1)} %collective-permute-done.10.share), custom_call_target="tpu_custom_call" | custom-call | tf_op jit(solution)/shard_map/pallas_call | solution.py:322
  54.6 4.4 %collective-permute-done.8.share = bf16[128,1024]{1,0:T(8,128)(2,1)S(1)} collective-permute-done((bf16[128,1024]{1,0:T(8,128)(2,1)S(1)}, bf16[128,1024]{1,0:T(8,128)(2,1)S(1)}, u32[]{:S(2)}, u32[]{:S(2)}) %collective-permute-start.8) | collective-permute-done | bytes 262176 | tf_op jit(solution)/shard_map/ppermute | solution.py:365
  59.0 0.7 %shard_map.159 = bf16[256,1024]{1,0:T(8,128)(2,1)} custom-call(f32[128,1024]{1,0:T(8,128)S(1)} %shard_map.155.base, bf16[128,1024]{1,0:T(8,128)(2,1)S(1)} %collective-permute-done.8.share, bf16[256,1024]{1,0:T(8,128)(2,1)} %shard_map.158.refs_0_), custom_call_target="tpu_custom_call", output_to_operand_aliasing={{}: (2, {})} | custom-call | tf_op jit(solution)/shard_map/pallas_call | solution.py:322
  (6 shorter events, 0.0 us)
Async XLA Ops:
  0.0 9.4 %copy-start.11 = (s32[256,32]{0,1:T(8,128)S(1)}, s32[256,32]{0,1:T(8,128)}, u32[]{:S(2)}) copy-start(s32[256,32]{0,1:T(8,128)} %param.23) | copy-start | bytes 98308
  0.0 9.4 %copy-start.14 = (f32[1024]{0:T(1024)S(1)}, f32[1024]{0:T(1024)}, u32[]{:S(2)}) copy-start(f32[1024]{0:T(1024)} %param.18) | copy-start | bytes 12292
  0.0 9.4 %copy-start.15 = (s32[256]{0:T(256)S(1)}, s32[256]{0:T(256)}, u32[]{:S(2)}) copy-start(s32[256]{0:T(256)} %param.24) | copy-start | bytes 3076
  1.0 8.4 %copy-start = (bf16[256,1024]{1,0:T(8,128)(2,1)S(1)}, bf16[256,1024]{1,0:T(8,128)(2,1)}, u32[]{:S(2)}) copy-start(bf16[256,1024]{1,0:T(8,128)(2,1)} %hidden.9) | copy-start | bytes 1572868
  1.0 12.7 %collective-permute-start.1 = (bf16[128,1024]{1,0:T(8,128)(2,1)S(1)}, bf16[128,1024]{1,0:T(8,128)(2,1)S(1)}, u32[]{:S(2)}, u32[]{:S(2)}) collective-permute-start(bf16[128,1024]{1,0:T(8,128)(2,1)S(1)} %constant_dynamic-slice_fusion), channel_id=1, source_target_pairs={{1,0},{0,1},{3,2},{2,3},{5,4},{4,5},{7,6},{6,7},{9,8},{8,9},{11,10... | collective-permute-start | bytes 786440 | tf_op jit(solution)/shard_map/ppermute | solution.py:365
  4.0 1.2 %copy-start.8 = (bf16[512,1024]{1,0:T(8,128)(2,1)S(1)}, bf16[512,1024]{1,0:T(8,128)(2,1)}, u32[]{:S(2)}) copy-start(bf16[512,1024]{1,0:T(8,128)(2,1)} %refs_0_.3) | copy-start | bytes 3145732
  5.3 11.0 %copy-start.7 = (bf16[1024,512]{1,0:T(8,128)(2,1)S(1)}, bf16[1024,512]{1,0:T(8,128)(2,1)}, u32[]{:S(2)}) copy-start(bf16[1024,512]{1,0:T(8,128)(2,1)} %refs_4_.7) | copy-start | bytes 3145732
  5.3 10.9 %copy-start.6 = (bf16[1024,512]{1,0:T(8,128)(2,1)S(1)}, bf16[1024,512]{1,0:T(8,128)(2,1)}, u32[]{:S(2)}) copy-start(bf16[1024,512]{1,0:T(8,128)(2,1)} %refs_3_.3) | copy-start | bytes 3145732
  5.4 18.9 %collective-permute-start.2 = (bf16[256,1024]{1,0:T(8,128)(2,1)S(1)}, bf16[256,1024]{1,0:T(8,128)(2,1)S(1)}, u32[]{:S(2)}, u32[]{:S(2)}) collective-permute-start(bf16[256,1024]{1,0:T(8,128)(2,1)S(1)} %get-tuple-element.32), channel_id=1, source_target_pairs={{1,0},{0,1},{3,2},{2,3},{5,4},{4,5},{7,6},{6,7},{9,8},{8,9},{11,10... | collective-permute-start | bytes 1572872 | tf_op jit(solution)/shard_map/ppermute | solution.py:365
  5.5 15.7 %collective-permute-start.3 = (bf16[128,1024]{1,0:T(8,128)(2,1)S(1)}, bf16[128,1024]{1,0:T(8,128)(2,1)S(1)}, u32[]{:S(2)}, u32[]{:S(2)}) collective-permute-start(bf16[128,1024]{1,0:T(8,128)(2,1)S(1)} %constant_dynamic-slice_fusion), channel_id=1, source_target_pairs={{2,0},{4,2},{6,4},{8,6},{10,8},{12,10},{14,12},{16,14},{18,16},{20... | collective-permute-start | bytes 786440 | tf_op jit(solution)/shard_map/ppermute | solution.py:375
  9.4 1.2 %copy-start.10 = (bf16[1024,512]{1,0:T(8,128)(2,1)S(1)}, bf16[1024,512]{1,0:T(8,128)(2,1)}, u32[]{:S(2)}) copy-start(bf16[1024,512]{1,0:T(8,128)(2,1)} %wq.3) | copy-start | bytes 3145732
  13.7 2.6 %copy-start.13 = (f32[1024]{0:T(1024)S(1)}, f32[1024]{0:T(1024)}, u32[]{:S(2)}) copy-start(f32[1024]{0:T(1024)} %param.16) | copy-start | bytes 12292
  13.7 8.5 %collective-permute-start.4 = (bf16[128,1024]{1,0:T(8,128)(2,1)S(1)}, bf16[128,1024]{1,0:T(8,128)(2,1)S(1)}, u32[]{:S(2)}, u32[]{:S(2)}) collective-permute-start(bf16[128,1024]{1,0:T(8,128)(2,1)S(1)} %collective-permute-done.1.refs_0_), channel_id=1, source_target_pairs={{0,2},{2,4},{4,6},{6,8},{8,10},{10,12},{12,14},{14,16},{16,18},{18... | collective-permute-start | bytes 786440 | tf_op jit(solution)/shard_map/ppermute | solution.py:409
  13.8 13.9 %collective-permute-start = (bf16[128,1024]{1,0:T(8,128)(2,1)S(1)}, bf16[128,1024]{1,0:T(8,128)(2,1)S(1)}, u32[]{:S(2)}, u32[]{:S(2)}) collective-permute-start(bf16[128,1024]{1,0:T(8,128)(2,1)S(1)} %get-tuple-element.29), channel_id=1, source_target_pairs={{1,0},{0,1},{3,2},{2,3},{5,4},{4,5},{7,6},{6,7},{9,8},{8,9},{11,10... | collective-permute-start | bytes 786440 | tf_op jit(solution)/shard_map/ppermute | solution.py:365
  16.3 1.2 %copy-start.9 = (bf16[512,1024]{1,0:T(8,128)(2,1)S(1)}, bf16[512,1024]{1,0:T(8,128)(2,1)}, u32[]{:S(2)}) copy-start(bf16[512,1024]{1,0:T(8,128)(2,1)} %refs_0_.3) | copy-start | bytes 3145732
  24.3 3.4 %copy-start.4 = (bf16[512,1024]{1,0:T(8,128)(2,1)S(1)}, bf16[512,1024]{1,0:T(8,128)(2,1)}, u32[]{:S(2)}) copy-start(bf16[512,1024]{1,0:T(8,128)(2,1)} %wo.3) | copy-start | bytes 3145732
  29.0 9.3 %collective-permute-start.5 = (bf16[128,1024]{1,0:T(8,128)(2,1)S(1)}, bf16[128,1024]{1,0:T(8,128)(2,1)S(1)}, u32[]{:S(2)}, u32[]{:S(2)}) collective-permute-start(bf16[128,1024]{1,0:T(8,128)(2,1)S(1)} %get-tuple-element.46.own), channel_id=1, source_target_pairs={{1,0},{0,1},{3,2},{2,3},{5,4},{4,5},{7,6},{6,7},{9,8},{8,9},{11,10... | collective-permute-start | bytes 786440 | tf_op jit(solution)/shard_map/ppermute | solution.py:365
  30.3 8.0 %copy-start.1 = (bf16[1024,512]{1,0:T(8,128)(2,1)S(1)}, bf16[1024,512]{1,0:T(8,128)(2,1)}, u32[]{:S(2)}) copy-start(bf16[1024,512]{1,0:T(8,128)(2,1)} %wq.5) | copy-start | bytes 3145732
  30.3 8.0 %copy-start.2 = (bf16[1024,512]{1,0:T(8,128)(2,1)S(1)}, bf16[1024,512]{1,0:T(8,128)(2,1)}, u32[]{:S(2)}) copy-start(bf16[1024,512]{1,0:T(8,128)(2,1)} %wk.3) | copy-start | bytes 3145732
  30.3 8.0 %copy-start.3 = (bf16[1024,512]{1,0:T(8,128)(2,1)S(1)}, bf16[1024,512]{1,0:T(8,128)(2,1)}, u32[]{:S(2)}) copy-start(bf16[1024,512]{1,0:T(8,128)(2,1)} %wv.3) | copy-start | bytes 3145732
  30.4 8.0 %copy-start.12 = (f32[1024]{0:T(1024)S(1)}, f32[1024]{0:T(1024)}, u32[]{:S(2)}) copy-start(f32[1024]{0:T(1024)} %param.25) | copy-start | bytes 12292
  31.2 10.5 %collective-permute-start.6 = (bf16[128,1024]{1,0:T(8,128)(2,1)S(1)}, bf16[128,1024]{1,0:T(8,128)(2,1)S(1)}, u32[]{:S(2)}, u32[]{:S(2)}) collective-permute-start(bf16[128,1024]{1,0:T(8,128)(2,1)S(1)} %shard_map.152.own), channel_id=1, source_target_pairs={{1,0},{0,1},{3,2},{2,3},{5,4},{4,5},{7,6},{6,7},{9,8},{8,9},{11,10... | collective-permute-start | bytes 786440 | tf_op jit(solution)/shard_map/ppermute | solution.py:365
  39.2 4.0 %copy-start.5 = (bf16[512,1024]{1,0:T(8,128)(2,1)S(1)}, bf16[512,1024]{1,0:T(8,128)(2,1)}, u32[]{:S(2)}) copy-start(bf16[512,1024]{1,0:T(8,128)(2,1)} %wo.5) | copy-start | bytes 3145732
  39.2 3.9 %collective-permute-start.9 = (bf16[128,1024]{1,0:T(8,128)(2,1)S(1)}, bf16[128,1024]{1,0:T(8,128)(2,1)S(1)}, u32[]{:S(2)}, u32[]{:S(2)}) collective-permute-start(bf16[128,1024]{1,0:T(8,128)(2,1)S(1)} %get-tuple-element.48.low), channel_id=1, source_target_pairs={{2,0},{4,2},{6,4},{8,6},{10,8},{12,10},{14,12},{16,14},{18,16},{20... | collective-permute-start | bytes 786440 | tf_op jit(solution)/shard_map/ppermute | solution.py:446
  42.5 8.5 %collective-permute-start.7 = (bf16[128,1024]{1,0:T(8,128)(2,1)S(1)}, bf16[128,1024]{1,0:T(8,128)(2,1)S(1)}, u32[]{:S(2)}, u32[]{:S(2)}) collective-permute-start(bf16[128,1024]{1,0:T(8,128)(2,1)S(1)} %get-tuple-element.51.high), channel_id=1, source_target_pairs={{0,2},{2,4},{4,6},{6,8},{8,10},{10,12},{12,14},{14,16},{16,18},{18... | collective-permute-start | bytes 786440 | tf_op jit(solution)/shard_map/ppermute | solution.py:447
  44.2 9.7 %collective-permute-start.10 = (bf16[128,1024]{1,0:T(8,128)(2,1)S(1)}, bf16[128,1024]{1,0:T(8,128)(2,1)S(1)}, u32[]{:S(2)}, u32[]{:S(2)}) collective-permute-start(bf16[128,1024]{1,0:T(8,128)(2,1)S(1)} %shard_map.156.share), channel_id=1, source_target_pairs={{1,0},{0,1},{3,2},{2,3},{5,4},{4,5},{7,6},{6,7},{9,8},{8,9},{11,10... | collective-permute-start | bytes 786440 | tf_op jit(solution)/shard_map/ppermute | solution.py:365
  52.1 6.9 %collective-permute-start.8 = (bf16[128,1024]{1,0:T(8,128)(2,1)S(1)}, bf16[128,1024]{1,0:T(8,128)(2,1)S(1)}, u32[]{:S(2)}, u32[]{:S(2)}) collective-permute-start(bf16[128,1024]{1,0:T(8,128)(2,1)S(1)} %shard_map.154.share), channel_id=1, source_target_pairs={{1,0},{0,1},{3,2},{2,3},{5,4},{4,5},{7,6},{6,7},{9,8},{8,9},{11,10... | collective-permute-start | bytes 786440 | tf_op jit(solution)/shard_map/ppermute | solution.py:365

commit v6 on v5

--- a/solution.py
+++ b/solution.py
@@ -260,13 +260,15 @@
     return hidden[at : at + own.shape[0], :].astype(f32) + total
 
 
-def node_kernel(at, hidden, own, other, gain, wq, wk, wv, query, pair, norm):
+def node_kernel(at, hidden, own, other, gain, wk, wv, norm, pair):
     norm[...] = layer_norm(latent_of(at, hidden, own, other), gain[...]).astype(bf16)
-    columns = query.shape[1]
-    scaled = dot(norm[...], wq[...]).astype(bf16) * (HEAD_DIM**-0.5)
-    query[...] = scaled.astype(bf16)
+    columns = wk.shape[1]
     for weight, col in ((wk, 0), (wv, columns)):
         pair[:, col : col + columns] = dot(norm[...], weight[...]).astype(bf16)
+
+
+def query_kernel(norm, wq, query):
+    query[...] = (dot(norm[...], wq[...]).astype(bf16) * (HEAD_DIM**-0.5)).astype(bf16)
 
 
 def window_bias(queries, keys, shift):
@@ -433,12 +435,15 @@
     other = [exchange(share) for share in own]
     queries, pairs = [], []
     for i in range(2):
-        query, pair = call(
+        norm, pair = call(
             functools.partial(node_kernel, i * half),
-            [shape_of(half, columns, dtype=bf16), shape_of(half, 2 * columns, dtype=bf16)],
-            [hidden_in, own[i], other[i], proc_gain, proc_wq, proc_wk, proc_wv],
-            [pltpu.VMEM((half, hidden_in.shape[1]), bf16)],
-            6 * half * proc_wq.size,
+            [shape_of(half, hidden_in.shape[1], dtype=bf16), shape_of(half, 2 * columns, dtype=bf16)],
+            [hidden_in, own[i], other[i], proc_gain, proc_wk, proc_wv],
+            (),
+            4 * half * proc_wq.size,
+        )
+        (query,) = call(
+            query_kernel, [shape_of(half, columns, dtype=bf16)], [norm, proc_wq], (), 2 * half * proc_wq.size
         )
         queries.append(query)
         pairs.append(pair)

time: 60 us -> 61.3 us (1.022)
  local copies, waits for them, and re-layouts: 4.7 us -> 5.58 us
    ppermute x7, waiting for transfers between devices: 13.2 us -> 14.4 us  [shifted(): lax.ppermute(value, 'mp', [((i + by) % peers, i) for i in range(peers)])]
    ppermute x1, waiting for transfers between devices: 5.47 us -> 4.4 us  [shards(): before = lax.ppermute(pairs[1][reach:] if reach else pairs[1], 'band', up)]
    unnamed x32, local copies, waits for them, and re-layouts: 3.73 us -> 4.61 us
    pallas_call x12 -> x14, Pallas kernels: 18.2 us -> 18.6 us  [call(): pl.pallas_call(kernel, out_shape=outs, in_specs=[whole(a.shape) for a in...]
where the time goes in v6:
time: 61.3 us; the launch traced here: 61 us
  Pallas kernels  20.1 us (33%)
  waiting for transfers between devices  19.8 us (32%)
  starting transfers between devices  15 us (24%)
  local copies, waits for them, and re-layouts  5.58 us (9%)
    pallas_call x14, Pallas kernels, call(): pl.pallas_call(kernel, out_shape=outs, in_specs=[whole(a.shape) for a in...  18.6 us
    ppermute x7, waiting for transfers between devices, shifted(): lax.ppermute(value, 'mp', [((i + by) % peers, i) for i in range(peers)])  14.4 us
    ppermute x7, starting transfers between devices, shifted(): lax.ppermute(value, 'mp', [((i + by) % peers, i) for i in range(peers)])  10.8 us
    unnamed x32, local copies, waits for them, and re-layouts  4.61 us
    ppermute x1, waiting for transfers between devices, shards(): before = lax.ppermute(pairs[1][reach:] if reach else pairs[1], 'band', up)  4.4 us
    ppermute x1, starting transfers between devices, shards(): near_rim = lax.ppermute(ends, ('band', 'mp'), outward)  3.9 us
    pallas_call x2, Pallas kernels, mix_half(): pl.pallas_call(functools.partial(mixed_kernel, at), out_shape=shape_of(*m...  1.49 us
  transfers between devices with their start and end apart: 11, of which 6 were waited for; matrix products, arithmetic and copies ran while one was open for 0% of the time, Pallas kernels for 30%

profile of v6, /device:TPU:0, one launch (start us, length us, event | category | flops | bytes accessed | tf_op | source)
XLA Modules:
  0.0 61.0 jit_solution(9173657926263699719)
XLA Ops:
  0.0 0.0 copy-start.11
  0.0 1.0 %constant_dynamic-slice_fusion = bf16[128,1024]{1,0:T(8,128)(2,1)S(1)} fusion(bf16[512,1024]{1,0:T(8,128)(2,1)} %refs_0_.3, s32[]{:T(128)S(6)} %select_n.3), kind=kLoop, calls=%fused_computation | loop fusion | bytes 524292 | tf_op jit(solution)/shard_map/dynamic_slice | solution.py:372
  1.0 0.0 copy-start
  1.0 3.0 %collective-permute-start.1 = (bf16[128,1024]{1,0:T(8,128)(2,1)S(1)}, bf16[128,1024]{1,0:T(8,128)(2,1)S(1)}, u32[]{:S(2)}, u32[]{:S(2)}) collective-permute-start(bf16[128,1024]{1,0:T(8,128)(2,1)S(1)} %constant_dynamic-slice_fusion), channel_id=1, source_target_pairs={{1,0},{0,1},{3,2},{2,3},{5,4},{4,5},{7,6},{6,7},{9,8},{8,9},{11,10... | collective-permute-start | bytes 786440 | tf_op jit(solution)/shard_map/ppermute | solution.py:367
  4.0 1.2 %copy-done.8 = bf16[512,1024]{1,0:T(8,128)(2,1)S(1)} copy-done((bf16[512,1024]{1,0:T(8,128)(2,1)S(1)}, bf16[512,1024]{1,0:T(8,128)(2,1)}, u32[]{:S(2)}) %copy-start.8) | copy-done | bytes 1048600
  5.3 0.1 shard_map.145
  5.3 0.0 copy-start.6
  5.4 0.1 collective-permute-start.2
  5.5 3.9 %collective-permute-start.3 = (bf16[128,1024]{1,0:T(8,128)(2,1)S(1)}, bf16[128,1024]{1,0:T(8,128)(2,1)S(1)}, u32[]{:S(2)}, u32[]{:S(2)}) collective-permute-start(bf16[128,1024]{1,0:T(8,128)(2,1)S(1)} %constant_dynamic-slice_fusion), channel_id=1, source_target_pairs={{2,0},{4,2},{6,4},{8,6},{10,8},{12,10},{14,12},{16,14},{18,16},{20... | collective-permute-start | bytes 786440 | tf_op jit(solution)/shard_map/ppermute | solution.py:377
  9.4 0.0 copy-done.11
  9.4 0.0 copy-done.14
  9.4 0.0 copy-done.15
  9.4 0.0 copy-done
  9.4 0.0 copy-start.10
  9.4 1.2 %copy-done.10 = bf16[1024,512]{1,0:T(8,128)(2,1)S(1)} copy-done((bf16[1024,512]{1,0:T(8,128)(2,1)S(1)}, bf16[1024,512]{1,0:T(8,128)(2,1)}, u32[]{:S(2)}) %copy-start.10) | copy-done | bytes 1048600
  10.6 3.0 %shard_map.146 = (f32[256,512]{1,0:T(8,128)S(1)}, f32[256,384]{1,0:T(8,128)S(1)}, f32[256,128]{1,0:T(8,128)S(1)}, f32[256,256]{1,0:T(8,128)S(1)}, bf16[256,512]{1,0:T(8,128)(2,1)S(1)}) custom-call(s32[32,256]{1,0:T(8,128)S(1)} %bitcast.5, s32[1,256]{1,0:T(1,128)S(1)} %bitcast.13, bf16[256,1024]{1,0:T(8,128)(2,1)S(1)} %copy-done, f32[1,1024]{1,0:T(1,128)S(1)} %bitcast.12, ...), custom_call_target="tpu_custom_call" | custom-call | flops 268435456 | bytes 3183616 | tf_op jit(solution)/shard_map/pallas_call | solution.py:32
  13.7 0.0 copy-start.13
  13.7 0.0 collective-permute-done.1.refs_0_
  13.7 0.1 collective-permute-start.4
  13.8 2.5 %collective-permute-start = (bf16[128,1024]{1,0:T(8,128)(2,1)S(1)}, bf16[128,1024]{1,0:T(8,128)(2,1)S(1)}, u32[]{:S(2)}, u32[]{:S(2)}) collective-permute-start(bf16[128,1024]{1,0:T(8,128)(2,1)S(1)} %get-tuple-element.29), channel_id=1, source_target_pairs={{1,0},{0,1},{3,2},{2,3},{5,4},{4,5},{7,6},{6,7},{9,8},{8,9},{11,10... | collective-permute-start | bytes 786440 | tf_op jit(solution)/shard_map/ppermute | solution.py:367
  16.3 0.0 copy-done.7
  16.3 0.0 copy-done.6
  16.3 0.0 copy-done.13
  16.3 1.2 %copy-done.9 = bf16[512,1024]{1,0:T(8,128)(2,1)S(1)} copy-done((bf16[512,1024]{1,0:T(8,128)(2,1)S(1)}, bf16[512,1024]{1,0:T(8,128)(2,1)}, u32[]{:S(2)}) %copy-start.9) | copy-done | bytes 1048600
  17.5 3.7 %shard_map.147 = (f32[256,512]{1,0:T(8,128)S(1)}, f32[256,512]{1,0:T(8,128)S(1)}, f32[256,512]{1,0:T(8,128)S(1)}) custom-call(bf16[512,1024]{1,0:T(8,128)(2,1)S(1)} %copy-done.9, f32[256,512]{1,0:T(8,128)S(1)} %get-tuple-element.36.refs_1_, f32[1,1024]{1,0:T(1,128)S(1)} %bitcast.8, bf16[1024,512]{1,0:T(8,128)(2,1)S(1)} %copy-done.6, ...), custom_call_target="tpu_custom_call" | custom-call | flops 2147483648 | bytes 5509120 | tf_op jit(solution)/shard_map/pallas_call | solution.py:32
  21.2 0.0 collective-permute-done.3.refs_0_
  21.2 1.0 %collective-permute-done.4.refs_1_ = bf16[128,1024]{1,0:T(8,128)(2,1)S(1)} collective-permute-done((bf16[128,1024]{1,0:T(8,128)(2,1)S(1)}, bf16[128,1024]{1,0:T(8,128)(2,1)S(1)}, u32[]{:S(2)}, u32[]{:S(2)}) %collective-permute-start.4) | collective-permute-done | bytes 262176 | tf_op jit(solution)/shard_map/ppermute | solution.py:411
  22.3 2.0 %shard_map.148 = (f32[256,512]{1,0:T(8,128)S(1)}, f32[256,512]{1,0:T(8,128)S(1)}, f32[256,512]{1,0:T(8,128)S(1)}) custom-call(bf16[128,1024]{1,0:T(8,128)(2,1)S(1)} %collective-permute-done.3.refs_0_, bf16[128,1024]{1,0:T(8,128)(2,1)S(1)} %collective-permute-done.4.refs_1_, f32[256,256]{1,0:T(8,128)S(1)} %get-tuple-element.35.refs_2_, ...), custom_call_target="tpu_custom_call" | custom-call | flops 1073741824 | bytes 6295552 | tf_op jit(solution)/shard_map/pallas_call | solution.py:32
  24.2 0.0 collective-permute-done.2.refs_1_
  24.3 0.0 copy-start.1
  24.3 3.4 %shard_map.149 = (f32[256,512]{1,0:T(8,128)S(1)}, f32[256,512]{1,0:T(8,128)S(1)}, f32[256,512]{1,0:T(8,128)S(1)}) custom-call(bf16[128,1024]{1,0:T(8,128)(2,1)S(1)} %collective-permute-done.1.refs_0_, bf16[256,1024]{1,0:T(8,128)(2,1)S(1)} %collective-permute-done.2.refs_1_, f32[256,384]{1,0:T(8,128)S(1)} %get-tuple-element.33.refs_2_, ...), custom_call_target="tpu_custom_call" | custom-call | flops 1610612736 | bytes 6688768 | tf_op jit(solution)/shard_map/pallas_call | solution.py:32
  27.6 0.0 collective-permute-done.refs_0_
  27.7 0.0 copy-done.1
  27.7 1.3 %shard_map.150 = (bf16[128,1024]{1,0:T(8,128)(2,1)S(1)}, bf16[128,512]{1,0:T(8,128)(2,1)S(1)}, bf16[128,512]{1,0:T(8,128)(2,1)S(1)}) custom-call(bf16[128,1024]{1,0:T(8,128)(2,1)S(1)} %collective-permute-done.refs_0_, f32[256,128]{1,0:T(8,128)S(1)} %get-tuple-element.30.refs_1_.log, f32[1,1024]{1,0:T(1,128)S(1)} %bitcast.11, ...), custom_call_target="tpu_custom_call" | custom-call | flops 536870912 | bytes 5902336 | tf_op jit(solution)/shard_map/pallas_call | solution.py:32
  29.0 1.3 %collective-permute-start.5 = (bf16[128,1024]{1,0:T(8,128)(2,1)S(1)}, bf16[128,1024]{1,0:T(8,128)(2,1)S(1)}, u32[]{:S(2)}, u32[]{:S(2)}) collective-permute-start(bf16[128,1024]{1,0:T(8,128)(2,1)S(1)} %get-tuple-element.46.own), channel_id=1, source_target_pairs={{1,0},{0,1},{3,2},{2,3},{5,4},{4,5},{7,6},{6,7},{9,8},{8,9},{11,10... | collective-permute-start | bytes 786440 | tf_op jit(solution)/shard_map/ppermute | solution.py:367
  30.3 0.8 %shard_map.153.own = bf16[128,1024]{1,0:T(8,128)(2,1)S(1)} custom-call(f32[256,128]{1,0:T(8,128)S(1)} %get-tuple-element.30.refs_1_.log, bf16[256,512]{1,0:T(8,128)(2,1)S(1)} %get-tuple-element.31.refs_5_.refs_6_.query, bf16[128,512]{1,0:T(8,128)(2,1)S(1)} %get-tuple-element.49.keys, bf16[128,512]{1,0:T(8,128)(2,1)S(1)} %get-tuple-element.50.values, ...), custom_call_target="tpu_custom_call" | custom-call | flops 134217728 | bytes 3538944 | tf_op jit(solution)/shard_map/pallas_call | solution.py:32
  31.2 0.8 %collective-permute-start.6 = (bf16[128,1024]{1,0:T(8,128)(2,1)S(1)}, bf16[128,1024]{1,0:T(8,128)(2,1)S(1)}, u32[]{:S(2)}, u32[]{:S(2)}) collective-permute-start(bf16[128,1024]{1,0:T(8,128)(2,1)S(1)} %shard_map.153.own), channel_id=1, source_target_pairs={{1,0},{0,1},{3,2},{2,3},{5,4},{4,5},{7,6},{6,7},{9,8},{8,9},{11,10... | collective-permute-start | bytes 786440 | tf_op jit(solution)/shard_map/ppermute | solution.py:367
  32.0 6.3 %collective-permute-done.5.other = bf16[128,1024]{1,0:T(8,128)(2,1)S(1)} collective-permute-done((bf16[128,1024]{1,0:T(8,128)(2,1)S(1)}, bf16[128,1024]{1,0:T(8,128)(2,1)S(1)}, u32[]{:S(2)}, u32[]{:S(2)}) %collective-permute-start.5) | collective-permute-done | bytes 262176 | tf_op jit(solution)/shard_map/ppermute | solution.py:367
  38.3 0.0 copy-done.2
  38.3 0.0 copy-done.3
  38.3 0.0 copy-done.12
  38.3 0.7 %shard_map.151 = (bf16[128,1024]{1,0:T(8,128)(2,1)S(1)}, bf16[128,1024]{1,0:T(8,128)(2,1)S(1)}) custom-call(bf16[256,1024]{1,0:T(8,128)(2,1)S(1)} %copy-done, bf16[128,1024]{1,0:T(8,128)(2,1)S(1)} %get-tuple-element.46.own, bf16[128,1024]{1,0:T(8,128)(2,1)S(1)} %collective-permute-done.5.other, f32[1,1024]{1,0:T(1,128)S(1)} %bitcast.6, ...), custom_call_target="tpu_custom_call" | custom-call | flops 268435456 | bytes 3674112 | tf_op jit(solution)/shard_map/pallas_call | solution.py:32
  39.0 0.0 copy-start.4
  39.0 0.1 collective-permute-start.9
  39.1 2.6 %collective-permute-done.6.other = bf16[128,1024]{1,0:T(8,128)(2,1)S(1)} collective-permute-done((bf16[128,1024]{1,0:T(8,128)(2,1)S(1)}, bf16[128,1024]{1,0:T(8,128)(2,1)S(1)}, u32[]{:S(2)}, u32[]{:S(2)}) %collective-permute-start.6) | collective-permute-done | bytes 262176 | tf_op jit(solution)/shard_map/ppermute | solution.py:367
  41.7 0.7 %shard_map.154 = (bf16[128,1024]{1,0:T(8,128)(2,1)S(1)}, bf16[128,1024]{1,0:T(8,128)(2,1)S(1)}) custom-call(bf16[256,1024]{1,0:T(8,128)(2,1)S(1)} %copy-done, bf16[128,1024]{1,0:T(8,128)(2,1)S(1)} %shard_map.153.own, bf16[128,1024]{1,0:T(8,128)(2,1)S(1)} %collective-permute-done.6.other, f32[1,1024]{1,0:T(1,128)S(1)} %bitcast.7, ...), custom_call_target="tpu_custom_call" | custom-call | flops 268435456 | bytes 3674112 | tf_op jit(solution)/shard_map/pallas_call | solution.py:32
  42.4 0.2 collective-permute-start.7
  42.6 0.0 copy-done.4
  42.6 0.3 shard_map.157.query
  43.0 0.0 copy-start.5
  43.0 0.3 shard_map.152.query
  43.3 0.0 collective-permute-done.9.halo
  43.3 0.9 %copy-done.5 = bf16[512,1024]{1,0:T(8,128)(2,1)S(1)} copy-done((bf16[512,1024]{1,0:T(8,128)(2,1)S(1)}, bf16[512,1024]{1,0:T(8,128)(2,1)}, u32[]{:S(2)}) %copy-start.5) | copy-done | bytes 1048600
  44.2 1.0 %shard_map.158.share = bf16[128,1024]{1,0:T(8,128)(2,1)S(1)} custom-call(bf16[128,512]{1,0:T(8,128)(2,1)S(1)} %shard_map.157.query, bf16[128,1024]{1,0:T(8,128)(2,1)S(1)} %get-tuple-element.48.low, bf16[128,1024]{1,0:T(8,128)(2,1)S(1)} %get-tuple-element.51.high, bf16[128,1024]{1,0:T(8,128)(2,1)S(1)} %collective-permute-done.9.halo, ...), custom_call_target="tpu_custom_call" | custom-call | flops 134217728 | bytes 2228224 | tf_op jit(solution)/shard_map/pallas_call | solution.py:32
  45.2 1.5 %collective-permute-start.10 = (bf16[128,1024]{1,0:T(8,128)(2,1)S(1)}, bf16[128,1024]{1,0:T(8,128)(2,1)S(1)}, u32[]{:S(2)}, u32[]{:S(2)}) collective-permute-start(bf16[128,1024]{1,0:T(8,128)(2,1)S(1)} %shard_map.158.share), channel_id=1, source_target_pairs={{1,0},{0,1},{3,2},{2,3},{5,4},{4,5},{7,6},{6,7},{9,8},{8,9},{11,10... | collective-permute-start | bytes 786440 | tf_op jit(solution)/shard_map/ppermute | solution.py:367
  46.7 4.4 %collective-permute-done.7.halo = bf16[128,1024]{1,0:T(8,128)(2,1)S(1)} collective-permute-done((bf16[128,1024]{1,0:T(8,128)(2,1)S(1)}, bf16[128,1024]{1,0:T(8,128)(2,1)S(1)}, u32[]{:S(2)}, u32[]{:S(2)}) %collective-permute-start.7) | collective-permute-done | bytes 262176 | tf_op jit(solution)/shard_map/ppermute | solution.py:452
  51.1 1.0 %shard_map.155.share = bf16[128,1024]{1,0:T(8,128)(2,1)S(1)} custom-call(bf16[128,512]{1,0:T(8,128)(2,1)S(1)} %shard_map.152.query, bf16[128,1024]{1,0:T(8,128)(2,1)S(1)} %get-tuple-element.48.low, bf16[128,1024]{1,0:T(8,128)(2,1)S(1)} %get-tuple-element.51.high, bf16[128,1024]{1,0:T(8,128)(2,1)S(1)} %collective-permute-done.7.halo, ...), custom_call_target="tpu_custom_call" | custom-call | flops 134217728 | bytes 2228224 | tf_op jit(solution)/shard_map/pallas_call | solution.py:32
  52.1 1.5 %collective-permute-start.8 = (bf16[128,1024]{1,0:T(8,128)(2,1)S(1)}, bf16[128,1024]{1,0:T(8,128)(2,1)S(1)}, u32[]{:S(2)}, u32[]{:S(2)}) collective-permute-start(bf16[128,1024]{1,0:T(8,128)(2,1)S(1)} %shard_map.155.share), channel_id=1, source_target_pairs={{1,0},{0,1},{3,2},{2,3},{5,4},{4,5},{7,6},{6,7},{9,8},{8,9},{11,10... | collective-permute-start | bytes 786440 | tf_op jit(solution)/shard_map/ppermute | solution.py:367
  53.6 0.1 shard_map.159.base
  53.8 0.1 shard_map.156.base
  53.9 0.1 collective-permute-done.10.share
  54.0 0.7 %shard_map.160.refs_0_ = bf16[256,1024]{1,0:T(8,128)(2,1)} custom-call(f32[128,1024]{1,0:T(8,128)S(1)} %shard_map.159.base, bf16[128,1024]{1,0:T(8,128)(2,1)S(1)} %collective-permute-done.10.share), custom_call_target="tpu_custom_call" | custom-call | tf_op jit(solution)/shard_map/pallas_call | solution.py:324
  54.7 5.4 %collective-permute-done.8.share = bf16[128,1024]{1,0:T(8,128)(2,1)S(1)} collective-permute-done((bf16[128,1024]{1,0:T(8,128)(2,1)S(1)}, bf16[128,1024]{1,0:T(8,128)(2,1)S(1)}, u32[]{:S(2)}, u32[]{:S(2)}) %collective-permute-start.8) | collective-permute-done | bytes 262176 | tf_op jit(solution)/shard_map/ppermute | solution.py:367
  60.1 0.7 %shard_map.161 = bf16[256,1024]{1,0:T(8,128)(2,1)} custom-call(f32[128,1024]{1,0:T(8,128)S(1)} %shard_map.156.base, bf16[128,1024]{1,0:T(8,128)(2,1)S(1)} %collective-permute-done.8.share, bf16[256,1024]{1,0:T(8,128)(2,1)} %shard_map.160.refs_0_), custom_call_target="tpu_custom_call", output_to_operand_aliasing={{}: (2, {})} | custom-call | tf_op jit(solution)/shard_map/pallas_call | solution.py:324
  (8 shorter events, 0.0 us)
Async XLA Ops:
  0.0 9.4 %copy-start.11 = (s32[256,32]{0,1:T(8,128)S(1)}, s32[256,32]{0,1:T(8,128)}, u32[]{:S(2)}) copy-start(s32[256,32]{0,1:T(8,128)} %param.23) | copy-start | bytes 98308
  0.0 9.4 %copy-start.14 = (f32[1024]{0:T(1024)S(1)}, f32[1024]{0:T(1024)}, u32[]{:S(2)}) copy-start(f32[1024]{0:T(1024)} %param.18) | copy-start | bytes 12292
  0.0 9.4 %copy-start.15 = (s32[256]{0:T(256)S(1)}, s32[256]{0:T(256)}, u32[]{:S(2)}) copy-start(s32[256]{0:T(256)} %param.24) | copy-start | bytes 3076
  1.0 8.4 %copy-start = (bf16[256,1024]{1,0:T(8,128)(2,1)S(1)}, bf16[256,1024]{1,0:T(8,128)(2,1)}, u32[]{:S(2)}) copy-start(bf16[256,1024]{1,0:T(8,128)(2,1)} %hidden.9) | copy-start | bytes 1572868
  1.0 12.7 %collective-permute-start.1 = (bf16[128,1024]{1,0:T(8,128)(2,1)S(1)}, bf16[128,1024]{1,0:T(8,128)(2,1)S(1)}, u32[]{:S(2)}, u32[]{:S(2)}) collective-permute-start(bf16[128,1024]{1,0:T(8,128)(2,1)S(1)} %constant_dynamic-slice_fusion), channel_id=1, source_target_pairs={{1,0},{0,1},{3,2},{2,3},{5,4},{4,5},{7,6},{6,7},{9,8},{8,9},{11,10... | collective-permute-start | bytes 786440 | tf_op jit(solution)/shard_map/ppermute | solution.py:367
  4.0 1.2 %copy-start.8 = (bf16[512,1024]{1,0:T(8,128)(2,1)S(1)}, bf16[512,1024]{1,0:T(8,128)(2,1)}, u32[]{:S(2)}) copy-start(bf16[512,1024]{1,0:T(8,128)(2,1)} %refs_0_.3) | copy-start | bytes 3145732
  5.3 11.0 %copy-start.7 = (bf16[1024,512]{1,0:T(8,128)(2,1)S(1)}, bf16[1024,512]{1,0:T(8,128)(2,1)}, u32[]{:S(2)}) copy-start(bf16[1024,512]{1,0:T(8,128)(2,1)} %refs_4_.7) | copy-start | bytes 3145732
  5.3 10.9 %copy-start.6 = (bf16[1024,512]{1,0:T(8,128)(2,1)S(1)}, bf16[1024,512]{1,0:T(8,128)(2,1)}, u32[]{:S(2)}) copy-start(bf16[1024,512]{1,0:T(8,128)(2,1)} %refs_3_.3) | copy-start | bytes 3145732
  5.4 18.9 %collective-permute-start.2 = (bf16[256,1024]{1,0:T(8,128)(2,1)S(1)}, bf16[256,1024]{1,0:T(8,128)(2,1)S(1)}, u32[]{:S(2)}, u32[]{:S(2)}) collective-permute-start(bf16[256,1024]{1,0:T(8,128)(2,1)S(1)} %get-tuple-element.32), channel_id=1, source_target_pairs={{1,0},{0,1},{3,2},{2,3},{5,4},{4,5},{7,6},{6,7},{9,8},{8,9},{11,10... | collective-permute-start | bytes 1572872 | tf_op jit(solution)/shard_map/ppermute | solution.py:367
  5.5 15.7 %collective-permute-start.3 = (bf16[128,1024]{1,0:T(8,128)(2,1)S(1)}, bf16[128,1024]{1,0:T(8,128)(2,1)S(1)}, u32[]{:S(2)}, u32[]{:S(2)}) collective-permute-start(bf16[128,1024]{1,0:T(8,128)(2,1)S(1)} %constant_dynamic-slice_fusion), channel_id=1, source_target_pairs={{2,0},{4,2},{6,4},{8,6},{10,8},{12,10},{14,12},{16,14},{18,16},{20... | collective-permute-start | bytes 786440 | tf_op jit(solution)/shard_map/ppermute | solution.py:377
  9.4 1.2 %copy-start.10 = (bf16[1024,512]{1,0:T(8,128)(2,1)S(1)}, bf16[1024,512]{1,0:T(8,128)(2,1)}, u32[]{:S(2)}) copy-start(bf16[1024,512]{1,0:T(8,128)(2,1)} %wq.3) | copy-start | bytes 3145732
  13.7 2.6 %copy-start.13 = (f32[1024]{0:T(1024)S(1)}, f32[1024]{0:T(1024)}, u32[]{:S(2)}) copy-start(f32[1024]{0:T(1024)} %param.16) | copy-start | bytes 12292
  13.7 8.5 %collective-permute-start.4 = (bf16[128,1024]{1,0:T(8,128)(2,1)S(1)}, bf16[128,1024]{1,0:T(8,128)(2,1)S(1)}, u32[]{:S(2)}, u32[]{:S(2)}) collective-permute-start(bf16[128,1024]{1,0:T(8,128)(2,1)S(1)} %collective-permute-done.1.refs_0_), channel_id=1, source_target_pairs={{0,2},{2,4},{4,6},{6,8},{8,10},{10,12},{12,14},{14,16},{16,18},{18... | collective-permute-start | bytes 786440 | tf_op jit(solution)/shard_map/ppermute | solution.py:411
  13.8 13.9 %collective-permute-start = (bf16[128,1024]{1,0:T(8,128)(2,1)S(1)}, bf16[128,1024]{1,0:T(8,128)(2,1)S(1)}, u32[]{:S(2)}, u32[]{:S(2)}) collective-permute-start(bf16[128,1024]{1,0:T(8,128)(2,1)S(1)} %get-tuple-element.29), channel_id=1, source_target_pairs={{1,0},{0,1},{3,2},{2,3},{5,4},{4,5},{7,6},{6,7},{9,8},{8,9},{11,10... | collective-permute-start | bytes 786440 | tf_op jit(solution)/shard_map/ppermute | solution.py:367
  16.3 1.2 %copy-start.9 = (bf16[512,1024]{1,0:T(8,128)(2,1)S(1)}, bf16[512,1024]{1,0:T(8,128)(2,1)}, u32[]{:S(2)}) copy-start(bf16[512,1024]{1,0:T(8,128)(2,1)} %refs_0_.3) | copy-start | bytes 3145732
  24.3 3.4 %copy-start.1 = (bf16[512,1024]{1,0:T(8,128)(2,1)S(1)}, bf16[512,1024]{1,0:T(8,128)(2,1)}, u32[]{:S(2)}) copy-start(bf16[512,1024]{1,0:T(8,128)(2,1)} %wo.3) | copy-start | bytes 3145732
  29.0 9.3 %collective-permute-start.5 = (bf16[128,1024]{1,0:T(8,128)(2,1)S(1)}, bf16[128,1024]{1,0:T(8,128)(2,1)S(1)}, u32[]{:S(2)}, u32[]{:S(2)}) collective-permute-start(bf16[128,1024]{1,0:T(8,128)(2,1)S(1)} %get-tuple-element.46.own), channel_id=1, source_target_pairs={{1,0},{0,1},{3,2},{2,3},{5,4},{4,5},{7,6},{6,7},{9,8},{8,9},{11,10... | collective-permute-start | bytes 786440 | tf_op jit(solution)/shard_map/ppermute | solution.py:367
  30.3 8.0 %copy-start.2 = (bf16[1024,512]{1,0:T(8,128)(2,1)S(1)}, bf16[1024,512]{1,0:T(8,128)(2,1)}, u32[]{:S(2)}) copy-start(bf16[1024,512]{1,0:T(8,128)(2,1)} %wk.3) | copy-start | bytes 3145732
  30.3 8.0 %copy-start.3 = (bf16[1024,512]{1,0:T(8,128)(2,1)S(1)}, bf16[1024,512]{1,0:T(8,128)(2,1)}, u32[]{:S(2)}) copy-start(bf16[1024,512]{1,0:T(8,128)(2,1)} %wv.3) | copy-start | bytes 3145732
  30.3 8.0 %copy-start.12 = (f32[1024]{0:T(1024)S(1)}, f32[1024]{0:T(1024)}, u32[]{:S(2)}) copy-start(f32[1024]{0:T(1024)} %param.25) | copy-start | bytes 12292
  31.2 10.5 %collective-permute-start.6 = (bf16[128,1024]{1,0:T(8,128)(2,1)S(1)}, bf16[128,1024]{1,0:T(8,128)(2,1)S(1)}, u32[]{:S(2)}, u32[]{:S(2)}) collective-permute-start(bf16[128,1024]{1,0:T(8,128)(2,1)S(1)} %shard_map.153.own), channel_id=1, source_target_pairs={{1,0},{0,1},{3,2},{2,3},{5,4},{4,5},{7,6},{6,7},{9,8},{8,9},{11,10... | collective-permute-start | bytes 786440 | tf_op jit(solution)/shard_map/ppermute | solution.py:367
  39.0 3.6 %copy-start.4 = (bf16[1024,512]{1,0:T(8,128)(2,1)S(1)}, bf16[1024,512]{1,0:T(8,128)(2,1)}, u32[]{:S(2)}) copy-start(bf16[1024,512]{1,0:T(8,128)(2,1)} %wq.5) | copy-start | bytes 3145732
  39.0 4.3 %collective-permute-start.9 = (bf16[128,1024]{1,0:T(8,128)(2,1)S(1)}, bf16[128,1024]{1,0:T(8,128)(2,1)S(1)}, u32[]{:S(2)}, u32[]{:S(2)}) collective-permute-start(bf16[128,1024]{1,0:T(8,128)(2,1)S(1)} %get-tuple-element.48.low), channel_id=1, source_target_pairs={{2,0},{4,2},{6,4},{8,6},{10,8},{12,10},{14,12},{16,14},{18,16},{20... | collective-permute-start | bytes 786440 | tf_op jit(solution)/shard_map/ppermute | solution.py:451
  42.4 8.7 %collective-permute-start.7 = (bf16[128,1024]{1,0:T(8,128)(2,1)S(1)}, bf16[128,1024]{1,0:T(8,128)(2,1)S(1)}, u32[]{:S(2)}, u32[]{:S(2)}) collective-permute-start(bf16[128,1024]{1,0:T(8,128)(2,1)S(1)} %get-tuple-element.51.high), channel_id=1, source_target_pairs={{0,2},{2,4},{4,6},{6,8},{8,10},{10,12},{12,14},{14,16},{16,18},{18... | collective-permute-start | bytes 786440 | tf_op jit(solution)/shard_map/ppermute | solution.py:452
  43.0 1.2 %copy-start.5 = (bf16[512,1024]{1,0:T(8,128)(2,1)S(1)}, bf16[512,1024]{1,0:T(8,128)(2,1)}, u32[]{:S(2)}) copy-start(bf16[512,1024]{1,0:T(8,128)(2,1)} %wo.5) | copy-start | bytes 3145732
  45.2 8.7 %collective-permute-start.10 = (bf16[128,1024]{1,0:T(8,128)(2,1)S(1)}, bf16[128,1024]{1,0:T(8,128)(2,1)S(1)}, u32[]{:S(2)}, u32[]{:S(2)}) collective-permute-start(bf16[128,1024]{1,0:T(8,128)(2,1)S(1)} %shard_map.158.share), channel_id=1, source_target_pairs={{1,0},{0,1},{3,2},{2,3},{5,4},{4,5},{7,6},{6,7},{9,8},{8,9},{11,10... | collective-permute-start | bytes 786440 | tf_op jit(solution)/shard_map/ppermute | solution.py:367
  52.1 8.0 %collective-permute-start.8 = (bf16[128,1024]{1,0:T(8,128)(2,1)S(1)}, bf16[128,1024]{1,0:T(8,128)(2,1)S(1)}, u32[]{:S(2)}, u32[]{:S(2)}) collective-permute-start(bf16[128,1024]{1,0:T(8,128)(2,1)S(1)} %shard_map.155.share), channel_id=1, source_target_pairs={{1,0},{0,1},{3,2},{2,3},{5,4},{4,5},{7,6},{6,7},{9,8},{8,9},{11,10... | collective-permute-start | bytes 786440 | tf_op jit(solution)/shard_map/ppermute | solution.py:367

commit v7 on v5

--- a/solution.py
+++ b/solution.py
@@ -59,7 +59,7 @@
     return lax.dot_general(a, b, (((1,), (1,)), ((), ())), preferred_element_type=f32)
 
 
-def norm_rows(src, gain, dst, base, block=64):
+def norm_rows(src, gain, dst, base, block=128):
     rows = src.shape[0]
     block = min(block, rows)
 

time: 60 us -> 59.9 us (level)
  Pallas kernels: 19.8 us -> 18.8 us
    pallas_call x12, Pallas kernels: 18.2 us -> 17.2 us  [call(): pl.pallas_call(kernel, out_shape=outs, in_specs=[whole(a.shape) for a in...]
  transfers between devices with their start and end apart: 11 -> 11, of which waited for: 6 -> 7; matrix products, arithmetic and copies ran while one was open for 0% -> 0% of each run, Pallas kernels for 30% -> 28%
where the time goes in v7:
time: 59.9 us; the launch traced here: 59.7 us
  waiting for transfers between devices  20.6 us (34%)
  Pallas kernels  18.8 us (31%)
  starting transfers between devices  15.3 us (26%)
  local copies, waits for them, and re-layouts  4.7 us (8%)
    pallas_call x12, Pallas kernels, call(): pl.pallas_call(kernel, out_shape=outs, in_specs=[whole(a.shape) for a in...  17.2 us
    ppermute x7, waiting for transfers between devices, shifted(): lax.ppermute(value, 'mp', [((i + by) % peers, i) for i in range(peers)])  13.4 us
    ppermute x7, starting transfers between devices, shifted(): lax.ppermute(value, 'mp', [((i + by) % peers, i) for i in range(peers)])  10.8 us
    ppermute x1, waiting for transfers between devices, shards(): before = lax.ppermute(pairs[1][reach:] if reach else pairs[1], 'band', up)  5.47 us
    ppermute x1, starting transfers between devices, shards(): near_rim = lax.ppermute(ends, ('band', 'mp'), outward)  3.9 us
    unnamed x32, local copies, waits for them, and re-layouts  3.73 us
    pallas_call x2, Pallas kernels, mix_half(): pl.pallas_call(functools.partial(mixed_kernel, at), out_shape=shape_of(*m...  1.48 us
    ppermute x1, waiting for transfers between devices, shards(): far_rim = lax.ppermute(after(edge, query), ('band', 'mp'), inward)  1.35 us
  transfers between devices with their start and end apart: 11, of which 7 were waited for; matrix products, arithmetic and copies ran while one was open for 0% of the time, Pallas kernels for 28%

profile of v7, /device:TPU:0, one launch (start us, length us, event | category | flops | bytes accessed | tf_op | source)
XLA Modules:
  0.0 59.7 jit_solution(9058283526161606873)
XLA Ops:
  0.0 0.0 copy-start.11
  0.0 0.0 copy-start.14
  0.0 0.0 copy-start.15
  0.0 1.0 %constant_dynamic-slice_fusion = bf16[128,1024]{1,0:T(8,128)(2,1)S(1)} fusion(bf16[512,1024]{1,0:T(8,128)(2,1)} %refs_0_.3, s32[]{:T(128)S(6)} %select_n.3), kind=kLoop, calls=%fused_computation | loop fusion | bytes 524292 | tf_op jit(solution)/shard_map/dynamic_slice | solution.py:370
  1.0 0.0 copy-start
  1.0 3.0 %collective-permute-start.1 = (bf16[128,1024]{1,0:T(8,128)(2,1)S(1)}, bf16[128,1024]{1,0:T(8,128)(2,1)S(1)}, u32[]{:S(2)}, u32[]{:S(2)}) collective-permute-start(bf16[128,1024]{1,0:T(8,128)(2,1)S(1)} %constant_dynamic-slice_fusion), channel_id=1, source_target_pairs={{1,0},{0,1},{3,2},{2,3},{5,4},{4,5},{7,6},{6,7},{9,8},{8,9},{11,10... | collective-permute-start | bytes 786440 | tf_op jit(solution)/shard_map/ppermute | solution.py:365
  4.0 0.0 copy-start.8
  4.0 1.2 %copy-done.8 = bf16[512,1024]{1,0:T(8,128)(2,1)S(1)} copy-done((bf16[512,1024]{1,0:T(8,128)(2,1)S(1)}, bf16[512,1024]{1,0:T(8,128)(2,1)}, u32[]{:S(2)}) %copy-start.8) | copy-done | bytes 1048600
  5.3 0.1 shard_map.145
  5.3 0.0 copy-start.6
  5.4 0.1 collective-permute-start.2
  5.5 3.9 %collective-permute-start.3 = (bf16[128,1024]{1,0:T(8,128)(2,1)S(1)}, bf16[128,1024]{1,0:T(8,128)(2,1)S(1)}, u32[]{:S(2)}, u32[]{:S(2)}) collective-permute-start(bf16[128,1024]{1,0:T(8,128)(2,1)S(1)} %constant_dynamic-slice_fusion), channel_id=1, source_target_pairs={{2,0},{4,2},{6,4},{8,6},{10,8},{12,10},{14,12},{16,14},{18,16},{20... | collective-permute-start | bytes 786440 | tf_op jit(solution)/shard_map/ppermute | solution.py:375
  9.4 0.0 copy-done.11
  9.4 0.0 copy-done.14
  9.4 0.0 copy-done.15
  9.4 0.0 copy-done
  9.4 0.0 copy-start.10
  9.4 1.2 %copy-done.10 = bf16[1024,512]{1,0:T(8,128)(2,1)S(1)} copy-done((bf16[1024,512]{1,0:T(8,128)(2,1)S(1)}, bf16[1024,512]{1,0:T(8,128)(2,1)}, u32[]{:S(2)}) %copy-start.10) | copy-done | bytes 1048600
  10.6 2.8 %shard_map.146 = (f32[256,512]{1,0:T(8,128)S(1)}, f32[256,384]{1,0:T(8,128)S(1)}, f32[256,128]{1,0:T(8,128)S(1)}, f32[256,256]{1,0:T(8,128)S(1)}, bf16[256,512]{1,0:T(8,128)(2,1)S(1)}) custom-call(s32[32,256]{1,0:T(8,128)S(1)} %bitcast.5, s32[1,256]{1,0:T(1,128)S(1)} %bitcast.13, bf16[256,1024]{1,0:T(8,128)(2,1)S(1)} %copy-done, f32[1,1024]{1,0:T(1,128)S(1)} %bitcast.12, ...), custom_call_target="tpu_custom_call" | custom-call | flops 268435456 | bytes 3183616 | tf_op jit(solution)/shard_map/pallas_call | solution.py:32
  13.4 0.0 copy-start.13
  13.4 0.0 collective-permute-done.1.refs_0_
  13.4 0.1 collective-permute-start.4
  13.5 2.5 %collective-permute-start = (bf16[128,1024]{1,0:T(8,128)(2,1)S(1)}, bf16[128,1024]{1,0:T(8,128)(2,1)S(1)}, u32[]{:S(2)}, u32[]{:S(2)}) collective-permute-start(bf16[128,1024]{1,0:T(8,128)(2,1)S(1)} %get-tuple-element.29), channel_id=1, source_target_pairs={{1,0},{0,1},{3,2},{2,3},{5,4},{4,5},{7,6},{6,7},{9,8},{8,9},{11,10... | collective-permute-start | bytes 786440 | tf_op jit(solution)/shard_map/ppermute | solution.py:365
  16.0 0.0 copy-done.7
  16.0 0.0 copy-done.6
  16.0 0.0 copy-done.13
  16.0 1.2 %copy-done.9 = bf16[512,1024]{1,0:T(8,128)(2,1)S(1)} copy-done((bf16[512,1024]{1,0:T(8,128)(2,1)S(1)}, bf16[512,1024]{1,0:T(8,128)(2,1)}, u32[]{:S(2)}) %copy-start.9) | copy-done | bytes 1048600
  17.2 3.4 %shard_map.147 = (f32[256,512]{1,0:T(8,128)S(1)}, f32[256,512]{1,0:T(8,128)S(1)}, f32[256,512]{1,0:T(8,128)S(1)}) custom-call(bf16[512,1024]{1,0:T(8,128)(2,1)S(1)} %copy-done.9, f32[256,512]{1,0:T(8,128)S(1)} %get-tuple-element.36.refs_1_, f32[1,1024]{1,0:T(1,128)S(1)} %bitcast.8, bf16[1024,512]{1,0:T(8,128)(2,1)S(1)} %copy-done.6, ...), custom_call_target="tpu_custom_call" | custom-call | flops 2147483648 | bytes 5509120 | tf_op jit(solution)/shard_map/pallas_call | solution.py:32
  20.6 0.0 collective-permute-done.3.refs_0_
  20.6 1.4 %collective-permute-done.4.refs_1_ = bf16[128,1024]{1,0:T(8,128)(2,1)S(1)} collective-permute-done((bf16[128,1024]{1,0:T(8,128)(2,1)S(1)}, bf16[128,1024]{1,0:T(8,128)(2,1)S(1)}, u32[]{:S(2)}, u32[]{:S(2)}) %collective-permute-start.4) | collective-permute-done | bytes 262176 | tf_op jit(solution)/shard_map/ppermute | solution.py:409
  22.0 2.0 %shard_map.148 = (f32[256,512]{1,0:T(8,128)S(1)}, f32[256,512]{1,0:T(8,128)S(1)}, f32[256,512]{1,0:T(8,128)S(1)}) custom-call(bf16[128,1024]{1,0:T(8,128)(2,1)S(1)} %collective-permute-done.3.refs_0_, bf16[128,1024]{1,0:T(8,128)(2,1)S(1)} %collective-permute-done.4.refs_1_, f32[256,256]{1,0:T(8,128)S(1)} %get-tuple-element.35.refs_2_, ...), custom_call_target="tpu_custom_call" | custom-call | flops 1073741824 | bytes 6295552 | tf_op jit(solution)/shard_map/pallas_call | solution.py:32
  24.0 0.0 collective-permute-done.2.refs_1_
  24.0 0.0 copy-start.4
  24.0 3.0 %shard_map.149 = (f32[256,512]{1,0:T(8,128)S(1)}, f32[256,512]{1,0:T(8,128)S(1)}, f32[256,512]{1,0:T(8,128)S(1)}) custom-call(bf16[128,1024]{1,0:T(8,128)(2,1)S(1)} %collective-permute-done.1.refs_0_, bf16[256,1024]{1,0:T(8,128)(2,1)S(1)} %collective-permute-done.2.refs_1_, f32[256,384]{1,0:T(8,128)S(1)} %get-tuple-element.33.refs_2_, ...), custom_call_target="tpu_custom_call" | custom-call | flops 1610612736 | bytes 6688768 | tf_op jit(solution)/shard_map/pallas_call | solution.py:32
  27.0 0.2 collective-permute-done.refs_0_
  27.2 0.0 copy-done.4
  27.2 1.3 %shard_map.150 = (bf16[128,1024]{1,0:T(8,128)(2,1)S(1)}, bf16[128,512]{1,0:T(8,128)(2,1)S(1)}, bf16[128,512]{1,0:T(8,128)(2,1)S(1)}) custom-call(bf16[128,1024]{1,0:T(8,128)(2,1)S(1)} %collective-permute-done.refs_0_, f32[256,128]{1,0:T(8,128)S(1)} %get-tuple-element.30.refs_1_.log, f32[1,1024]{1,0:T(1,128)S(1)} %bitcast.11, ...), custom_call_target="tpu_custom_call" | custom-call | flops 536870912 | bytes 5902336 | tf_op jit(solution)/shard_map/pallas_call | solution.py:32
  28.5 1.8 %collective-permute-start.5 = (bf16[128,1024]{1,0:T(8,128)(2,1)S(1)}, bf16[128,1024]{1,0:T(8,128)(2,1)S(1)}, u32[]{:S(2)}, u32[]{:S(2)}) collective-permute-start(bf16[128,1024]{1,0:T(8,128)(2,1)S(1)} %get-tuple-element.46.own), channel_id=1, source_target_pairs={{1,0},{0,1},{3,2},{2,3},{5,4},{4,5},{7,6},{6,7},{9,8},{8,9},{11,10... | collective-permute-start | bytes 786440 | tf_op jit(solution)/shard_map/ppermute | solution.py:365
  30.4 0.9 %shard_map.152.own = bf16[128,1024]{1,0:T(8,128)(2,1)S(1)} custom-call(f32[256,128]{1,0:T(8,128)S(1)} %get-tuple-element.30.refs_1_.log, bf16[256,512]{1,0:T(8,128)(2,1)S(1)} %get-tuple-element.31.refs_5_.refs_6_.query, bf16[128,512]{1,0:T(8,128)(2,1)S(1)} %get-tuple-element.49.keys, bf16[128,512]{1,0:T(8,128)(2,1)S(1)} %get-tuple-element.50.values, ...), custom_call_target="tpu_custom_call" | custom-call | flops 134217728 | bytes 3538944 | tf_op jit(solution)/shard_map/pallas_call | solution.py:32
  31.2 0.3 collective-permute-start.6
  31.6 6.3 %collective-permute-done.5.other = bf16[128,1024]{1,0:T(8,128)(2,1)S(1)} collective-permute-done((bf16[128,1024]{1,0:T(8,128)(2,1)S(1)}, bf16[128,1024]{1,0:T(8,128)(2,1)S(1)}, u32[]{:S(2)}, u32[]{:S(2)}) %collective-permute-start.5) | collective-permute-done | bytes 262176 | tf_op jit(solution)/shard_map/ppermute | solution.py:365
  37.8 0.0 copy-done.1
  37.8 0.0 copy-done.2
  37.9 0.0 copy-done.3
  37.9 0.0 copy-done.12
  37.9 0.8 %shard_map.151 = (bf16[128,512]{1,0:T(8,128)(2,1)S(1)}, bf16[128,1024]{1,0:T(8,128)(2,1)S(1)}) custom-call(bf16[256,1024]{1,0:T(8,128)(2,1)S(1)} %copy-done, bf16[128,1024]{1,0:T(8,128)(2,1)S(1)} %get-tuple-element.46.own, bf16[128,1024]{1,0:T(8,128)(2,1)S(1)} %collective-permute-done.5.other, f32[1,1024]{1,0:T(1,128)S(1)} %bitcast.6, ...), custom_call_target="tpu_custom_call" | custom-call | flops 402653184 | bytes 4591616 | tf_op jit(solution)/shard_map/pallas_call | solution.py:32
  38.7 0.0 copy-start.5
  38.7 0.4 collective-permute-start.9
  39.1 2.6 %collective-permute-done.6.other = bf16[128,1024]{1,0:T(8,128)(2,1)S(1)} collective-permute-done((bf16[128,1024]{1,0:T(8,128)(2,1)S(1)}, bf16[128,1024]{1,0:T(8,128)(2,1)S(1)}, u32[]{:S(2)}, u32[]{:S(2)}) %collective-permute-start.6) | collective-permute-done | bytes 262176 | tf_op jit(solution)/shard_map/ppermute | solution.py:365
  41.7 0.8 %shard_map.153 = (bf16[128,512]{1,0:T(8,128)(2,1)S(1)}, bf16[128,1024]{1,0:T(8,128)(2,1)S(1)}) custom-call(bf16[256,1024]{1,0:T(8,128)(2,1)S(1)} %copy-done, bf16[128,1024]{1,0:T(8,128)(2,1)S(1)} %shard_map.152.own, bf16[128,1024]{1,0:T(8,128)(2,1)S(1)} %collective-permute-done.6.other, f32[1,1024]{1,0:T(1,128)S(1)} %bitcast.7, ...), custom_call_target="tpu_custom_call" | custom-call | flops 402653184 | bytes 4591616 | tf_op jit(solution)/shard_map/pallas_call | solution.py:32
  42.5 0.1 collective-permute-start.7
  42.6 0.4 collective-permute-done.9.halo
  43.0 0.0 copy-done.5
  43.0 1.0 %shard_map.156.share = bf16[128,1024]{1,0:T(8,128)(2,1)S(1)} custom-call(bf16[128,512]{1,0:T(8,128)(2,1)S(1)} %get-tuple-element.52.query, bf16[128,1024]{1,0:T(8,128)(2,1)S(1)} %get-tuple-element.48.low, bf16[128,1024]{1,0:T(8,128)(2,1)S(1)} %get-tuple-element.51.high, bf16[128,1024]{1,0:T(8,128)(2,1)S(1)} %collective-permute-done.9.halo, ...), custom_call_target="tpu_custom_call" | custom-call | flops 134217728 | bytes 2228224 | tf_op jit(solution)/shard_map/pallas_call | solution.py:32
  44.0 1.5 %collective-permute-start.10 = (bf16[128,1024]{1,0:T(8,128)(2,1)S(1)}, bf16[128,1024]{1,0:T(8,128)(2,1)S(1)}, u32[]{:S(2)}, u32[]{:S(2)}) collective-permute-start(bf16[128,1024]{1,0:T(8,128)(2,1)S(1)} %shard_map.156.share), channel_id=1, source_target_pairs={{1,0},{0,1},{3,2},{2,3},{5,4},{4,5},{7,6},{6,7},{9,8},{8,9},{11,10... | collective-permute-start | bytes 786440 | tf_op jit(solution)/shard_map/ppermute | solution.py:365
  45.6 5.5 %collective-permute-done.7.halo = bf16[128,1024]{1,0:T(8,128)(2,1)S(1)} collective-permute-done((bf16[128,1024]{1,0:T(8,128)(2,1)S(1)}, bf16[128,1024]{1,0:T(8,128)(2,1)S(1)}, u32[]{:S(2)}, u32[]{:S(2)}) %collective-permute-start.7) | collective-permute-done | bytes 262176 | tf_op jit(solution)/shard_map/ppermute | solution.py:447
  51.1 1.0 %shard_map.154.share = bf16[128,1024]{1,0:T(8,128)(2,1)S(1)} custom-call(bf16[128,512]{1,0:T(8,128)(2,1)S(1)} %get-tuple-element.47.query, bf16[128,1024]{1,0:T(8,128)(2,1)S(1)} %get-tuple-element.48.low, bf16[128,1024]{1,0:T(8,128)(2,1)S(1)} %get-tuple-element.51.high, bf16[128,1024]{1,0:T(8,128)(2,1)S(1)} %collective-permute-done.7.halo, ...), custom_call_target="tpu_custom_call" | custom-call | flops 134217728 | bytes 2228224 | tf_op jit(solution)/shard_map/pallas_call | solution.py:32
  52.1 1.5 %collective-permute-start.8 = (bf16[128,1024]{1,0:T(8,128)(2,1)S(1)}, bf16[128,1024]{1,0:T(8,128)(2,1)S(1)}, u32[]{:S(2)}, u32[]{:S(2)}) collective-permute-start(bf16[128,1024]{1,0:T(8,128)(2,1)S(1)} %shard_map.154.share), channel_id=1, source_target_pairs={{1,0},{0,1},{3,2},{2,3},{5,4},{4,5},{7,6},{6,7},{9,8},{8,9},{11,10... | collective-permute-start | bytes 786440 | tf_op jit(solution)/shard_map/ppermute | solution.py:365
  53.6 0.1 shard_map.157.base
  53.7 0.1 shard_map.155.base
  53.8 0.0 collective-permute-done.10.share
  53.9 0.7 %shard_map.158.refs_0_ = bf16[256,1024]{1,0:T(8,128)(2,1)} custom-call(f32[128,1024]{1,0:T(8,128)S(1)} %shard_map.157.base, bf16[128,1024]{1,0:T(8,128)(2,1)S(1)} %collective-permute-done.10.share), custom_call_target="tpu_custom_call" | custom-call | tf_op jit(solution)/shard_map/pallas_call | solution.py:322
  54.6 4.3 %collective-permute-done.8.share = bf16[128,1024]{1,0:T(8,128)(2,1)S(1)} collective-permute-done((bf16[128,1024]{1,0:T(8,128)(2,1)S(1)}, bf16[128,1024]{1,0:T(8,128)(2,1)S(1)}, u32[]{:S(2)}, u32[]{:S(2)}) %collective-permute-start.8) | collective-permute-done | bytes 262176 | tf_op jit(solution)/shard_map/ppermute | solution.py:365
  58.9 0.7 %shard_map.159 = bf16[256,1024]{1,0:T(8,128)(2,1)} custom-call(f32[128,1024]{1,0:T(8,128)S(1)} %shard_map.155.base, bf16[128,1024]{1,0:T(8,128)(2,1)S(1)} %collective-permute-done.8.share, bf16[256,1024]{1,0:T(8,128)(2,1)} %shard_map.158.refs_0_), custom_call_target="tpu_custom_call", output_to_operand_aliasing={{}: (2, {})} | custom-call | tf_op jit(solution)/shard_map/pallas_call | solution.py:322
  (6 shorter events, 0.0 us)
Async XLA Ops:
  0.0 9.4 %copy-start.11 = (s32[256,32]{0,1:T(8,128)S(1)}, s32[256,32]{0,1:T(8,128)}, u32[]{:S(2)}) copy-start(s32[256,32]{0,1:T(8,128)} %param.23) | copy-start | bytes 98308
  0.0 9.4 %copy-start.14 = (f32[1024]{0:T(1024)S(1)}, f32[1024]{0:T(1024)}, u32[]{:S(2)}) copy-start(f32[1024]{0:T(1024)} %param.18) | copy-start | bytes 12292
  0.0 9.4 %copy-start.15 = (s32[256]{0:T(256)S(1)}, s32[256]{0:T(256)}, u32[]{:S(2)}) copy-start(s32[256]{0:T(256)} %param.24) | copy-start | bytes 3076
  1.0 8.4 %copy-start = (bf16[256,1024]{1,0:T(8,128)(2,1)S(1)}, bf16[256,1024]{1,0:T(8,128)(2,1)}, u32[]{:S(2)}) copy-start(bf16[256,1024]{1,0:T(8,128)(2,1)} %hidden.9) | copy-start | bytes 1572868
  1.0 12.4 %collective-permute-start.1 = (bf16[128,1024]{1,0:T(8,128)(2,1)S(1)}, bf16[128,1024]{1,0:T(8,128)(2,1)S(1)}, u32[]{:S(2)}, u32[]{:S(2)}) collective-permute-start(bf16[128,1024]{1,0:T(8,128)(2,1)S(1)} %constant_dynamic-slice_fusion), channel_id=1, source_target_pairs={{1,0},{0,1},{3,2},{2,3},{5,4},{4,5},{7,6},{6,7},{9,8},{8,9},{11,10... | collective-permute-start | bytes 786440 | tf_op jit(solution)/shard_map/ppermute | solution.py:365
  4.0 1.2 %copy-start.8 = (bf16[512,1024]{1,0:T(8,128)(2,1)S(1)}, bf16[512,1024]{1,0:T(8,128)(2,1)}, u32[]{:S(2)}) copy-start(bf16[512,1024]{1,0:T(8,128)(2,1)} %refs_0_.3) | copy-start | bytes 3145732
  5.3 10.7 %copy-start.7 = (bf16[1024,512]{1,0:T(8,128)(2,1)S(1)}, bf16[1024,512]{1,0:T(8,128)(2,1)}, u32[]{:S(2)}) copy-start(bf16[1024,512]{1,0:T(8,128)(2,1)} %refs_4_.7) | copy-start | bytes 3145732
  5.3 10.7 %copy-start.6 = (bf16[1024,512]{1,0:T(8,128)(2,1)S(1)}, bf16[1024,512]{1,0:T(8,128)(2,1)}, u32[]{:S(2)}) copy-start(bf16[1024,512]{1,0:T(8,128)(2,1)} %refs_3_.3) | copy-start | bytes 3145732
  5.4 18.6 %collective-permute-start.2 = (bf16[256,1024]{1,0:T(8,128)(2,1)S(1)}, bf16[256,1024]{1,0:T(8,128)(2,1)S(1)}, u32[]{:S(2)}, u32[]{:S(2)}) collective-permute-start(bf16[256,1024]{1,0:T(8,128)(2,1)S(1)} %get-tuple-element.32), channel_id=1, source_target_pairs={{1,0},{0,1},{3,2},{2,3},{5,4},{4,5},{7,6},{6,7},{9,8},{8,9},{11,10... | collective-permute-start | bytes 1572872 | tf_op jit(solution)/shard_map/ppermute | solution.py:365
  5.5 15.1 %collective-permute-start.3 = (bf16[128,1024]{1,0:T(8,128)(2,1)S(1)}, bf16[128,1024]{1,0:T(8,128)(2,1)S(1)}, u32[]{:S(2)}, u32[]{:S(2)}) collective-permute-start(bf16[128,1024]{1,0:T(8,128)(2,1)S(1)} %constant_dynamic-slice_fusion), channel_id=1, source_target_pairs={{2,0},{4,2},{6,4},{8,6},{10,8},{12,10},{14,12},{16,14},{18,16},{20... | collective-permute-start | bytes 786440 | tf_op jit(solution)/shard_map/ppermute | solution.py:375
  9.4 1.2 %copy-start.10 = (bf16[1024,512]{1,0:T(8,128)(2,1)S(1)}, bf16[1024,512]{1,0:T(8,128)(2,1)}, u32[]{:S(2)}) copy-start(bf16[1024,512]{1,0:T(8,128)(2,1)} %wq.3) | copy-start | bytes 3145732
  13.4 2.6 %copy-start.13 = (f32[1024]{0:T(1024)S(1)}, f32[1024]{0:T(1024)}, u32[]{:S(2)}) copy-start(f32[1024]{0:T(1024)} %param.16) | copy-start | bytes 12292
  13.4 8.5 %collective-permute-start.4 = (bf16[128,1024]{1,0:T(8,128)(2,1)S(1)}, bf16[128,1024]{1,0:T(8,128)(2,1)S(1)}, u32[]{:S(2)}, u32[]{:S(2)}) collective-permute-start(bf16[128,1024]{1,0:T(8,128)(2,1)S(1)} %collective-permute-done.1.refs_0_), channel_id=1, source_target_pairs={{0,2},{2,4},{4,6},{6,8},{8,10},{10,12},{12,14},{14,16},{16,18},{18... | collective-permute-start | bytes 786440 | tf_op jit(solution)/shard_map/ppermute | solution.py:409
  13.5 13.7 %collective-permute-start = (bf16[128,1024]{1,0:T(8,128)(2,1)S(1)}, bf16[128,1024]{1,0:T(8,128)(2,1)S(1)}, u32[]{:S(2)}, u32[]{:S(2)}) collective-permute-start(bf16[128,1024]{1,0:T(8,128)(2,1)S(1)} %get-tuple-element.29), channel_id=1, source_target_pairs={{1,0},{0,1},{3,2},{2,3},{5,4},{4,5},{7,6},{6,7},{9,8},{8,9},{11,10... | collective-permute-start | bytes 786440 | tf_op jit(solution)/shard_map/ppermute | solution.py:365
  16.0 1.2 %copy-start.9 = (bf16[512,1024]{1,0:T(8,128)(2,1)S(1)}, bf16[512,1024]{1,0:T(8,128)(2,1)}, u32[]{:S(2)}) copy-start(bf16[512,1024]{1,0:T(8,128)(2,1)} %refs_0_.3) | copy-start | bytes 3145732
  24.0 3.2 %copy-start.4 = (bf16[512,1024]{1,0:T(8,128)(2,1)S(1)}, bf16[512,1024]{1,0:T(8,128)(2,1)}, u32[]{:S(2)}) copy-start(bf16[512,1024]{1,0:T(8,128)(2,1)} %wo.3) | copy-start | bytes 3145732
  28.5 9.3 %collective-permute-start.5 = (bf16[128,1024]{1,0:T(8,128)(2,1)S(1)}, bf16[128,1024]{1,0:T(8,128)(2,1)S(1)}, u32[]{:S(2)}, u32[]{:S(2)}) collective-permute-start(bf16[128,1024]{1,0:T(8,128)(2,1)S(1)} %get-tuple-element.46.own), channel_id=1, source_target_pairs={{1,0},{0,1},{3,2},{2,3},{5,4},{4,5},{7,6},{6,7},{9,8},{8,9},{11,10... | collective-permute-start | bytes 786440 | tf_op jit(solution)/shard_map/ppermute | solution.py:365
  30.3 7.5 %copy-start.1 = (bf16[1024,512]{1,0:T(8,128)(2,1)S(1)}, bf16[1024,512]{1,0:T(8,128)(2,1)}, u32[]{:S(2)}) copy-start(bf16[1024,512]{1,0:T(8,128)(2,1)} %wq.5) | copy-start | bytes 3145732
  30.3 7.5 %copy-start.2 = (bf16[1024,512]{1,0:T(8,128)(2,1)S(1)}, bf16[1024,512]{1,0:T(8,128)(2,1)}, u32[]{:S(2)}) copy-start(bf16[1024,512]{1,0:T(8,128)(2,1)} %wk.3) | copy-start | bytes 3145732
  30.3 7.5 %copy-start.3 = (bf16[1024,512]{1,0:T(8,128)(2,1)S(1)}, bf16[1024,512]{1,0:T(8,128)(2,1)}, u32[]{:S(2)}) copy-start(bf16[1024,512]{1,0:T(8,128)(2,1)} %wv.3) | copy-start | bytes 3145732
  30.4 7.5 %copy-start.12 = (f32[1024]{0:T(1024)S(1)}, f32[1024]{0:T(1024)}, u32[]{:S(2)}) copy-start(f32[1024]{0:T(1024)} %param.25) | copy-start | bytes 12292
  31.2 10.5 %collective-permute-start.6 = (bf16[128,1024]{1,0:T(8,128)(2,1)S(1)}, bf16[128,1024]{1,0:T(8,128)(2,1)S(1)}, u32[]{:S(2)}, u32[]{:S(2)}) collective-permute-start(bf16[128,1024]{1,0:T(8,128)(2,1)S(1)} %shard_map.152.own), channel_id=1, source_target_pairs={{1,0},{0,1},{3,2},{2,3},{5,4},{4,5},{7,6},{6,7},{9,8},{8,9},{11,10... | collective-permute-start | bytes 786440 | tf_op jit(solution)/shard_map/ppermute | solution.py:365
  38.7 4.3 %copy-start.5 = (bf16[512,1024]{1,0:T(8,128)(2,1)S(1)}, bf16[512,1024]{1,0:T(8,128)(2,1)}, u32[]{:S(2)}) copy-start(bf16[512,1024]{1,0:T(8,128)(2,1)} %wo.5) | copy-start | bytes 3145732
  38.7 4.3 %collective-permute-start.9 = (bf16[128,1024]{1,0:T(8,128)(2,1)S(1)}, bf16[128,1024]{1,0:T(8,128)(2,1)S(1)}, u32[]{:S(2)}, u32[]{:S(2)}) collective-permute-start(bf16[128,1024]{1,0:T(8,128)(2,1)S(1)} %get-tuple-element.48.low), channel_id=1, source_target_pairs={{2,0},{4,2},{6,4},{8,6},{10,8},{12,10},{14,12},{16,14},{18,16},{20... | collective-permute-start | bytes 786440 | tf_op jit(solution)/shard_map/ppermute | solution.py:446
  42.5 8.5 %collective-permute-start.7 = (bf16[128,1024]{1,0:T(8,128)(2,1)S(1)}, bf16[128,1024]{1,0:T(8,128)(2,1)S(1)}, u32[]{:S(2)}, u32[]{:S(2)}) collective-permute-start(bf16[128,1024]{1,0:T(8,128)(2,1)S(1)} %get-tuple-element.51.high), channel_id=1, source_target_pairs={{0,2},{2,4},{4,6},{6,8},{8,10},{10,12},{12,14},{14,16},{16,18},{18... | collective-permute-start | bytes 786440 | tf_op jit(solution)/shard_map/ppermute | solution.py:447
  44.0 9.8 %collective-permute-start.10 = (bf16[128,1024]{1,0:T(8,128)(2,1)S(1)}, bf16[128,1024]{1,0:T(8,128)(2,1)S(1)}, u32[]{:S(2)}, u32[]{:S(2)}) collective-permute-start(bf16[128,1024]{1,0:T(8,128)(2,1)S(1)} %shard_map.156.share), channel_id=1, source_target_pairs={{1,0},{0,1},{3,2},{2,3},{5,4},{4,5},{7,6},{6,7},{9,8},{8,9},{11,10... | collective-permute-start | bytes 786440 | tf_op jit(solution)/shard_map/ppermute | solution.py:365
  52.1 6.8 %collective-permute-start.8 = (bf16[128,1024]{1,0:T(8,128)(2,1)S(1)}, bf16[128,1024]{1,0:T(8,128)(2,1)S(1)}, u32[]{:S(2)}, u32[]{:S(2)}) collective-permute-start(bf16[128,1024]{1,0:T(8,128)(2,1)S(1)} %shard_map.154.share), channel_id=1, source_target_pairs={{1,0},{0,1},{3,2},{2,3},{5,4},{4,5},{7,6},{6,7},{9,8},{8,9},{11,10... | collective-permute-start | bytes 786440 | tf_op jit(solution)/shard_map/ppermute | solution.py:365
